TPU v7x, 32 devices: a whole 2x2x4 slice. The times are simulated.
32 devices in a mesh: section: 4 (over x, core), dp: 8 (over z, y).
Axes of the slice: x: 2, y: 2, z: 4, core: 2. Of those that a mesh axis runs over, the one named last changes fastest.
Arguments:
- x_in: bfloat16 [16384, 384], P('dp'), may hold values from -6 to 6
- targets: float32 [16384, 192], P('dp'), may hold values from 0.02 to 20
- valid_len: int32 [32], replicated, may hold values from 64 to 512, as said below
- present_stems: int32 [32, 4], replicated, may hold values 0 or 1
- w_master: float32 [4, 192, 9216], P('section', 'dp'), may hold values from -3 to 3
- norm_gains: float32 [4, 2, 384], P('section', None, 'dp'), may hold values from 0.5 to 1.5
- gain_m: float32 [4, 2, 384], P('section', None, 'dp'), may hold values from -0.00030517578 to 0.00030517578
- gain_v: float32 [4, 2, 384], P('section', None, 'dp'), may hold values from 8e-11 to 1.3e-09
- l_stats: float32 [4, 192, 9216], P('section', 'dp'), may hold values from -1 to 1, as said below
- r_stats: float32 [4, 192, 9216], P('section', 'dp'), may hold values from -1 to 1, as said below
- l_roots: float32 [4, 192, 9216], P('section', 'dp'), may hold values from -20 to 120, as said below
- r_roots: float32 [4, 192, 9216], P('section', 'dp'), may hold values from -20 to 120, as said below
- step_count: int32 [1], replicated, may hold values from 2 to 20
Outputs:
- w_new: float32 [4, 192, 9216], P('section', 'dp')
- grad_blocks: float32 [4, 192, 9216], P('section', 'dp')
- l_new: float32 [4, 192, 9216], P('section', 'dp')
- r_new: float32 [4, 192, 9216], P('section', 'dp')
- gains_new: float32 [4, 2, 384], P('section', None, 'dp')
- m_new: float32 [4, 2, 384], P('section', None, 'dp')
- v_new: float32 [4, 2, 384], P('section', None, 'dp')
- loss_value: float32 [], replicated
- grad_norm: float32 [], replicated
- rms: float32 [4, 3], P('section')
Inputs may be any that keep to these rules, and one draw needn't show every extreme that they name: `valid_len`: some segment has all 512 frames valid. `l_stats`: each block is symmetric. `r_stats`: each block is symmetric. `l_roots`: each block is symmetric. `r_roots`: each block is symmetric.
All inputs are finite; a program needn't handle non-finite values.
Results may differ from a plain program's by a relative error of at most 0.012.
The roundings to bfloat16 on the way count: a program that leaves them out, or rounds other values in their place, can miss the bound.
Values may be sent and summed in bfloat16 or wider, within the bound.
A program may use at most 128 MiB of HBM per device.

v0:
```python
import math

import jax
import jax.numpy as jnp
from jax import lax
from jax.sharding import PartitionSpec as P

FF = 1536
HEADS = 8


def from_behind(value, axis, by):
    peers = lax.axis_size(axis)
    pairs = [(i, i + by) for i in range(peers) if 0 <= i + by < peers]
    return lax.ppermute(value, axis, pairs)


def unblock(blocks, row_count, col_count, block_size):
    return (
        blocks.reshape(row_count // block_size, col_count // block_size, block_size, block_size)
        .transpose(0, 2, 1, 3)
        .reshape(row_count, col_count)
    )


def to_blocks(matrix, block_size):
    row_count, col_count = matrix.shape
    return (
        matrix.reshape(row_count // block_size, block_size, col_count // block_size, block_size)
        .transpose(0, 2, 1, 3)
        .reshape(-1, block_size * block_size)
    )


def split_matrices(blocks, model_width):
    block_size = model_width // 4
    shapes = (
        (model_width, 3 * model_width),
        (model_width, model_width),
        (model_width, FF),
        (FF, model_width),
    )
    result = []
    offset = 0
    for row_count, col_count in shapes:
        number = row_count * col_count // (block_size * block_size)
        result.append(unblock(blocks[offset : offset + number], row_count, col_count, block_size))
        offset = offset + number
    return result


def rms_norm(stream, gain):
    factor = lax.rsqrt(jnp.mean(stream * stream, axis=-1, keepdims=True) + 1e-06)
    return (stream * factor * gain, factor)


def norm_back(stream, factor, gain, grad):
    scaled = grad * gain
    grad_in = factor * scaled - stream * factor**3 * jnp.mean(
        stream * scaled, axis=-1, keepdims=True
    )
    return (grad_in, jnp.sum(grad * stream * factor, axis=0))


def gelu_slope(pre_act):
    return (
        0.5 * (1.0 + lax.erf(pre_act * 0.7071067811865476))
        + pre_act * jnp.exp(-0.5 * pre_act * pre_act) * 0.3989422804014327
    )


def layer_forward(stream, matrices, gain_pair, length):
    w_qkv, w_out, w_up, w_down = matrices
    row_count, model_width = stream.shape
    head_dim = model_width // HEADS
    frames = jnp.arange(row_count)
    norm_one, scale_one = rms_norm(stream, gain_pair[0])
    normed = norm_one.astype(jnp.bfloat16)
    qkv_all = jnp.dot(normed, w_qkv, preferred_element_type=jnp.float32).astype(jnp.bfloat16)
    queries = qkv_all[:, :model_width].reshape(row_count, HEADS, head_dim)
    key_rows = qkv_all[:, model_width : 2 * model_width].reshape(row_count, HEADS, head_dim)
    value_rows = qkv_all[:, 2 * model_width :].reshape(row_count, HEADS, head_dim)
    masking = jnp.where(frames < length, 0.0, -1e30).astype(jnp.float32)
    scores = jnp.einsum(
        "qhe,khe->hqk", queries, key_rows, preferred_element_type=jnp.float32
    ) * head_dim ** (-0.5)
    attn_probs = jax.nn.softmax(scores + masking[None, None, :], axis=-1)
    probs_low = attn_probs.astype(jnp.bfloat16)
    attended = (
        jnp.einsum("hqk,khe->qhe", probs_low, value_rows, preferred_element_type=jnp.float32)
        .reshape(row_count, model_width)
        .astype(jnp.bfloat16)
    )
    branch_attn = jnp.dot(attended, w_out, preferred_element_type=jnp.float32)
    middle = stream + branch_attn
    norm_two, scale_two = rms_norm(middle, gain_pair[1])
    normed_two = norm_two.astype(jnp.bfloat16)
    pre_act = jnp.dot(normed_two, w_up, preferred_element_type=jnp.float32)
    hidden = jax.nn.gelu(pre_act, approximate=False).astype(jnp.bfloat16)
    branch_ffn = jnp.dot(hidden, w_down, preferred_element_type=jnp.float32)
    kept_vals = (
        scale_one,
        normed,
        queries,
        key_rows,
        value_rows,
        attn_probs,
        probs_low,
        attended,
        middle,
        scale_two,
        normed_two,
        pre_act,
        hidden,
    )
    return (middle + branch_ffn, branch_attn, branch_ffn, kept_vals)


def layer_backward(stream, matrices, gain_pair, length, upstream):
    w_qkv, w_out, w_up, w_down = matrices
    row_count, model_width = stream.shape
    head_dim = model_width // HEADS
    output, branch_attn, branch_ffn, kept_vals = layer_forward(stream, matrices, gain_pair, length)
    (
        scale_one,
        normed,
        queries,
        key_rows,
        value_rows,
        attn_probs,
        probs_low,
        attended,
        middle,
        scale_two,
        normed_two,
        pre_act,
        hidden,
    ) = kept_vals
    grad_ffn = upstream.astype(jnp.bfloat16)
    grad_down = jnp.dot(hidden.T, grad_ffn, preferred_element_type=jnp.float32)
    grad_hidden = jnp.dot(grad_ffn, w_down.T, preferred_element_type=jnp.float32)
    grad_pre = (grad_hidden * gelu_slope(pre_act)).astype(jnp.bfloat16)
    grad_up = jnp.dot(normed_two.T, grad_pre, preferred_element_type=jnp.float32)
    back_mid, gain_two = norm_back(
        middle,
        scale_two,
        gain_pair[1],
        jnp.dot(grad_pre, w_up.T, preferred_element_type=jnp.float32),
    )
    grad_mid = upstream + back_mid
    grad_branch = grad_mid.astype(jnp.bfloat16)
    grad_out = jnp.dot(attended.T, grad_branch, preferred_element_type=jnp.float32)
    grad_att = (
        jnp.dot(grad_branch, w_out.T, preferred_element_type=jnp.float32)
        .astype(jnp.bfloat16)
        .reshape(row_count, HEADS, head_dim)
    )
    grad_value = jnp.einsum("hqk,qhe->khe", probs_low, grad_att, preferred_element_type=jnp.float32)
    grad_probs = jnp.einsum(
        "qhe,khe->hqk", grad_att, value_rows, preferred_element_type=jnp.float32
    )
    grad_scores = (
        attn_probs * (grad_probs - jnp.sum(attn_probs * grad_probs, axis=-1, keepdims=True))
    ).astype(jnp.bfloat16)
    grad_query = jnp.einsum(
        "hqk,khe->qhe", grad_scores, key_rows, preferred_element_type=jnp.float32
    ) * head_dim ** (-0.5)
    grad_key = jnp.einsum(
        "hqk,qhe->khe", grad_scores, queries, preferred_element_type=jnp.float32
    ) * head_dim ** (-0.5)
    grad_qkv = jnp.concatenate(
        [
            grad_query.reshape(row_count, model_width),
            grad_key.reshape(row_count, model_width),
            grad_value.reshape(row_count, model_width),
        ],
        axis=1,
    ).astype(jnp.bfloat16)
    grad_wqkv = jnp.dot(normed.T, grad_qkv, preferred_element_type=jnp.float32)
    back_in, gain_one = norm_back(
        stream,
        scale_one,
        gain_pair[0],
        jnp.dot(grad_qkv, w_qkv.T, preferred_element_type=jnp.float32),
    )
    return (
        grad_mid + back_in,
        (grad_wqkv, grad_out, grad_up, grad_down),
        jnp.stack([gain_one, gain_two]),
    )


def spectral_terms(output, target, length, present_row, frame_count):
    row_count, model_width = output.shape
    bin_count = model_width // 8
    spectra = output.reshape(row_count, 4, 2, bin_count)
    real_part = spectra[:, :, 0]
    imag_part = spectra[:, :, 1]
    magnitude = jnp.sqrt(real_part * real_part + imag_part * imag_part + 0.01)
    differ = magnitude - target.reshape(row_count, 4, bin_count)
    smooth_err = jnp.sqrt(differ * differ + 0.01)
    weight = (jnp.arange(row_count) < length).astype(jnp.float32)[:, None, None] * present_row[
        None, :, None
    ]
    loss_slope = weight * differ / smooth_err / magnitude / frame_count
    grad_spec = jnp.stack([loss_slope * real_part, loss_slope * imag_part], axis=2).reshape(
        row_count, model_width
    )
    return (jnp.sum(smooth_err * weight), grad_spec)


def body(
    x_in,
    targets,
    valid_len,
    present_stems,
    w_master,
    norm_gains,
    gain_m,
    gain_v,
    l_stats,
    r_stats,
    l_roots,
    r_roots,
    step_count,
):
    model_width = x_in.shape[1]
    block_size = model_width // 4
    sections = lax.axis_size("section")
    section_idx = lax.axis_index("section")
    half_way = sections // 2
    groups = lax.axis_size("dp")
    group_idx = lax.axis_index("dp")
    micro_count = valid_len.shape[0] // groups
    seg_len = x_in.shape[0] // micro_count
    own_blocks = w_master.shape[1]
    own_gain = norm_gains.shape[2]
    full_w, full_g = (
        lax.all_gather(w_master.astype(jnp.bfloat16), "dp", axis=1, tiled=True),
        lax.all_gather(norm_gains.astype(jnp.bfloat16), "dp", axis=2, tiled=True),
    )
    matrices = split_matrices(full_w[0], model_width)
    gain_pair = full_g[0].astype(jnp.float32)
    lengths = lax.dynamic_slice_in_dim(valid_len, group_idx * micro_count, micro_count)
    stem_flags = lax.dynamic_slice_in_dim(
        present_stems, group_idx * micro_count, micro_count
    ).astype(jnp.float32)
    frame_count = jnp.sum(valid_len).astype(jnp.float32)
    decoder = section_idx >= half_way
    encoder = section_idx < half_way
    is_last = section_idx == sections - 1
    act_shape = (micro_count, seg_len, model_width)

    def forward_step(step_idx, loop_state):
        in_rows, kept_prev, skip_store, loss_grads, loss_sum, sq_sums = loop_state
        micro_idx = step_idx - section_idx
        active = (micro_idx >= 0) & (micro_idx < micro_count)
        slot_idx = jnp.clip(micro_idx, 0, micro_count - 1)
        fresh_rows = lax.dynamic_slice_in_dim(x_in, slot_idx * seg_len, seg_len, 0)
        previous = jnp.where(section_idx == 0, fresh_rows, in_rows)
        stream = previous.astype(jnp.float32) + jnp.where(
            decoder, skip_store[slot_idx].astype(jnp.float32), 0.0
        )
        length = lengths[slot_idx]
        target = lax.dynamic_slice_in_dim(targets, slot_idx * seg_len, seg_len, 0)

        def forward_compute_fn(operand):
            output, branch_attn, branch_ffn, kept_vals = layer_forward(
                stream, matrices, gain_pair, length
            )
            valid = (jnp.arange(seg_len) < length).astype(jnp.float32)[:, None]
            squares = jnp.stack(
                [
                    jnp.sum(valid * stream * stream),
                    jnp.sum(valid * branch_attn * branch_attn),
                    jnp.sum(valid * branch_ffn * branch_ffn),
                ]
            )
            seg_loss, grad_spec = spectral_terms(
                output, target, length, stem_flags[slot_idx], frame_count
            )
            return (output, squares, seg_loss, grad_spec)

        def forward_spare_fn(operand):
            empty = jnp.zeros((seg_len, model_width), jnp.float32)
            return (empty, jnp.zeros((3,), jnp.float32), jnp.zeros((), jnp.float32), empty)

        output, squares, seg_loss, grad_spec = lax.cond(
            active, forward_compute_fn, forward_spare_fn, 0
        )
        kept_prev = kept_prev.at[slot_idx].set(jnp.where(active, previous, kept_prev[slot_idx]))
        loss_grads = loss_grads.at[slot_idx].set(
            jnp.where(active & is_last, grad_spec, loss_grads[slot_idx])
        )
        loss_sum = loss_sum + jnp.where(is_last, seg_loss, 0.0)
        sq_sums = sq_sums + squares
        sent_rows = output.astype(jnp.bfloat16)
        in_rows = from_behind(sent_rows, "section", 1)
        from_encoder = from_behind(sent_rows, "section", half_way)
        recv_idx = step_idx - section_idx + half_way
        usable = decoder & (recv_idx >= 0) & (recv_idx < micro_count)
        recv_slot = jnp.clip(recv_idx, 0, micro_count - 1)
        skip_store = skip_store.at[recv_slot].set(
            jnp.where(usable, from_encoder, skip_store[recv_slot])
        )
        return (in_rows, kept_prev, skip_store, loss_grads, loss_sum, sq_sums)

    start_state = (
        jnp.zeros((seg_len, model_width), jnp.bfloat16),
        jnp.zeros(act_shape, jnp.bfloat16),
        jnp.zeros(act_shape, jnp.bfloat16),
        jnp.zeros(act_shape, jnp.float32),
        jnp.zeros((), jnp.float32),
        jnp.zeros((3,), jnp.float32),
    )
    unused_rows, kept_prev, skip_store, loss_grads, loss_sum, sq_sums = lax.fori_loop(
        0, micro_count + sections - 1, forward_step, start_state
    )

    def backward_step(step_idx, loop_state):
        in_grads, skip_grad_store, grad_mats, grad_gains = loop_state
        micro_idx = step_idx - (sections - 1 - section_idx)
        active = (micro_idx >= 0) & (micro_idx < micro_count)
        slot_idx = jnp.clip(micro_idx, 0, micro_count - 1)
        upstream = jnp.where(
            is_last,
            loss_grads[slot_idx],
            in_grads.astype(jnp.float32)
            + jnp.where(encoder, skip_grad_store[slot_idx].astype(jnp.float32), 0.0),
        )
        stream = kept_prev[slot_idx].astype(jnp.float32) + jnp.where(
            decoder, skip_store[slot_idx].astype(jnp.float32), 0.0
        )
        length = lengths[slot_idx]

        def backward_compute_fn(operand):
            return layer_backward(stream, matrices, gain_pair, length, upstream)

        def backward_spare_fn(operand):
            return (
                jnp.zeros_like(stream),
                tuple((jnp.zeros(mat.shape, jnp.float32) for mat in matrices)),
                jnp.zeros((2, model_width), jnp.float32),
            )

        grad_stream, layer_mats, layer_gains = lax.cond(
            active, backward_compute_fn, backward_spare_fn, 0
        )
        grad_mats = tuple((total + piece for total, piece in zip(grad_mats, layer_mats)))
        grad_gains = grad_gains + layer_gains
        grad_rows = grad_stream.astype(jnp.bfloat16)
        in_grads = from_behind(grad_rows, "section", -1)
        from_decoder = from_behind(grad_rows, "section", -half_way)
        recv_idx = micro_idx + half_way
        usable = encoder & (recv_idx >= 0) & (recv_idx < micro_count)
        recv_slot = jnp.clip(recv_idx, 0, micro_count - 1)
        skip_grad_store = skip_grad_store.at[recv_slot].set(
            jnp.where(usable, from_decoder, skip_grad_store[recv_slot])
        )
        return (in_grads, skip_grad_store, grad_mats, grad_gains)

    back_state = (
        jnp.zeros((seg_len, model_width), jnp.bfloat16),
        jnp.zeros(act_shape, jnp.bfloat16),
        tuple((jnp.zeros(mat.shape, jnp.float32) for mat in matrices)),
        jnp.zeros((2, model_width), jnp.float32),
    )
    unused_grads, unused_store, grad_mats, grad_gains = lax.fori_loop(
        0, micro_count + sections - 1, backward_step, back_state
    )
    grad_all = jnp.concatenate([to_blocks(mat, block_size) for mat in grad_mats], axis=0)
    summed_w, summed_g = lax.psum((grad_all, grad_gains), "dp")
    own_grad = lax.dynamic_slice_in_dim(summed_w, group_idx * own_blocks, own_blocks, 0)
    own_gain_grad = lax.dynamic_slice_in_dim(summed_g, group_idx * own_gain, own_gain, 1)
    own_square = jnp.sum(own_grad * own_grad) + jnp.sum(own_gain_grad * own_gain_grad)
    rows_local = jnp.zeros((sections, 3), jnp.float32).at[section_idx].set(sq_sums)
    total_square, loss_value, rows_total = lax.psum(
        (own_square, loss_sum / frame_count, rows_local), ("section", "dp")
    )
    grad_norm = jnp.sqrt(total_square)
    clip_limit = 0.00015 * math.sqrt(
        sections * (own_blocks * groups * block_size * block_size + 2 * model_width)
    )
    factor = clip_limit / jnp.maximum(grad_norm, clip_limit)
    grad_blocks = own_grad * factor
    square = (own_blocks, block_size, block_size)
    shaped = grad_blocks.reshape(square)
    highest = lax.Precision.HIGHEST
    l_new = 0.95 * l_stats[0].reshape(square) + 0.05 * jnp.einsum(
        "bij,bkj->bik", shaped, shaped, precision=highest
    )
    r_new = 0.95 * r_stats[0].reshape(square) + 0.05 * jnp.einsum(
        "bji,bjk->bik", shaped, shaped, precision=highest
    )
    left_side = jnp.einsum("bij,bjk->bik", l_roots[0].reshape(square), shaped, precision=highest)
    precond = jnp.einsum("bij,bjk->bik", left_side, r_roots[0].reshape(square), precision=highest)
    master = w_master[0]
    w_new = master - 0.5 * (precond.reshape(master.shape) + 0.01 * master)
    gain_grad = own_gain_grad * factor
    m_new = 0.9 * gain_m[0] + 0.1 * gain_grad
    v_new = 0.999 * gain_v[0] + 0.001 * gain_grad * gain_grad
    step_num = step_count[0].astype(jnp.float32)
    m_hat = m_new / (1.0 - jnp.power(0.9, step_num))
    v_hat = v_new / (1.0 - jnp.power(0.999, step_num))
    gains_new = norm_gains[0] - 0.5 * m_hat / (jnp.sqrt(v_hat) + 1e-08)
    rms = jnp.sqrt(rows_total[section_idx] / (frame_count * model_width)).reshape(1, 3)
    return (
        w_new[None],
        grad_blocks[None],
        l_new.reshape(master.shape)[None],
        r_new.reshape(master.shape)[None],
        gains_new[None],
        m_new[None],
        v_new[None],
        loss_value,
        grad_norm,
        rms,
    )


def solution(mesh):
    return jax.shard_map(
        body,
        mesh=mesh,
        in_specs=(
            P("dp", None),
            P("dp", None),
            P(),
            P(),
            P("section", "dp", None),
            P("section", None, "dp"),
            P("section", None, "dp"),
            P("section", None, "dp"),
            P("section", "dp", None),
            P("section", "dp", None),
            P("section", "dp", None),
            P("section", "dp", None),
            P(),
        ),
        out_specs=(
            P("section", "dp", None),
            P("section", "dp", None),
            P("section", "dp", None),
            P("section", "dp", None),
            P("section", None, "dp"),
            P("section", None, "dp"),
            P("section", None, "dp"),
            P(),
            P(),
            P("section", None),
        ),
        check_vma=False,
    )
```

profile of v0, /device:TPU:2, one launch (start us, length us, event | category | flops | bytes accessed | tf_op | source)
XLA Modules:
  0.0 1375.6 jit_solution(1695151941423023869)
XLA Ops:
  14.1 31.4 %all_gather.6 = bf16[1,2,384]{1,0,2:T(2,128)(2,1)S(1)} all-gather(bf16[1,2,48]{1,0,2:T(2,128)(2,1)S(1)} %copy.192), channel_id=1, replica_groups=mesh['section'=4,'dp'=8] {'dp'}, dimensions={2}, use_global_device_ids=true | all-gather | bytes 1728 | tf_op jit(solution)/shard_map/all_gather | solution.py:240
  45.8 32.6 %all-gather.2.cloned.1.call-done = bf16[1,192,9216]{2,1,0:T(8,128)(2,1)} async-done(((bf16[1,24,9216]{2,1,0:T(8,128)(2,1)}), bf16[1,192,9216]{2,1,0:T(8,128)(2,1)}) %all-gather.2.cloned.1.call-update) | async-done | bytes 3538960 | tf_op jit(solution)/shard_map/all_gather | solution.py:239
  102.2 424.0 %while.58 = (s32[]{:T(128)}, bf16[512,384]{0,1:T(8,128)(2,1)S(1)}, bf16[4,512,384]{1,2,0:T(8,128)(2,1)}, bf16[4,512,384]{1,2,0:T(8,128)(2,1)S(1)}, f32[4,512,384...) while((s32[]{:T(128)}, bf16[512,384]{0,1:T(8,128)(2,1)S(1)}, ...), condition=%wide.region_14.15_spmd.clone, body=%wide.region_1.14_spmd.clone.sunk | while | flops 2289604096 | bytes 59352684 | solution.py:316
  119.2 38.0 %collective-permute-done.1 = bf16[512,384]{0,1:T(8,128)(2,1)} collective-permute-done((bf16[512,384]{0,1:T(8,128)(2,1)}, bf16[512,384]{0,1:T(8,128)(2,1)}, u32[]{:S(2)}, u32[]{:S(2)}) %collective-permute-start.1) | collective-permute-done | bytes 393248 | tf_op jit(solution)/shard_map/while/body/eval_jaxpr/ppermute | solution.py:15
  174.5 40.1 %collective-permute-done = bf16[512,384]{0,1:T(8,128)(2,1)} collective-permute-done((bf16[512,384]{0,1:T(8,128)(2,1)}, bf16[512,384]{0,1:T(8,128)(2,1)}, u32[]{:S(2)}, u32[]{:S(2)}) %collective-permute-start) | collective-permute-done | bytes 393248 | tf_op jit(solution)/shard_map/while/body/eval_jaxpr/ppermute | solution.py:15
  222.2 45.3 %conditional.6 = (f32[3]{0:T(128)}, f32[]{:T(128)}, f32[512,384]{0,1:T(8,128)S(1)}, bf16[512,384]{0,1:T(8,128)(2,1)}) conditional(s32[]{:T(128)} %convert_element_type.378, () %tuple.195, (s32[4]{0:T(128)}, s32[]{:T(128)}, pred[]{:T(512)}, bf16[4,512,384]{1,2,0:T(8,128)(2,1)S(1)}, f32[512,384]{0,1:T(8,128)S(1)}, /*index=5*/f32[2,384]{1,0:T(2,128)S(1)}, ...), branch_computations={%region_2.2_spmd, %region_3.11_spmd} | conditional | flops 2287834624 | bytes 44013292 | solution.py:288
  232.8 7.9 fusion.178
  247.5 12.2 fusion.172
  285.6 45.3 %conditional.6 = (f32[3]{0:T(128)}, f32[]{:T(128)}, f32[512,384]{0,1:T(8,128)S(1)}, bf16[512,384]{0,1:T(8,128)(2,1)}) conditional(s32[]{:T(128)} %convert_element_type.378, () %tuple.195, (s32[4]{0:T(128)}, s32[]{:T(128)}, pred[]{:T(512)}, bf16[4,512,384]{1,2,0:T(8,128)(2,1)S(1)}, f32[512,384]{0,1:T(8,128)S(1)}, /*index=5*/f32[2,384]{1,0:T(2,128)S(1)}, ...), branch_computations={%region_2.2_spmd, %region_3.11_spmd} | conditional | flops 2287834624 | bytes 44013292 | solution.py:288
  296.2 7.9 fusion.178
  310.9 12.2 fusion.172
  349.0 45.3 %conditional.6 = (f32[3]{0:T(128)}, f32[]{:T(128)}, f32[512,384]{0,1:T(8,128)S(1)}, bf16[512,384]{0,1:T(8,128)(2,1)}) conditional(s32[]{:T(128)} %convert_element_type.378, () %tuple.195, (s32[4]{0:T(128)}, s32[]{:T(128)}, pred[]{:T(512)}, bf16[4,512,384]{1,2,0:T(8,128)(2,1)S(1)}, f32[512,384]{0,1:T(8,128)S(1)}, /*index=5*/f32[2,384]{1,0:T(2,128)S(1)}, ...), branch_computations={%region_2.2_spmd, %region_3.11_spmd} | conditional | flops 2287834624 | bytes 44013292 | solution.py:288
  359.5 7.9 fusion.178
  374.3 12.2 fusion.172
  412.2 45.2 %conditional.6 = (f32[3]{0:T(128)}, f32[]{:T(128)}, f32[512,384]{0,1:T(8,128)S(1)}, bf16[512,384]{0,1:T(8,128)(2,1)}) conditional(s32[]{:T(128)} %convert_element_type.378, () %tuple.195, (s32[4]{0:T(128)}, s32[]{:T(128)}, pred[]{:T(512)}, bf16[4,512,384]{1,2,0:T(8,128)(2,1)S(1)}, f32[512,384]{0,1:T(8,128)S(1)}, /*index=5*/f32[2,384]{1,0:T(2,128)S(1)}, ...), branch_computations={%region_2.2_spmd, %region_3.11_spmd} | conditional | flops 2287834624 | bytes 44013292 | solution.py:288
  422.8 7.9 fusion.178
  437.5 12.2 fusion.172
  477.7 36.6 %collective-permute-start = (bf16[512,384]{0,1:T(8,128)(2,1)}, bf16[512,384]{0,1:T(8,128)(2,1)}, u32[]{:S(2)}, u32[]{:S(2)}) collective-permute-start(bf16[512,384]{0,1:T(8,128)(2,1)} %get-tuple-element.2080), channel_id=1, source_target_pairs={{0,8},{8,16},{16,24},{1,9},{9,17},{17,25},{2,10},{10,18},{18,26},{... | collective-permute-start | bytes 1179656 | tf_op jit(solution)/shard_map/while/body/eval_jaxpr/ppermute | solution.py:15
  528.2 497.3 %while.59 = (s32[]{:T(128)}, bf16[512,384]{0,1:T(8,128)(2,1)}, bf16[4,512,384]{1,2,0:T(8,128)(2,1)}, f32[384,1152]{1,0:T(8,128)}, f32[384,384]{1,0:T(8,128)}, /*...) while((s32[]{:T(128)}, bf16[512,384]{0,1:T(8,128)(2,1)}, ...), condition=%wide.region_28.29_spmd.clone, body=%wide.region_15.28_spmd.clone.sunk | while | flops 6157961216 | bytes 282397248 | solution.py:368
  529.6 4.8 conditional.7
  534.3 5.9 collective-permute-start.3
  555.5 30.8 %collective-permute-done.2 = bf16[512,384]{0,1:T(8,128)(2,1)} collective-permute-done((bf16[512,384]{0,1:T(8,128)(2,1)}, bf16[512,384]{0,1:T(8,128)(2,1)}, u32[]{:S(2)}, u32[]{:S(2)}) %collective-permute-start.2) | collective-permute-done | bytes 393248 | tf_op jit(solution)/shard_map/while/body/eval_jaxpr/ppermute | solution.py:15
  587.4 53.0 %conditional.7 = (f32[384,1152]{1,0:T(8,128)}, f32[384,384]{1,0:T(8,128)}, f32[384,1536]{1,0:T(8,128)S(1)}, f32[1536,384]{1,0:T(8,128)}, f32[2,384]{1,0:T(2,128)S(1)}, /*index=5*/bf16[512,384]{0,1:T(8,128)(2,1)}) conditional(s32[]{:T(128)} %convert_element_type.379, () %tuple.198, (s32[]{:T(128)}, bf16[4,512,384]{1,2,0:T(8,128)(2,1)}, pred[]{:T(512)}, ...), branch_computations={%region_16.16_spmd, %region_17.26_spmd} | conditional | flops 6154027520 | bytes 205684368 | solution.py:346
  597.0 6.5 fusion.176
  604.4 4.3 fusion.99
  631.9 8.6 fusion.95
  660.8 53.0 %conditional.7 = (f32[384,1152]{1,0:T(8,128)}, f32[384,384]{1,0:T(8,128)}, f32[384,1536]{1,0:T(8,128)S(1)}, f32[1536,384]{1,0:T(8,128)}, f32[2,384]{1,0:T(2,128)S(1)}, /*index=5*/bf16[512,384]{0,1:T(8,128)(2,1)}) conditional(s32[]{:T(128)} %convert_element_type.379, () %tuple.198, (s32[]{:T(128)}, bf16[4,512,384]{1,2,0:T(8,128)(2,1)}, pred[]{:T(512)}, ...), branch_computations={%region_16.16_spmd, %region_17.26_spmd} | conditional | flops 6154027520 | bytes 205684368 | solution.py:346
  670.4 6.5 fusion.176
  677.8 4.3 fusion.99
  705.2 8.6 fusion.95
  715.9 5.1 collective-permute-start.2
  737.4 53.0 %conditional.7 = (f32[384,1152]{1,0:T(8,128)}, f32[384,384]{1,0:T(8,128)}, f32[384,1536]{1,0:T(8,128)S(1)}, f32[1536,384]{1,0:T(8,128)}, f32[2,384]{1,0:T(2,128)S(1)}, /*index=5*/bf16[512,384]{0,1:T(8,128)(2,1)}) conditional(s32[]{:T(128)} %convert_element_type.379, () %tuple.198, (s32[]{:T(128)}, bf16[4,512,384]{1,2,0:T(8,128)(2,1)}, pred[]{:T(512)}, ...), branch_computations={%region_16.16_spmd, %region_17.26_spmd} | conditional | flops 6154027520 | bytes 205684368 | solution.py:346
  747.0 6.5 fusion.176
  781.8 8.6 fusion.95
  811.0 53.0 %conditional.7 = (f32[384,1152]{1,0:T(8,128)}, f32[384,384]{1,0:T(8,128)}, f32[384,1536]{1,0:T(8,128)S(1)}, f32[1536,384]{1,0:T(8,128)}, f32[2,384]{1,0:T(2,128)S(1)}, /*index=5*/bf16[512,384]{0,1:T(8,128)(2,1)}) conditional(s32[]{:T(128)} %convert_element_type.379, () %tuple.198, (s32[]{:T(128)}, bf16[4,512,384]{1,2,0:T(8,128)(2,1)}, pred[]{:T(512)}, ...), branch_computations={%region_16.16_spmd, %region_17.26_spmd} | conditional | flops 6154027520 | bytes 205684368 | solution.py:346
  820.6 6.5 fusion.176
  855.4 8.6 fusion.95
  884.6 4.8 conditional.7
  889.4 46.6 %collective-permute-start.3 = (bf16[512,384]{0,1:T(8,128)(2,1)}, bf16[512,384]{0,1:T(8,128)(2,1)}, u32[]{:S(2)}, u32[]{:S(2)}) collective-permute-start(bf16[512,384]{0,1:T(8,128)(2,1)} %get-tuple-element.2109), channel_id=1, source_target_pairs={{16,0},{24,8},{17,1},{25,9},{18,2},{26,10},{19,3},{27,11},{20,4},{... | collective-permute-start | bytes 1179656 | tf_op jit(solution)/shard_map/while/body/eval_jaxpr/ppermute | solution.py:15
  936.0 4.8 collective-permute-start.2
  957.2 4.8 conditional.7
  962.0 46.0 %collective-permute-start.3 = (bf16[512,384]{0,1:T(8,128)(2,1)}, bf16[512,384]{0,1:T(8,128)(2,1)}, u32[]{:S(2)}, u32[]{:S(2)}) collective-permute-start(bf16[512,384]{0,1:T(8,128)(2,1)} %get-tuple-element.2109), channel_id=1, source_target_pairs={{16,0},{24,8},{17,1},{25,9},{18,2},{26,10},{19,3},{27,11},{20,4},{... | collective-permute-start | bytes 1179656 | tf_op jit(solution)/shard_map/while/body/eval_jaxpr/ppermute | solution.py:15
  1031.0 4.4 reshape.618
  1042.4 4.4 reshape.620
  1062.3 4.9 pad_maximum_fusion.6
  1077.5 19.9 %psum.36 = f32[2,384]{1,0:T(2,128)S(1)} all-reduce(f32[2,384]{1,0:T(2,128)S(1)} %copy-done.36), channel_id=1, replica_groups=mesh['section'=4,'dp'=8] {'dp'}, use_global_device_ids=true, to_apply=%region_31.32 | all-reduce | flops 768 | bytes 6144 | tf_op jit(solution)/shard_map/psum | solution.py:372
  1098.0 202.9 %all-reduce.3.cloned.1.call-done = f32[192,9216]{1,0:T(8,128)} async-done(((f32[192,9216]{1,0:T(8,128)}), f32[192,9216]{1,0:T(8,128)}) %all-reduce.3.cloned.1.call-update) | async-done | bytes 7077904 | tf_op jit(solution)/shard_map/psum | solution.py:372
  1304.2 40.4 %all-reduce = (f32[]{:T(128)}, f32[]{:T(128)}, f32[4,3]{1,0:T(4,128)}) all-reduce(f32[]{:T(128)S(6)} %add.412, f32[]{:T(128)S(6)} %div.90, f32[4,3]{1,0:T(4,128)S(1)} %scatter.19), channel_id=1, replica_groups=mesh['section'=4,'dp'=8] {'section','dp'}, use_global_device_ids=true, to_apply=%region_33.34 | all-reduce | flops 14 | bytes 112 | tf_op jit(solution)/shard_map/psum | solution.py:377
  (873 shorter events, 609.3 us)
Async XLA Ops:
  7.2 71.2 %all-gather.2.cloned.1.call-start = ((), (), s32[]{:S(2)}) async-start(), calls=%async_computation | async-start | bytes 3981312 | tf_op jit(solution)/shard_map/all_gather | solution.py:239
  9.2 1291.7 %all-reduce.3.cloned.1.call-start = ((), (), s32[]{:S(2)}) async-start(), calls=%async_computation.1 | async-start | bytes 14155776 | tf_op jit(solution)/shard_map/psum | solution.py:372
  105.4 9.2 copy-start.38
  105.4 51.7 %collective-permute-start.1 = (bf16[512,384]{0,1:T(8,128)(2,1)}, bf16[512,384]{0,1:T(8,128)(2,1)}, u32[]{:S(2)}, u32[]{:S(2)}) collective-permute-start(bf16[512,384]{0,1:T(8,128)(2,1)} %get-tuple-element.2080), channel_id=1, source_target_pairs={{0,16},{8,24},{1,17},{9,25},{2,18},{10,26},{3,19},{11,27},{4,20},{... | collective-permute-start | bytes 1179656 | tf_op jit(solution)/shard_map/while/body/eval_jaxpr/ppermute | solution.py:15
  106.9 11.3 collective-permute-start
  115.2 43.7 %copy-start.39 = (f32[3]{0:T(128)}, f32[3]{0:T(128)S(1)}, u32[]{:S(2)}) copy-start(f32[3]{0:T(128)S(1)} %fusion.234) | copy-start | bytes 40 | tf_op jit(solution)/shard_map/while
  161.8 9.2 copy-start.38
  161.8 57.3 %collective-permute-start.1 = (bf16[512,384]{0,1:T(8,128)(2,1)}, bf16[512,384]{0,1:T(8,128)(2,1)}, u32[]{:S(2)}, u32[]{:S(2)}) collective-permute-start(bf16[512,384]{0,1:T(8,128)(2,1)} %get-tuple-element.2080), channel_id=1, source_target_pairs={{0,16},{8,24},{1,17},{9,25},{2,18},{10,26},{3,19},{11,27},{4,20},{... | collective-permute-start | bytes 1179656 | tf_op jit(solution)/shard_map/while/body/eval_jaxpr/ppermute | solution.py:15
  163.2 51.4 %collective-permute-start = (bf16[512,384]{0,1:T(8,128)(2,1)}, bf16[512,384]{0,1:T(8,128)(2,1)}, u32[]{:S(2)}, u32[]{:S(2)}) collective-permute-start(bf16[512,384]{0,1:T(8,128)(2,1)} %get-tuple-element.2080), channel_id=1, source_target_pairs={{0,8},{8,16},{16,24},{1,9},{9,17},{17,25},{2,10},{10,18},{18,26},{... | collective-permute-start | bytes 1179656 | tf_op jit(solution)/shard_map/while/body/eval_jaxpr/ppermute | solution.py:15
  171.6 49.3 %copy-start.39 = (f32[3]{0:T(128)}, f32[3]{0:T(128)S(1)}, u32[]{:S(2)}) copy-start(f32[3]{0:T(128)S(1)} %fusion.234) | copy-start | bytes 40 | tf_op jit(solution)/shard_map/while
  267.5 14.9 %collective-permute-start.1 = (bf16[512,384]{0,1:T(8,128)(2,1)}, bf16[512,384]{0,1:T(8,128)(2,1)}, u32[]{:S(2)}, u32[]{:S(2)}) collective-permute-start(bf16[512,384]{0,1:T(8,128)(2,1)} %get-tuple-element.2080), channel_id=1, source_target_pairs={{0,16},{8,24},{1,17},{9,25},{2,18},{10,26},{3,19},{11,27},{4,20},{... | collective-permute-start | bytes 1179656 | tf_op jit(solution)/shard_map/while/body/eval_jaxpr/ppermute | solution.py:15
  268.8 11.3 collective-permute-start
  330.9 14.9 %collective-permute-start.1 = (bf16[512,384]{0,1:T(8,128)(2,1)}, bf16[512,384]{0,1:T(8,128)(2,1)}, u32[]{:S(2)}, u32[]{:S(2)}) collective-permute-start(bf16[512,384]{0,1:T(8,128)(2,1)} %get-tuple-element.2080), channel_id=1, source_target_pairs={{0,16},{8,24},{1,17},{9,25},{2,18},{10,26},{3,19},{11,27},{4,20},{... | collective-permute-start | bytes 1179656 | tf_op jit(solution)/shard_map/while/body/eval_jaxpr/ppermute | solution.py:15
  332.2 12.4 collective-permute-start
  394.2 9.1 copy-start.38
  394.2 15.8 %collective-permute-start.1 = (bf16[512,384]{0,1:T(8,128)(2,1)}, bf16[512,384]{0,1:T(8,128)(2,1)}, u32[]{:S(2)}, u32[]{:S(2)}) collective-permute-start(bf16[512,384]{0,1:T(8,128)(2,1)} %get-tuple-element.2080), channel_id=1, source_target_pairs={{0,16},{8,24},{1,17},{9,25},{2,18},{10,26},{3,19},{11,27},{4,20},{... | collective-permute-start | bytes 1179656 | tf_op jit(solution)/shard_map/while/body/eval_jaxpr/ppermute | solution.py:15
  395.5 13.5 collective-permute-start
  457.4 15.2 %collective-permute-start.1 = (bf16[512,384]{0,1:T(8,128)(2,1)}, bf16[512,384]{0,1:T(8,128)(2,1)}, u32[]{:S(2)}, u32[]{:S(2)}) collective-permute-start(bf16[512,384]{0,1:T(8,128)(2,1)} %get-tuple-element.2080), channel_id=1, source_target_pairs={{0,16},{8,24},{1,17},{9,25},{2,18},{10,26},{3,19},{11,27},{4,20},{... | collective-permute-start | bytes 1179656 | tf_op jit(solution)/shard_map/while/body/eval_jaxpr/ppermute | solution.py:15
  458.7 12.9 collective-permute-start
  476.3 43.9 %copy-start.38 = (f32[3]{0:T(128)S(1)}, f32[3]{0:T(128)}, u32[]{:S(2)}) copy-start(f32[3]{0:T(128)} %get-tuple-element.2172) | copy-start | bytes 40 | tf_op jit(solution)/shard_map/while
  476.3 49.1 %collective-permute-start.1 = (bf16[512,384]{0,1:T(8,128)(2,1)}, bf16[512,384]{0,1:T(8,128)(2,1)}, u32[]{:S(2)}, u32[]{:S(2)}) collective-permute-start(bf16[512,384]{0,1:T(8,128)(2,1)} %get-tuple-element.2080), channel_id=1, source_target_pairs={{0,16},{8,24},{1,17},{9,25},{2,18},{10,26},{3,19},{11,27},{4,20},{... | collective-permute-start | bytes 1179656 | tf_op jit(solution)/shard_map/while/body/eval_jaxpr/ppermute | solution.py:15
  477.7 46.7 %collective-permute-start = (bf16[512,384]{0,1:T(8,128)(2,1)}, bf16[512,384]{0,1:T(8,128)(2,1)}, u32[]{:S(2)}, u32[]{:S(2)}) collective-permute-start(bf16[512,384]{0,1:T(8,128)(2,1)} %get-tuple-element.2080), channel_id=1, source_target_pairs={{0,8},{8,16},{16,24},{1,9},{9,17},{17,25},{2,10},{10,18},{18,26},{... | collective-permute-start | bytes 1179656 | tf_op jit(solution)/shard_map/while/body/eval_jaxpr/ppermute | solution.py:15
  534.3 19.6 %collective-permute-start.3 = (bf16[512,384]{0,1:T(8,128)(2,1)}, bf16[512,384]{0,1:T(8,128)(2,1)}, u32[]{:S(2)}, u32[]{:S(2)}) collective-permute-start(bf16[512,384]{0,1:T(8,128)(2,1)} %get-tuple-element.2109), channel_id=1, source_target_pairs={{16,0},{24,8},{17,1},{25,9},{18,2},{26,10},{19,3},{27,11},{20,4},{... | collective-permute-start | bytes 1179656 | tf_op jit(solution)/shard_map/while/body/eval_jaxpr/ppermute | solution.py:15
  540.2 46.0 %collective-permute-start.2 = (bf16[512,384]{0,1:T(8,128)(2,1)}, bf16[512,384]{0,1:T(8,128)(2,1)}, u32[]{:S(2)}, u32[]{:S(2)}) collective-permute-start(bf16[512,384]{0,1:T(8,128)(2,1)} %get-tuple-element.2109), channel_id=1, source_target_pairs={{8,0},{16,8},{24,16},{9,1},{17,9},{25,17},{10,2},{18,10},{26,18},{... | collective-permute-start | bytes 1179656 | tf_op jit(solution)/shard_map/while/body/eval_jaxpr/ppermute | solution.py:15
  549.5 36.7 %copy-start.9 = (f32[384,1152]{1,0:T(8,128)}, f32[384,1152]{1,0:T(8,128)S(1)}, u32[]{:S(2)}) copy-start(f32[384,1152]{1,0:T(8,128)S(1)} %select_add_fusion.13) | copy-start | bytes 5308420 | tf_op jit(solution)/shard_map/while
  549.5 36.7 %copy-start.3 = (bf16[4,512,384]{1,2,0:T(8,128)(2,1)S(1)}, bf16[4,512,384]{1,2,0:T(8,128)(2,1)}, u32[]{:S(2)}) copy-start(bf16[4,512,384]{1,2,0:T(8,128)(2,1)} %copy-done.2) | copy-start | bytes 4718596 | tf_op jit(solution)/shard_map/while
  552.1 34.1 %copy-start.35 = (f32[2,384]{1,0:T(2,128)}, f32[2,384]{1,0:T(2,128)S(1)}, u32[]{:S(2)}) copy-start(f32[2,384]{1,0:T(2,128)S(1)} %select_add_fusion.17) | copy-start | bytes 9220 | tf_op jit(solution)/shard_map/while
  587.4 37.9 %copy-start.4 = (bf16[4,512,384]{1,2,0:T(8,128)(2,1)}, bf16[4,512,384]{1,2,0:T(8,128)(2,1)S(1)}, u32[]{:S(2)}) copy-start(bf16[4,512,384]{1,2,0:T(8,128)(2,1)S(1)} %get-tuple-element.1251) | copy-start | bytes 4718596 | tf_op jit(solution)/shard_map/while/body/eval_jaxpr/cond
  590.4 35.0 %copy-start.31 = (f32[384]{0:T(512)}, f32[384]{0:T(512)S(1)}, u32[]{:S(2)}) copy-start(f32[384]{0:T(512)S(1)} %get-tuple-element.1707) | copy-start | bytes 4612 | tf_op jit(solution)/shard_map/while/body/eval_jaxpr/cond
  640.5 17.6 %collective-permute-start.3 = (bf16[512,384]{0,1:T(8,128)(2,1)}, bf16[512,384]{0,1:T(8,128)(2,1)}, u32[]{:S(2)}, u32[]{:S(2)}) collective-permute-start(bf16[512,384]{0,1:T(8,128)(2,1)} %get-tuple-element.2109), channel_id=1, source_target_pairs={{16,0},{24,8},{17,1},{25,9},{18,2},{26,10},{19,3},{27,11},{20,4},{... | collective-permute-start | bytes 1179656 | tf_op jit(solution)/shard_map/while/body/eval_jaxpr/ppermute | solution.py:15
  642.5 17.0 %collective-permute-start.2 = (bf16[512,384]{0,1:T(8,128)(2,1)}, bf16[512,384]{0,1:T(8,128)(2,1)}, u32[]{:S(2)}, u32[]{:S(2)}) collective-permute-start(bf16[512,384]{0,1:T(8,128)(2,1)} %get-tuple-element.2109), channel_id=1, source_target_pairs={{8,0},{16,8},{24,16},{9,1},{17,9},{25,17},{10,2},{18,10},{26,18},{... | collective-permute-start | bytes 1179656 | tf_op jit(solution)/shard_map/while/body/eval_jaxpr/ppermute | solution.py:15
  660.8 37.9 %copy-start.4 = (bf16[4,512,384]{1,2,0:T(8,128)(2,1)}, bf16[4,512,384]{1,2,0:T(8,128)(2,1)S(1)}, u32[]{:S(2)}) copy-start(bf16[4,512,384]{1,2,0:T(8,128)(2,1)S(1)} %get-tuple-element.1251) | copy-start | bytes 4718596 | tf_op jit(solution)/shard_map/while/body/eval_jaxpr/cond
  663.7 35.0 %copy-start.31 = (f32[384]{0:T(512)}, f32[384]{0:T(512)S(1)}, u32[]{:S(2)}) copy-start(f32[384]{0:T(512)S(1)} %get-tuple-element.1707) | copy-start | bytes 4612 | tf_op jit(solution)/shard_map/while/body/eval_jaxpr/cond
  713.8 20.8 %collective-permute-start.3 = (bf16[512,384]{0,1:T(8,128)(2,1)}, bf16[512,384]{0,1:T(8,128)(2,1)}, u32[]{:S(2)}, u32[]{:S(2)}) collective-permute-start(bf16[512,384]{0,1:T(8,128)(2,1)} %get-tuple-element.2109), channel_id=1, source_target_pairs={{16,0},{24,8},{17,1},{25,9},{18,2},{26,10},{19,3},{27,11},{20,4},{... | collective-permute-start | bytes 1179656 | tf_op jit(solution)/shard_map/while/body/eval_jaxpr/ppermute | solution.py:15
  715.9 20.3 %collective-permute-start.2 = (bf16[512,384]{0,1:T(8,128)(2,1)}, bf16[512,384]{0,1:T(8,128)(2,1)}, u32[]{:S(2)}, u32[]{:S(2)}) collective-permute-start(bf16[512,384]{0,1:T(8,128)(2,1)} %get-tuple-element.2109), channel_id=1, source_target_pairs={{8,0},{16,8},{24,16},{9,1},{17,9},{25,17},{10,2},{18,10},{26,18},{... | collective-permute-start | bytes 1179656 | tf_op jit(solution)/shard_map/while/body/eval_jaxpr/ppermute | solution.py:15
  737.4 37.9 %copy-start.4 = (bf16[4,512,384]{1,2,0:T(8,128)(2,1)}, bf16[4,512,384]{1,2,0:T(8,128)(2,1)S(1)}, u32[]{:S(2)}) copy-start(bf16[4,512,384]{1,2,0:T(8,128)(2,1)S(1)} %get-tuple-element.1251) | copy-start | bytes 4718596 | tf_op jit(solution)/shard_map/while/body/eval_jaxpr/cond
  740.3 35.0 %copy-start.31 = (f32[384]{0:T(512)}, f32[384]{0:T(512)S(1)}, u32[]{:S(2)}) copy-start(f32[384]{0:T(512)S(1)} %get-tuple-element.1707) | copy-start | bytes 4612 | tf_op jit(solution)/shard_map/while/body/eval_jaxpr/cond
  790.4 17.8 %collective-permute-start.3 = (bf16[512,384]{0,1:T(8,128)(2,1)}, bf16[512,384]{0,1:T(8,128)(2,1)}, u32[]{:S(2)}, u32[]{:S(2)}) collective-permute-start(bf16[512,384]{0,1:T(8,128)(2,1)} %get-tuple-element.2109), channel_id=1, source_target_pairs={{16,0},{24,8},{17,1},{25,9},{18,2},{26,10},{19,3},{27,11},{20,4},{... | collective-permute-start | bytes 1179656 | tf_op jit(solution)/shard_map/while/body/eval_jaxpr/ppermute | solution.py:15
  792.5 17.3 %collective-permute-start.2 = (bf16[512,384]{0,1:T(8,128)(2,1)}, bf16[512,384]{0,1:T(8,128)(2,1)}, u32[]{:S(2)}, u32[]{:S(2)}) collective-permute-start(bf16[512,384]{0,1:T(8,128)(2,1)} %get-tuple-element.2109), channel_id=1, source_target_pairs={{8,0},{16,8},{24,16},{9,1},{17,9},{25,17},{10,2},{18,10},{26,18},{... | collective-permute-start | bytes 1179656 | tf_op jit(solution)/shard_map/while/body/eval_jaxpr/ppermute | solution.py:15
  811.0 37.9 %copy-start.4 = (bf16[4,512,384]{1,2,0:T(8,128)(2,1)}, bf16[4,512,384]{1,2,0:T(8,128)(2,1)S(1)}, u32[]{:S(2)}) copy-start(bf16[4,512,384]{1,2,0:T(8,128)(2,1)S(1)} %get-tuple-element.1251) | copy-start | bytes 4718596 | tf_op jit(solution)/shard_map/while/body/eval_jaxpr/cond
  813.9 35.0 %copy-start.31 = (f32[384]{0:T(512)}, f32[384]{0:T(512)S(1)}, u32[]{:S(2)}) copy-start(f32[384]{0:T(512)S(1)} %get-tuple-element.1707) | copy-start | bytes 4612 | tf_op jit(solution)/shard_map/while/body/eval_jaxpr/cond
  864.0 17.8 %collective-permute-start.3 = (bf16[512,384]{0,1:T(8,128)(2,1)}, bf16[512,384]{0,1:T(8,128)(2,1)}, u32[]{:S(2)}, u32[]{:S(2)}) collective-permute-start(bf16[512,384]{0,1:T(8,128)(2,1)} %get-tuple-element.2109), channel_id=1, source_target_pairs={{16,0},{24,8},{17,1},{25,9},{18,2},{26,10},{19,3},{27,11},{20,4},{... | collective-permute-start | bytes 1179656 | tf_op jit(solution)/shard_map/while/body/eval_jaxpr/ppermute | solution.py:15
  866.1 17.3 %collective-permute-start.2 = (bf16[512,384]{0,1:T(8,128)(2,1)}, bf16[512,384]{0,1:T(8,128)(2,1)}, u32[]{:S(2)}, u32[]{:S(2)}) collective-permute-start(bf16[512,384]{0,1:T(8,128)(2,1)} %get-tuple-element.2109), channel_id=1, source_target_pairs={{8,0},{16,8},{24,16},{9,1},{17,9},{25,17},{10,2},{18,10},{26,18},{... | collective-permute-start | bytes 1179656 | tf_op jit(solution)/shard_map/while/body/eval_jaxpr/ppermute | solution.py:15
  889.4 65.1 %collective-permute-start.3 = (bf16[512,384]{0,1:T(8,128)(2,1)}, bf16[512,384]{0,1:T(8,128)(2,1)}, u32[]{:S(2)}, u32[]{:S(2)}) collective-permute-start(bf16[512,384]{0,1:T(8,128)(2,1)} %get-tuple-element.2109), channel_id=1, source_target_pairs={{16,0},{24,8},{17,1},{25,9},{18,2},{26,10},{19,3},{27,11},{20,4},{... | collective-permute-start | bytes 1179656 | tf_op jit(solution)/shard_map/while/body/eval_jaxpr/ppermute | solution.py:15
  936.0 20.0 %collective-permute-start.2 = (bf16[512,384]{0,1:T(8,128)(2,1)}, bf16[512,384]{0,1:T(8,128)(2,1)}, u32[]{:S(2)}, u32[]{:S(2)}) collective-permute-start(bf16[512,384]{0,1:T(8,128)(2,1)} %get-tuple-element.2109), channel_id=1, source_target_pairs={{8,0},{16,8},{24,16},{9,1},{17,9},{25,17},{10,2},{18,10},{26,18},{... | collective-permute-start | bytes 1179656 | tf_op jit(solution)/shard_map/while/body/eval_jaxpr/ppermute | solution.py:15
  962.0 61.5 %collective-permute-start.3 = (bf16[512,384]{0,1:T(8,128)(2,1)}, bf16[512,384]{0,1:T(8,128)(2,1)}, u32[]{:S(2)}, u32[]{:S(2)}) collective-permute-start(bf16[512,384]{0,1:T(8,128)(2,1)} %get-tuple-element.2109), channel_id=1, source_target_pairs={{16,0},{24,8},{17,1},{25,9},{18,2},{26,10},{19,3},{27,11},{20,4},{... | collective-permute-start | bytes 1179656 | tf_op jit(solution)/shard_map/while/body/eval_jaxpr/ppermute | solution.py:15
  1008.0 17.1 %collective-permute-start.2 = (bf16[512,384]{0,1:T(8,128)(2,1)}, bf16[512,384]{0,1:T(8,128)(2,1)}, u32[]{:S(2)}, u32[]{:S(2)}) collective-permute-start(bf16[512,384]{0,1:T(8,128)(2,1)} %get-tuple-element.2109), channel_id=1, source_target_pairs={{8,0},{16,8},{24,16},{9,1},{17,9},{25,17},{10,2},{18,10},{26,18},{... | collective-permute-start | bytes 1179656 | tf_op jit(solution)/shard_map/while/body/eval_jaxpr/ppermute | solution.py:15
  1357.4 10.1 copy-start.1
  (164 other events, 560.8 us)
Sparse Core Ops, SparseCore 0:
  10.8 67.5 all-gather.1
  1067.3 233.6 all-reduce.2
where the time goes:
time: 1390 us; the launch traced here: 1380 us
  waiting for transfers between devices  355 us (26%)
  matrix products  272 us (20%)
  other arithmetic  232 us (17%)
  local copies, waits for them, and re-layouts  214 us (15%)
  starting transfers between devices  184 us (13%)
  blocking collectives  91.6 us (7%)
  between operations  19.3 us (1%)
    psum x1, waiting for transfers between devices, body(): summed_w, summed_g = lax.psum((grad_all, grad_gains), 'dp')  203 us
    ppermute x28, starting transfers between devices, from_behind(): return lax.ppermute(value, axis, pairs)  184 us
    ppermute x28, waiting for transfers between devices, from_behind(): return lax.ppermute(value, axis, pairs)  120 us
    add x28, other arithmetic, backward_step(): total + piece  74.3 us
    sub x8, matrix products, layer_forward(): attn_probs = jax.nn.softmax(scores + masking[None, None, :], axis=-1)  57.5 us
    dot_general x4, matrix products, layer_forward(): branch_ffn = jnp.dot(hidden, w_down, preferred_element_type=jnp.float32)  48.7 us
    psum x1, blocking collectives, body(): lax.psum((own_square, loss_sum / frame_count, rows_local), ('section', 'd...  40.4 us
    dot_general x8, matrix products, layer_forward(): jnp.einsum('hqk,khe->qhe', probs_low, value_rows, preferred_element_type=...  34.5 us
  transfers between devices with their start and end apart: 30, of which 12 were waited for; matrix products, arithmetic and copies ran while one was open for 13% of the time, Pallas kernels for 0%

commit v1 on v0

--- a/solution.py
+++ b/solution.py
@@ -1,12 +1,293 @@
+import functools
 import math
 
 import jax
 import jax.numpy as jnp
 from jax import lax
+from jax.experimental import pallas as pl
+from jax.experimental.pallas import tpu as pltpu
 from jax.sharding import PartitionSpec as P
 
+HEADS = 8
+F32 = jnp.float32
+BF16 = jnp.bfloat16
+VMEM_LIMIT = 60 * 1024 * 1024
+
+
+def dot_nn(a, b):
+    return lax.dot_general(a, b, (((1,), (0,)), ((), ())), preferred_element_type=F32)
+
+
+def dot_nt(a, b):
+    return lax.dot_general(a, b, (((1,), (1,)), ((), ())), preferred_element_type=F32)
+
+
+def dot_tn(a, b):
+    return lax.dot_general(a, b, (((0,), (0,)), ((), ())), preferred_element_type=F32)
+
+
+def gelu_parts(x):
+    ax = jnp.abs(x)
+    bell = jnp.exp(-0.5 * x * x)
+    t = 1.0 / (1.0 + (0.3275911 * 0.7071067811865476) * ax)
+    poly = t * (
+        0.5 * 0.254829592
+        + t
+        * (
+            0.5 * -0.284496736
+            + t * (0.5 * 1.421413741 + t * (0.5 * -1.453152027 + t * (0.5 * 1.061405429)))
+        )
+    )
+    tail = poly * bell
+    cdf = jnp.where(x >= 0.0, 1.0 - tail, tail)
+    return x * cdf, cdf + x * bell * 0.3989422804014327
+
+
+def stack_quads(w_ref, first, step, number):
+    return jnp.concatenate([w_ref[0, first + step * i] for i in range(number)], axis=0)
+
+
+def forward_kernel(
+    layers, half, info_ref, scale_ref, x_ref, target_ref, w_ref, gain_ref,
+    probs_ref, heads_ref, att_ref, middle_ref, hidden_ref, slope_ref, sent_ref, loss_grad_ref, stats_ref,
+    hold_ref, out_ref,
+):
+    seg, width = x_ref.shape
+    dim = width // HEADS
+    part = width // 4
+    layer = pl.program_id(0)
+    rows = 256
+    chunks = seg // rows
+    length = info_ref[0]
+
+    @pl.when(layer == 0)
+    def _():
+        sent_ref[0] = x_ref[...]
+        stats_ref[...] = jnp.zeros_like(stats_ref)
+
+    def stream_of(at):
+        prev = sent_ref[layer, at].astype(F32)
+        skip = sent_ref[jnp.maximum(layer + 1 - half, 0), at].astype(F32)
+        return prev + jnp.where(layer >= half, skip, 0.0)
+
+    gain_one = gain_ref[0, 0:1]
+    gain_two = gain_ref[0, 1:2]
+
+    def qkv_step(i, _):
+        at = pl.ds(pl.multiple_of(i * rows, rows), rows)
+        stream = stream_of(at)
+        factor = lax.rsqrt(jnp.mean(stream * stream, axis=-1, keepdims=True) + 1e-06)
+        normed = (stream * factor * gain_one).astype(BF16)
+        for t in range(3):
+            qkv = dot_nn(normed, stack_quads(w_ref, t, 3, 4)).astype(BF16)
+            for h in range(HEADS):
+                heads_ref[0, t * HEADS + h, at] = qkv[:, h * dim : (h + 1) * dim]
+        return 0
+
+    lax.fori_loop(0, chunks, qkv_step, 0)
+    frames = lax.broadcasted_iota(jnp.int32, (1, seg), 1)
+    masking = jnp.where(frames < length, 0.0, -1e30).astype(F32)
+
+    def head_step(h, _):
+        keys = heads_ref[0, HEADS + h]
+        values = heads_ref[0, 2 * HEADS + h]
+        for i in range(chunks):
+            at = pl.ds(i * rows, rows)
+            scores = dot_nt(heads_ref[0, h, at], keys) * dim ** (-0.5) + masking
+            top = jnp.max(scores, axis=-1, keepdims=True)
+            expd = jnp.exp(scores - top)
+            probs = (expd * (1.0 / jnp.sum(expd, axis=-1, keepdims=True))).astype(BF16)
+            probs_ref[0, h, at] = probs
+            hold_ref[h, at] = dot_nn(probs, values).astype(BF16)
+        return 0
+
+    lax.fori_loop(0, HEADS, head_step, 0)
+
+    def ffn_step(i, _):
+        at = pl.ds(pl.multiple_of(i * rows, rows), rows)
+        attended = jnp.concatenate([hold_ref[h, at] for h in range(HEADS)], axis=1)
+        att_ref[0, at] = attended
+        branch_attn = dot_nn(attended, stack_quads(w_ref, 12, 1, 4))
+        stream = stream_of(at)
+        middle = stream + branch_attn
+        middle_ref[0, at] = middle
+        factor = lax.rsqrt(jnp.mean(middle * middle, axis=-1, keepdims=True) + 1e-06)
+        normed = (middle * factor * gain_two).astype(BF16)
+        branch_ffn = jnp.zeros((rows, width), F32)
+        for c in range(4):
+            pre_act = dot_nn(normed, stack_quads(w_ref, 16 + c, 4, 4))
+            hidden, slope = gelu_parts(pre_act)
+            hidden = hidden.astype(BF16)
+            hidden_ref[0, c, at] = hidden
+            slope_ref[0, c, at] = slope.astype(BF16)
+            branch_ffn = branch_ffn + dot_nn(hidden, stack_quads(w_ref, 32 + 4 * c, 1, 4))
+        output = middle + branch_ffn
+        out_ref[at] = output
+        sent_ref[jnp.minimum(layer + 1, layers - 1), at] = jnp.where(
+            layer + 1 < layers, output.astype(BF16), sent_ref[layers - 1, at]
+        )
+        valid = (lax.broadcasted_iota(jnp.int32, (rows, 1), 0) + i * rows < length).astype(F32)
+        for k, value in enumerate((stream, branch_attn, branch_ffn)):
+            stats_ref[layer, k : k + 1] += jnp.sum(valid * value * value, axis=0, keepdims=True)
+        return 0
+
+    lax.fori_loop(0, chunks, ffn_step, 0)
+
+    @pl.when(layer == layers - 1)
+    def _():
+        bins = width // 8
+        lane = lax.broadcasted_iota(jnp.int32, (1, width), 1)
+        is_real = lax.rem(lane, 2 * bins) < bins
+        stem = lane // (2 * bins)
+        present = jnp.zeros((1, width), F32)
+        for k in range(4):
+            present = jnp.where(stem == k, info_ref[1 + k].astype(F32), present)
+        inverse = scale_ref[0]
+
+        def loss_step(i, _):
+            at = pl.ds(pl.multiple_of(i * rows, rows), rows)
+            output = out_ref[at]
+            square = output * output
+            other = jnp.where(
+                is_real, pltpu.roll(square, width - bins, 1), pltpu.roll(square, bins, 1)
+            )
+            magnitude = jnp.sqrt(square + other + 0.01)
+            goal = target_ref[at]
+            goal = jnp.concatenate(
+                [goal[:, (k // 2) * bins : (k // 2 + 1) * bins] for k in range(8)], axis=1
+            )
+            differ = magnitude - goal
+            smooth = jnp.sqrt(differ * differ + 0.01)
+            valid = (lax.broadcasted_iota(jnp.int32, (rows, 1), 0) + i * rows < length).astype(F32)
+            weight = valid * present
+            loss_grad_ref[at] = weight * differ * output * inverse / (smooth * magnitude)
+            stats_ref[0, 3:4] += jnp.sum(
+                jnp.where(is_real, weight * smooth, 0.0), axis=0, keepdims=True
+            )
+            return 0
+
+        lax.fori_loop(0, chunks, loss_step, 0)
+
+
+def norm_reverse(value, gain, grad):
+    factor = lax.rsqrt(jnp.mean(value * value, axis=-1, keepdims=True) + 1e-06)
+    scaled = grad * gain
+    mean = jnp.mean(value * scaled, axis=-1, keepdims=True)
+    unit = value * factor
+    back = factor * scaled - unit * (factor * factor * mean)
+    return back, jnp.sum(grad * unit, axis=0, keepdims=True), (unit * gain).astype(BF16)
+
+
+def backward_kernel(
+    layers, half, loss_grad_ref, w_ref, gain_ref, sent_ref,
+    probs_ref, heads_ref, att_ref, middle_ref, hidden_ref, slope_ref,
+    grads_ref, gain_grad_ref,
+    sends_ref, dffn_ref, dpre_ref, normed_ref, dmid_ref, datt_ref, dhold_ref, dheads_ref, dqkv_ref,
+):
+    seg, width = loss_grad_ref.shape
+    dim = width // HEADS
+    part = width // 4
+    layer = layers - 1 - pl.program_id(0)
+    rows = 256
+    chunks = seg // rows
+    gain_one = gain_ref[0, 0:1]
+    gain_two = gain_ref[0, 1:2]
+    gain_grad_ref[...] = jnp.zeros_like(gain_grad_ref)
+
+    @pl.when(layer == layers - 1)
+    def _():
+        sends_ref[...] = jnp.zeros_like(sends_ref)
+
+    def put_grad(first, step, value):
+        for r in range(4):
+            grads_ref[0, first + step * r] = value[r * part : (r + 1) * part].astype(grads_ref.dtype)
+
+    def ffn_step(i, _):
+        at = pl.ds(pl.multiple_of(i * rows, rows), rows)
+        later = sends_ref[jnp.minimum(layer + 1, layers - 1), at].astype(F32)
+        skip = sends_ref[jnp.minimum(layer + half, layers - 1), at].astype(F32)
+        upstream = jnp.where(
+            layer == layers - 1, loss_grad_ref[at], later + jnp.where(layer + half < layers, skip, 0.0)
+        )
+        dffn = upstream.astype(BF16)
+        dffn_ref[at] = dffn
+        dnormed = jnp.zeros((rows, width), F32)
+        for c in range(4):
+            dhidden = dot_nt(dffn, stack_quads(w_ref, 32 + 4 * c, 1, 4))
+            dpre = (dhidden * slope_ref[0, c, at].astype(F32)).astype(BF16)
+            dpre_ref[c, at] = dpre
+            dnormed = dnormed + dot_nt(dpre, stack_quads(w_ref, 16 + c, 4, 4))
+        back, gain_grad, normed = norm_reverse(middle_ref[0, at], gain_two, dnormed)
+        gain_grad_ref[0, 1:2] += gain_grad
+        normed_ref[at] = normed
+        dmid = upstream + back
+        dmid_ref[at] = dmid
+        datt = dmid.astype(BF16)
+        datt_ref[at] = datt
+        dattended = dot_nt(datt, stack_quads(w_ref, 12, 1, 4)).astype(BF16)
+        for h in range(HEADS):
+            dhold_ref[h, at] = dattended[:, h * dim : (h + 1) * dim]
+        return 0
+
+    lax.fori_loop(0, chunks, ffn_step, 0)
+
+    def ffn_grad_step(c, _):
+        put_grad(32 + 4 * c, 1, dot_tn(hidden_ref[0, c], dffn_ref[...]))
+        put_grad(16 + c, 4, dot_tn(normed_ref[...], dpre_ref[c]))
+        return 0
+
+    lax.fori_loop(0, 4, ffn_grad_step, 0)
+    put_grad(12, 1, dot_tn(att_ref[0], datt_ref[...]))
+
+    def head_step(h, _):
+        queries = heads_ref[0, h]
+        keys = heads_ref[0, HEADS + h]
+        values = heads_ref[0, 2 * HEADS + h]
+        dkeys = jnp.zeros((seg, dim), F32)
+        dvalues = jnp.zeros((seg, dim), F32)
+        for i in range(chunks):
+            at = pl.ds(i * rows, rows)
+            probs = probs_ref[0, h, at]
+            dhold = dhold_ref[h, at]
+            dprobs = dot_nt(dhold, values)
+            wide = probs.astype(F32)
+            dot_sum = jnp.sum(wide * dprobs, axis=-1, keepdims=True)
+            dscores = (wide * (dprobs - dot_sum)).astype(BF16)
+            dheads_ref[h, at] = (dot_nn(dscores, keys) * dim ** (-0.5)).astype(BF16)
+            dvalues = dvalues + dot_tn(probs, dhold)
+            dkeys = dkeys + dot_tn(dscores, heads_ref[0, h, at])
+        dheads_ref[HEADS + h] = (dkeys * dim ** (-0.5)).astype(BF16)
+        dheads_ref[2 * HEADS + h] = dvalues.astype(BF16)
+        return 0
+
+    lax.fori_loop(0, HEADS, head_step, 0)
+
+    def qkv_step(i, _):
+        at = pl.ds(pl.multiple_of(i * rows, rows), rows)
+        dnormed = jnp.zeros((rows, width), F32)
+        for t in range(3):
+            dqkv = jnp.concatenate([dheads_ref[t * HEADS + h, at] for h in range(HEADS)], axis=1)
+            dqkv_ref[t, at] = dqkv
+            dnormed = dnormed + dot_nt(dqkv, stack_quads(w_ref, t, 3, 4))
+        prev = sent_ref[layer, at].astype(F32)
+        skip = sent_ref[jnp.maximum(layer + 1 - half, 0), at].astype(F32)
+        stream = prev + jnp.where(layer >= half, skip, 0.0)
+        back, gain_grad, normed = norm_reverse(stream, gain_one, dnormed)
+        gain_grad_ref[0, 0:1] += gain_grad
+        normed_ref[at] = normed
+        sends_ref[layer, at] = (dmid_ref[at] + back).astype(BF16)
+        return 0
+
+    lax.fori_loop(0, chunks, qkv_step, 0)
+
+    def qkv_grad_step(t, _):
+        put_grad(t, 3, dot_tn(normed_ref[...], dqkv_ref[t]))
+        return 0
+
+    lax.fori_loop(0, 3, qkv_grad_step, 0)
+
+
 FF = 1536
-HEADS = 8
 
 
 def from_behind(value, axis, by):
@@ -75,8 +356,8 @@
     head_dim = model_width // HEADS
     frames = jnp.arange(row_count)
     norm_one, scale_one = rms_norm(stream, gain_pair[0])
-    normed = norm_one.astype(jnp.bfloat16)
-    qkv_all = jnp.dot(normed, w_qkv, preferred_element_type=jnp.float32).astype(jnp.bfloat16)
+    normed = norm_one.astype(BF16)
+    qkv_all = jnp.dot(normed, w_qkv, preferred_element_type=jnp.float32).astype(BF16)
     queries = qkv_all[:, :model_width].reshape(row_count, HEADS, head_dim)
     key_rows = qkv_all[:, model_width : 2 * model_width].reshape(row_count, HEADS, head_dim)
     value_rows = qkv_all[:, 2 * model_width :].reshape(row_count, HEADS, head_dim)
@@ -85,18 +366,18 @@
         "qhe,khe->hqk", queries, key_rows, preferred_element_type=jnp.float32
     ) * head_dim ** (-0.5)
     attn_probs = jax.nn.softmax(scores + masking[None, None, :], axis=-1)
-    probs_low = attn_probs.astype(jnp.bfloat16)
+    probs_low = attn_probs.astype(BF16)
     attended = (
         jnp.einsum("hqk,khe->qhe", probs_low, value_rows, preferred_element_type=jnp.float32)
         .reshape(row_count, model_width)
-        .astype(jnp.bfloat16)
+        .astype(BF16)
     )
     branch_attn = jnp.dot(attended, w_out, preferred_element_type=jnp.float32)
     middle = stream + branch_attn
     norm_two, scale_two = rms_norm(middle, gain_pair[1])
-    normed_two = norm_two.astype(jnp.bfloat16)
+    normed_two = norm_two.astype(BF16)
     pre_act = jnp.dot(normed_two, w_up, preferred_element_type=jnp.float32)
-    hidden = jax.nn.gelu(pre_act, approximate=False).astype(jnp.bfloat16)
+    hidden = jax.nn.gelu(pre_act, approximate=False).astype(BF16)
     branch_ffn = jnp.dot(hidden, w_down, preferred_element_type=jnp.float32)
     kept_vals = (
         scale_one,
@@ -136,10 +417,10 @@
         pre_act,
         hidden,
     ) = kept_vals
-    grad_ffn = upstream.astype(jnp.bfloat16)
+    grad_ffn = upstream.astype(BF16)
     grad_down = jnp.dot(hidden.T, grad_ffn, preferred_element_type=jnp.float32)
     grad_hidden = jnp.dot(grad_ffn, w_down.T, preferred_element_type=jnp.float32)
-    grad_pre = (grad_hidden * gelu_slope(pre_act)).astype(jnp.bfloat16)
+    grad_pre = (grad_hidden * gelu_slope(pre_act)).astype(BF16)
     grad_up = jnp.dot(normed_two.T, grad_pre, preferred_element_type=jnp.float32)
     back_mid, gain_two = norm_back(
         middle,
@@ -148,11 +429,11 @@
         jnp.dot(grad_pre, w_up.T, preferred_element_type=jnp.float32),
     )
     grad_mid = upstream + back_mid
-    grad_branch = grad_mid.astype(jnp.bfloat16)
+    grad_branch = grad_mid.astype(BF16)
     grad_out = jnp.dot(attended.T, grad_branch, preferred_element_type=jnp.float32)
     grad_att = (
         jnp.dot(grad_branch, w_out.T, preferred_element_type=jnp.float32)
-        .astype(jnp.bfloat16)
+        .astype(BF16)
         .reshape(row_count, HEADS, head_dim)
     )
     grad_value = jnp.einsum("hqk,qhe->khe", probs_low, grad_att, preferred_element_type=jnp.float32)
@@ -161,7 +442,7 @@
     )
     grad_scores = (
         attn_probs * (grad_probs - jnp.sum(attn_probs * grad_probs, axis=-1, keepdims=True))
-    ).astype(jnp.bfloat16)
+    ).astype(BF16)
     grad_query = jnp.einsum(
         "hqk,khe->qhe", grad_scores, key_rows, preferred_element_type=jnp.float32
     ) * head_dim ** (-0.5)
@@ -175,7 +456,7 @@
             grad_value.reshape(row_count, model_width),
         ],
         axis=1,
-    ).astype(jnp.bfloat16)
+    ).astype(BF16)
     grad_wqkv = jnp.dot(normed.T, grad_qkv, preferred_element_type=jnp.float32)
     back_in, gain_one = norm_back(
         stream,
@@ -209,7 +490,7 @@
     return (jnp.sum(smooth_err * weight), grad_spec)
 
 
-def body(
+def pipelined_body(
     x_in,
     targets,
     valid_len,
@@ -236,8 +517,8 @@
     own_blocks = w_master.shape[1]
     own_gain = norm_gains.shape[2]
     full_w, full_g = (
-        lax.all_gather(w_master.astype(jnp.bfloat16), "dp", axis=1, tiled=True),
-        lax.all_gather(norm_gains.astype(jnp.bfloat16), "dp", axis=2, tiled=True),
+        lax.all_gather(w_master.astype(BF16), "dp", axis=1, tiled=True),
+        lax.all_gather(norm_gains.astype(BF16), "dp", axis=2, tiled=True),
     )
     matrices = split_matrices(full_w[0], model_width)
     gain_pair = full_g[0].astype(jnp.float32)
@@ -294,7 +575,7 @@
         )
         loss_sum = loss_sum + jnp.where(is_last, seg_loss, 0.0)
         sq_sums = sq_sums + squares
-        sent_rows = output.astype(jnp.bfloat16)
+        sent_rows = output.astype(BF16)
         in_rows = from_behind(sent_rows, "section", 1)
         from_encoder = from_behind(sent_rows, "section", half_way)
         recv_idx = step_idx - section_idx + half_way
@@ -306,9 +587,9 @@
         return (in_rows, kept_prev, skip_store, loss_grads, loss_sum, sq_sums)
 
     start_state = (
-        jnp.zeros((seg_len, model_width), jnp.bfloat16),
-        jnp.zeros(act_shape, jnp.bfloat16),
-        jnp.zeros(act_shape, jnp.bfloat16),
+        jnp.zeros((seg_len, model_width), BF16),
+        jnp.zeros(act_shape, BF16),
+        jnp.zeros(act_shape, BF16),
         jnp.zeros(act_shape, jnp.float32),
         jnp.zeros((), jnp.float32),
         jnp.zeros((3,), jnp.float32),
@@ -348,7 +629,7 @@
         )
         grad_mats = tuple((total + piece for total, piece in zip(grad_mats, layer_mats)))
         grad_gains = grad_gains + layer_gains
-        grad_rows = grad_stream.astype(jnp.bfloat16)
+        grad_rows = grad_stream.astype(BF16)
         in_grads = from_behind(grad_rows, "section", -1)
         from_decoder = from_behind(grad_rows, "section", -half_way)
         recv_idx = micro_idx + half_way
@@ -360,8 +641,8 @@
         return (in_grads, skip_grad_store, grad_mats, grad_gains)
 
     back_state = (
-        jnp.zeros((seg_len, model_width), jnp.bfloat16),
-        jnp.zeros(act_shape, jnp.bfloat16),
+        jnp.zeros((seg_len, model_width), BF16),
+        jnp.zeros(act_shape, BF16),
         tuple((jnp.zeros(mat.shape, jnp.float32) for mat in matrices)),
         jnp.zeros((2, model_width), jnp.float32),
     )
@@ -418,36 +699,194 @@
     )
 
 
+def layer_block(shape):
+    return pl.BlockSpec((1,) + shape, lambda i: (i,) + (0,) * len(shape))
+
+
+def whole_block(shape):
+    return pl.BlockSpec(shape, lambda i: (0,) * len(shape))
+
+
+def forward(layers, info, inverse, x_seg, target_seg, full_w, full_g):
+    seg, width = x_seg.shape
+    dim = width // HEADS
+    part = width // 4
+    half = layers // 2
+    shapes = (
+        (HEADS, seg, seg), (3 * HEADS, seg, dim), (seg, width), (seg, width), (4, seg, width), (4, seg, width)
+    )
+    kinds = (BF16, BF16, BF16, F32, BF16, BF16)
+    return pl.pallas_call(
+        functools.partial(forward_kernel, layers, half),
+        grid=(layers,),
+        in_specs=[
+            pl.BlockSpec(memory_space=pltpu.SMEM),
+            pl.BlockSpec(memory_space=pltpu.SMEM),
+            whole_block((seg, width)),
+            whole_block((seg, width // 2)),
+            layer_block((48, part, width)),
+            layer_block((2, width)),
+        ],
+        out_specs=[layer_block(s) for s in shapes]
+        + [whole_block((layers, seg, width)), whole_block((seg, width)), whole_block((layers, 8, width))],
+        out_shape=[jax.ShapeDtypeStruct((layers,) + s, k) for s, k in zip(shapes, kinds)]
+        + [
+            jax.ShapeDtypeStruct((layers, seg, width), BF16),
+            jax.ShapeDtypeStruct((seg, width), F32),
+            jax.ShapeDtypeStruct((layers, 8, width), F32),
+        ],
+        scratch_shapes=[pltpu.VMEM((HEADS, seg, dim), BF16), pltpu.VMEM((seg, width), F32)],
+        compiler_params=pltpu.CompilerParams(vmem_limit_bytes=VMEM_LIMIT),
+    )(info, inverse, x_seg, target_seg, full_w, full_g)
+
+
+def backward(layers, loss_grad, full_w, full_g, sent, saved):
+    seg, width = loss_grad.shape
+    dim = width // HEADS
+    part = width // 4
+    half = layers // 2
+
+    def from_end(array):
+        shape = array.shape[1:]
+        return pl.BlockSpec((1,) + shape, lambda i: (layers - 1 - i,) + (0,) * len(shape))
+
+    return pl.pallas_call(
+        functools.partial(backward_kernel, layers, half),
+        grid=(layers,),
+        in_specs=[
+            whole_block((seg, width)),
+            from_end(full_w),
+            from_end(full_g),
+            whole_block((layers, seg, width)),
+        ]
+        + [from_end(a) for a in saved],
+        out_specs=[
+            pl.BlockSpec((1, 48, part, width), lambda i: (layers - 1 - i, 0, 0, 0)),
+            pl.BlockSpec((1, 8, width), lambda i: (layers - 1 - i, 0, 0)),
+        ],
+        out_shape=[
+            jax.ShapeDtypeStruct((layers, 48, part, width), BF16),
+            jax.ShapeDtypeStruct((layers, 8, width), F32),
+        ],
+        scratch_shapes=[
+            pltpu.VMEM((layers, seg, width), BF16),
+            pltpu.VMEM((seg, width), BF16),
+            pltpu.VMEM((4, seg, width), BF16),
+            pltpu.VMEM((seg, width), BF16),
+            pltpu.VMEM((seg, width), F32),
+            pltpu.VMEM((seg, width), BF16),
+            pltpu.VMEM((HEADS, seg, dim), BF16),
+            pltpu.VMEM((3 * HEADS, seg, dim), BF16),
+            pltpu.VMEM((3, seg, width), BF16),
+        ],
+        compiler_params=pltpu.CompilerParams(vmem_limit_bytes=VMEM_LIMIT),
+    )(loss_grad, full_w, full_g, sent, *saved)
+
+
+def body(
+    x_in, targets, valid_len, present_stems, w_master, norm_gains, gain_m, gain_v,
+    l_stats, r_stats, l_roots, r_roots, step_count,
+):
+    width = x_in.shape[1]
+    part = width // 4
+    layers = lax.axis_size("section")
+    section_idx = lax.axis_index("section")
+    groups = lax.axis_size("dp")
+    group_idx = lax.axis_index("dp")
+    micro = valid_len.shape[0] // groups
+    seg = x_in.shape[0] // micro
+    own_blocks = w_master.shape[1]
+    own_gain = norm_gains.shape[2]
+    own_w = (
+        w_master[0].astype(BF16).reshape(own_blocks // 4, 4, part, part).transpose(0, 2, 1, 3)
+        .reshape(own_blocks // 4, part, width)
+    )
+    full_w = lax.all_gather(own_w, ("section", "dp"), axis=0, tiled=True).reshape(
+        layers, -1, part, width
+    )
+    full_g = lax.all_gather(
+        lax.all_gather(norm_gains[0], "dp", axis=1, tiled=True), "section", axis=0
+    ).astype(BF16).astype(F32)
+    slot = jnp.minimum(section_idx, micro - 1)
+    used = (section_idx < micro).astype(jnp.int32)
+    at = group_idx * micro + slot
+    info = jnp.concatenate([valid_len[at][None] * used, present_stems[at] * used])
+    frame_count = jnp.sum(valid_len).astype(F32)
+    x_seg = lax.dynamic_slice_in_dim(x_in, slot * seg, seg, 0)
+    target_seg = lax.dynamic_slice_in_dim(targets, slot * seg, seg, 0)
+    *saved, sent, loss_grad, stats = forward(
+        layers, info, (1.0 / frame_count)[None], x_seg, target_seg, full_w, full_g
+    )
+    grads, gain_grads = backward(layers, loss_grad, full_w, full_g, sent, saved)
+    own_quads = lax.psum_scatter(
+        grads.reshape(-1, part, width), ("section", "dp"), scatter_dimension=0, tiled=True
+    ).astype(F32)
+    own_grad = (
+        own_quads.reshape(own_blocks // 4, part, 4, part).transpose(0, 2, 1, 3)
+        .reshape(own_blocks, part * part)
+    )
+    summed_g, sums = lax.psum((gain_grads[:, :2], jnp.sum(stats, axis=2)), ("section", "dp"))
+    own_gain_grad = lax.dynamic_slice(
+        summed_g, (section_idx, 0, group_idx * own_gain), (1, 2, own_gain)
+    )[0]
+    own_square = jnp.sum(own_grad * own_grad) + jnp.sum(own_gain_grad * own_gain_grad)
+    total_square = lax.psum(own_square, ("section", "dp"))
+    loss_value = sums[0, 3] / frame_count
+    grad_norm = jnp.sqrt(total_square)
+    clip_limit = 0.00015 * math.sqrt(layers * (own_blocks * groups * part * part + 2 * width))
+    factor = clip_limit / jnp.maximum(grad_norm, clip_limit)
+    grad_blocks = own_grad * factor
+    square = (own_blocks, part, part)
+    shaped = grad_blocks.reshape(square)
+    highest = lax.Precision.HIGHEST
+    l_new = 0.95 * l_stats[0].reshape(square) + 0.05 * jnp.einsum(
+        "bij,bkj->bik", shaped, shaped, precision=highest
+    )
+    r_new = 0.95 * r_stats[0].reshape(square) + 0.05 * jnp.einsum(
+        "bji,bjk->bik", shaped, shaped, precision=highest
+    )
+    left_side = jnp.einsum("bij,bjk->bik", l_roots[0].reshape(square), shaped, precision=highest)
+    precond = jnp.einsum("bij,bjk->bik", left_side, r_roots[0].reshape(square), precision=highest)
+    master = w_master[0]
+    w_new = master - 0.5 * (precond.reshape(master.shape) + 0.01 * master)
+    gain_grad = own_gain_grad * factor
+    m_new = 0.9 * gain_m[0] + 0.1 * gain_grad
+    v_new = 0.999 * gain_v[0] + 0.001 * gain_grad * gain_grad
+    step_num = step_count[0].astype(F32)
+    m_hat = m_new / (1.0 - jnp.power(0.9, step_num))
+    v_hat = v_new / (1.0 - jnp.power(0.999, step_num))
+    gains_new = norm_gains[0] - 0.5 * m_hat / (jnp.sqrt(v_hat) + 1e-08)
+    rms = jnp.sqrt(sums[section_idx, :3] / (frame_count * width)).reshape(1, 3)
+    return (
+        w_new[None],
+        grad_blocks[None],
+        l_new.reshape(master.shape)[None],
+        r_new.reshape(master.shape)[None],
+        gains_new[None],
+        m_new[None],
+        v_new[None],
+        loss_value,
+        grad_norm,
+        rms,
+    )
+
+
 def solution(mesh):
+    def step(*args):
+        layers, groups = mesh.shape["section"], mesh.shape["dp"]
+        micro, own_blocks = args[2].shape[0] // groups, args[4].shape[1]
+        if micro <= layers and own_blocks % 4 == 0:
+            return body(*args)
+        return pipelined_body(*args)
+
+    block = P("section", "dp", None)
+    gain = P("section", None, "dp")
     return jax.shard_map(
-        body,
+        step,
         mesh=mesh,
         in_specs=(
-            P("dp", None),
-            P("dp", None),
-            P(),
-            P(),
-            P("section", "dp", None),
-            P("section", None, "dp"),
-            P("section", None, "dp"),
-            P("section", None, "dp"),
-            P("section", "dp", None),
-            P("section", "dp", None),
-            P("section", "dp", None),
-            P("section", "dp", None),
-            P(),
+            P("dp", None), P("dp", None), P(), P(), block, gain, gain, gain, block, block, block, block, P(),
         ),
-        out_specs=(
-            P("section", "dp", None),
-            P("section", "dp", None),
-            P("section", "dp", None),
-            P("section", "dp", None),
-            P("section", None, "dp"),
-            P("section", None, "dp"),
-            P("section", None, "dp"),
-            P(),
-            P(),
-            P("section", None),
-        ),
+        out_specs=(block, block, block, block, gain, gain, gain, P(), P(), P("section", None)),
         check_vma=False,
     )

time: 1390 us -> 516 us (0.37)
  matrix products: 272 us -> 8.17 us
  other arithmetic: 232 us -> 14.6 us
  local copies, waits for them, and re-layouts: 214 us -> 25.7 us
  starting transfers between devices: 184 us -> 0.08 us
  waiting for transfers between devices: 355 us -> 173 us
  Pallas kernels: 0 us -> 155 us
  blocking collectives: 91.6 us -> 116 us
    dot_general x80 -> x0, matrix products: 207 us -> none  [the longest x4 48.7 us: layer_forward(): branch_ffn = jnp.dot(hidden, w_down, preferred_element_type=jnp.float32)]
    psum x1 -> x0, waiting for transfers between devices: 203 us -> none  [body(): summed_w, summed_g = lax.psum((grad_all, grad_gains), 'dp')]
    ppermute x28 -> x0, starting transfers between devices: 184 us -> none  [from_behind(): return lax.ppermute(value, axis, pairs)]
    pallas_call x0 -> x2, Pallas kernels: none -> 155 us  [the longest x1 82.9 us: backward(): pl.pallas_call(functools.partial(backward_kernel, layers, half), grid=(la...]
    ppermute x28 -> x0, waiting for transfers between devices: 120 us -> none  [from_behind(): return lax.ppermute(value, axis, pairs)]
    reduce_scatter x0 -> x1, waiting for transfers between devices: none -> 111 us  [body(): lax.psum_scatter(grads.reshape(-1, part, width), ('section', 'dp'), scatt...]
    add x46 -> x0, other arithmetic: 79.8 us -> none  [the longest x28 74.3 us: backward_step(): total + piece]
    sub x8 -> x0, matrix products: 57.5 us -> none  [layer_forward(): attn_probs = jax.nn.softmax(scores + masking[None, None, :], axis=-1)]
  transfers between devices with their start and end apart: 30 -> 2, of which waited for: 12 -> 2; matrix products, arithmetic and copies ran while one was open for 13% -> 3% of each run, Pallas kernels for 0% -> 0%
where the time goes in v1:
time: 516 us; the launch traced here: 515 us
  waiting for transfers between devices  173 us (34%)
  Pallas kernels  155 us (30%)
  blocking collectives  116 us (22%)
  local copies, waits for them, and re-layouts  25.7 us (5%)
  between operations  21.4 us (4%)
  other arithmetic  14.6 us (3%)
  matrix products  8.17 us (2%)
    reduce_scatter x1, waiting for transfers between devices, body(): lax.psum_scatter(grads.reshape(-1, part, width), ('section', 'dp'), scatt...  111 us
    pallas_call x1, Pallas kernels, backward(): pl.pallas_call(functools.partial(backward_kernel, layers, half), grid=(la...  82.9 us
    pallas_call x1, Pallas kernels, forward(): pl.pallas_call(functools.partial(forward_kernel, layers, half), grid=(lay...  72.3 us
    all_gather x1, waiting for transfers between devices, body(): lax.all_gather(own_w, ('section', 'dp'), axis=0, tiled=True)  62.1 us
    psum x1, blocking collectives, body(): total_square = lax.psum(own_square, ('section', 'dp'))  40.2 us
    psum x1, blocking collectives, body(): lax.psum((gain_grads[:, :2], jnp.sum(stats, axis=2)), ('section', 'dp'))  39.3 us
    all_gather x1, blocking collectives, body(): lax.all_gather(norm_gains[0], 'dp', axis=1, tiled=True)  31.5 us
  transfers between devices with their start and end apart: 2, of which 2 were waited for; matrix products, arithmetic and copies ran while one was open for 3% of the time, Pallas kernels for 0%

profile of v1, /device:TPU:2, one launch (start us, length us, event | category | flops | bytes accessed | tf_op | source)
XLA Modules:
  0.0 514.7 jit_solution(9610395246223882283)
XLA Ops:
  7.2 1.3 convert_element_type.28
  8.6 0.6 convert_element_type.29
  9.2 0.3 copy.38
  9.5 1.2 reshape.76
  10.8 0.6 reduce_sum.36
  11.4 0.6 dynamic_slice.18
  12.0 1.0 constant_dynamic-slice_fusion.2
  13.0 1.0 copy.34.target_ref
  14.8 31.5 %all-gather = bf16[1,2,384]{1,0,2:T(2,128)(2,1)S(1)} all-gather(bf16[1,2,48]{1,0,2:T(2,128)(2,1)S(1)} %copy.29), channel_id=2, replica_groups=mesh['section'=4,'dp'=8] {'dp'}, dimensions={2}, use_global_device_ids=true | all-gather | bytes 1728 | tf_op jit(solution)/shard_map/all_gather | solution.py:808
  46.3 0.1 copy.30
  46.4 5.2 %all-gather.1 = bf16[4,2,384]{2,1,0:T(2,128)(2,1)S(1)} all-gather(bf16[1,2,384]{2,1,0:T(2,128)(2,1)S(1)} %copy.30), channel_id=3, replica_groups=mesh['section'=4,'dp'=8] {'section'}, dimensions={0}, use_global_device_ids=true | all-gather | bytes 7680 | tf_op jit(solution)/shard_map/all_gather | solution.py:807
  51.5 0.6 convert_element_type.40.gain_ref
  52.8 0.2 multiply_reduce_fusion
  53.0 0.6 pad_add_fusion.info_ref
  53.6 0.8 constant_dynamic-slice_fusion.3.x_ref
  54.4 62.1 %all-gather.4.cloned.1.call-done = bf16[192,96,384]{2,1,0:T(8,128)(2,1)} async-done(((bf16[6,96,384]{2,1,0:T(8,128)(2,1)}), bf16[192,96,384]{2,1,0:T(8,128)(2,1)}) %all-gather.4.cloned.1.call-update) | async-done | bytes 14155792 | tf_op jit(solution)/shard_map/all_gather | solution.py:804
  116.5 72.3 %shard_map.204 = (bf16[4,8,512,512]{3,2,1,0:T(8,128)(2,1)}, bf16[4,24,512,48]{3,2,1,0:T(8,128)(2,1)}, bf16[4,512,384]{2,1,0:T(8,128)(2,1)}, f32[4,512,384]{2,1,0...) custom-call(s32[5]{0:T(128)} %pad_add_fusion.info_ref, ...), custom_call_target="tpu_custom_call" | custom-call | tf_op jit(solution)/shard_map/pallas_call | solution.py:719
  188.8 82.9 %shard_map.205 = (bf16[4,48,96,384]{3,2,1,0:T(8,128)(2,1)}, f32[4,8,384]{2,1,0:T(8,128)}) custom-call(f32[512,384]{1,0:T(8,128)} %get-tuple-element.21.loss_grad_ref, bf16[4,48,96,384]{3,2,1,0:T(8,128)(2,1)} %bitcast.25, f32[4,2,384]{2,1,0:T(2,128)} %convert_element_type.40.gain_ref, bf16[4,512,384]{2,1,0:T(8,128)(2,1)} %get-tuple-element.22.sent_ref, ...), custom_call_target="tpu_custom_call" | custom-call | tf_op jit(solution)/shard_map/pallas_call | solution.py:753
  272.5 0.3 copy-done.6
  272.9 0.5 reshape_squeeze.8
  273.3 1.6 reshape_squeeze.9
  275.0 1.5 broadcast_multiply_fusion.1
  276.4 1.5 mul.172
  277.9 1.3 broadcast_multiply_fusion
  279.3 1.5 mul.175
  280.8 0.8 slice.18
  281.7 39.3 %psum.21 = f32[4,2,384]{2,1,0:T(2,128)S(1)} all-reduce(f32[4,2,384]{2,1,0:T(2,128)S(1)} %slice.18), channel_id=1, replica_groups=mesh['section'=4,'dp'=8] {'section','dp'}, use_global_device_ids=true, to_apply=%region_3.0 | all-reduce | flops 3072 | bytes 24576 | tf_op jit(solution)/shard_map/psum | solution.py:828
  321.0 0.7 multiply_reduce_fusion.1
  321.7 111.3 %reduce-scatter.2.cloned.1.call-done = bf16[6,96,384]{2,1,0:T(8,128)(2,1)} async-done(((bf16[192,96,384]{2,1,0:T(8,128)(2,1)}), bf16[6,96,384]{2,1,0:T(8,128)(2,1)}) %reduce-scatter.2.cloned.1.call-update) | async-done | bytes 442384 | tf_op jit(solution)/shard_map/reduce_scatter | solution.py:821
  432.9 1.8 fusion.2
  436.1 40.2 %all-reduce = (f32[]{:T(128)}, f32[4,8]{1,0:T(4,128)}) all-reduce(f32[]{:T(128)S(6)} %add.61, f32[4,8]{1,0:T(4,128)S(1)} %reduce_sum.39), channel_id=1, replica_groups=mesh['section'=4,'dp'=8] {'section','dp'}, use_global_device_ids=true, to_apply=%region_5.0 | all-reduce | flops 33 | bytes 264 | tf_op jit(solution)/shard_map/psum | solution.py:833
  477.0 1.1 convert_multiply_fusion
  478.1 1.2 fusion.7
  479.3 1.7 mul.168
  481.0 1.3 pad_maximum_fusion
  482.3 1.2 fusion.8
  483.6 1.3 fusion.9
  484.9 1.6 reshape.79
  486.5 2.3 multiply_subtract_fusion
  488.8 2.6 fusion.1
  491.4 1.6 broadcast_in_dim_reshape.6
  493.0 3.1 fusion
  496.1 3.0 broadcast_in_dim_reshape.7
  499.0 1.1 copy.37
  500.2 2.9 mul.170
  503.1 0.6 slice.23
  503.7 0.5 fusion.5
  504.9 0.7 divide_subtract_fusion
  (33 shorter events, 0.4 us)
Async XLA Ops:
  7.2 46.5 %copy-start = (bf16[2048,384]{1,0:T(8,128)(2,1)S(1)}, bf16[2048,384]{1,0:T(8,128)(2,1)}, u32[]{:S(2)}) copy-start(bf16[2048,384]{1,0:T(8,128)(2,1)} %param.13) | copy-start | bytes 4718596
  7.2 109.3 %all-gather.4.cloned.1.call-start = ((), (), s32[]{:S(2)}) async-start(), calls=%async_computation.1 | async-start | bytes 14598144 | tf_op jit(solution)/shard_map/all_gather | solution.py:804
  9.2 1.6 copy-start.13
  10.7 4.0 copy-start.8
  10.7 42.2 %copy-start.9 = (s32[32,4]{0,1:T(4,128)S(1)}, s32[32,4]{0,1:T(4,128)}, u32[]{:S(2)}) copy-start(s32[32,4]{0,1:T(4,128)} %param.16) | copy-start | bytes 1540
  10.7 422.2 %reduce-scatter.2.cloned.1.call-start = ((), (), s32[]{:S(2)}) async-start(), calls=%async_computation.2 | async-start | bytes 14598144 | tf_op jit(solution)/shard_map/reduce_scatter | solution.py:821
  271.7 1.2 copy-start.6
  279.3 2.4 copy-start.7
  484.9 1.6 copy-start.5
  486.5 2.3 copy-start.4
  491.4 1.6 copy-start.3
  496.1 3.0 copy-start.2
  499.0 6.5 %copy-start.1 = (bf16[2048,384]{1,0:T(8,128)(2,1)S(1)}, bf16[2048,384]{1,0:T(8,128)(2,1)}, u32[]{:S(2)}) copy-start(bf16[2048,384]{1,0:T(8,128)(2,1)} %param.13) | copy-start | bytes 4718596
  500.2 2.9 copy-start.12
  500.2 4.7 copy-start.10
  500.2 4.7 copy-start.11
Sparse Core Ops, SparseCore 0:
  11.5 104.9 all-gather.3
  271.8 161.0 reduce-scatter.1

commit v2 on v1

--- a/solution.py
+++ b/solution.py
@@ -47,10 +47,178 @@
     return jnp.concatenate([w_ref[0, first + step * i] for i in range(number)], axis=0)
 
 
+MESH = pl.DeviceIdType.MESH
+
+
+def mesh_place():
+    section = lax.axis_index("section")
+    group = lax.axis_index("dp")
+    core = lax.rem(section, 2)
+    y = lax.rem(group, 2)
+    z = group // 2
+    z_peers = (z, z + 1 - 2 * lax.rem(z, 2), lax.rem(z + 2, 4), 3 - z)
+    return section, group, core, y, z_peers
+
+
+def remote(source, target, send_sem, recv_sem, section, group):
+    return pltpu.make_async_remote_copy(
+        src_ref=source, dst_ref=target, send_sem=send_sem, recv_sem=recv_sem,
+        device_id=(section, group), device_id_type=MESH,
+    )
+
+
+def greet(places):
+    barrier = pltpu.get_barrier_semaphore()
+    for place in places:
+        pl.semaphore_signal(barrier, inc=1, device_id=place, device_id_type=MESH)
+    pl.semaphore_wait(barrier, len(places))
+
+
+class Gather:
+    def __init__(self, own_ref, gain_ref, w_ref, gains_ref, sems):
+        self.own, self.gain, self.w, self.gains = own_ref, gain_ref, w_ref, gains_ref
+        self.spread, self.z_sems, self.y_sems, self.core_sems, self.gain_sems, self.local = sems
+        self.section, self.group, self.core, self.y, self.z_peers = mesh_place()
+        self.quads = own_ref.shape[0] // 2
+        self.others = [lax.rem(self.section + k, 4) for k in range(1, 4)]
+        self.places = [(o, self.group) for o in self.others] + [
+            (self.section, lax.rem(self.group + k, 8)) for k in range(1, 8)
+        ]
+
+    def piece(self, layer, group):
+        return self.w.at[layer, pl.ds(group * 2 * self.quads + self.quads * self.core, self.quads)]
+
+    def spread_copy(self, k):
+        peer = self.others[k]
+        half = lax.rem(peer, 2) * self.quads
+        return remote(
+            self.own.at[pl.ds(half, self.quads)],
+            self.w.at[self.section, pl.ds(self.group * 2 * self.quads + half, self.quads)],
+            self.spread.at[0, k], self.spread.at[1, k], peer, self.group,
+        )
+
+    def spread_wait(self, layer):
+        for k in range(3):
+            @pl.when(lax.rem(layer + k + 1, 4) == self.section)
+            def _():
+                ref = self.piece(layer, self.group)
+                remote(ref, ref, self.spread.at[0, k], self.spread.at[1, k], self.others[0], self.group).wait_recv()
+
+    def z_copy(self, layer, k):
+        ref = self.piece(layer, self.group)
+        return remote(
+            ref, ref, self.z_sems.at[0, layer, k], self.z_sems.at[1, layer, k],
+            self.section, self.z_peers[k] * 2 + self.y,
+        )
+
+    def z_landed(self, layer, k):
+        ref = self.piece(layer, self.z_peers[k] * 2 + self.y)
+        return remote(
+            ref, ref, self.z_sems.at[0, layer, k], self.z_sems.at[1, layer, k],
+            self.section, self.z_peers[k] * 2 + self.y,
+        )
+
+    def y_copy(self, layer, k, mine=True):
+        y = self.y if mine else 1 - self.y
+        ref = self.piece(layer, self.z_peers[k] * 2 + y)
+        return remote(
+            ref, ref, self.y_sems.at[0, layer, k], self.y_sems.at[1, layer, k],
+            self.section, self.group + 1 - 2 * self.y,
+        )
+
+    def core_copy(self, layer, k, mine=True):
+        y = self.y if k < 4 else 1 - self.y
+        core = self.core if mine else 1 - self.core
+        at = (self.z_peers[k % 4] * 2 + y) * 2 * self.quads + self.quads * core
+        ref = self.w.at[layer, pl.ds(at, self.quads)]
+        return remote(
+            ref, ref, self.core_sems.at[0, layer, k], self.core_sems.at[1, layer, k],
+            self.section + 1 - 2 * self.core, self.group,
+        )
+
+    def gain_copy(self, k):
+        if k < 7:
+            peer = lax.rem(self.group + k + 1, 8)
+            return remote(
+                self.gain, self.gains.at[self.section, self.group],
+                self.gain_sems.at[0, k], self.gain_sems.at[1, k], self.section, peer,
+            )
+        ref = self.gains.at[self.section]
+        return remote(
+            ref, ref, self.gain_sems.at[0, k], self.gain_sems.at[1, k], self.others[k - 7], self.group
+        )
+
+    def gain_landed(self, k):
+        if k < 7:
+            ref = self.gains.at[self.section, lax.rem(self.group - k - 1 + 8, 8)]
+        else:
+            ref = self.gains.at[lax.rem(self.section - (k - 6) + 4, 4)]
+        return remote(ref, ref, self.gain_sems.at[0, k], self.gain_sems.at[1, k], self.section, self.group)
+
+    def begin(self):
+        greet(self.places)
+        for k in range(3):
+            self.spread_copy(k).start()
+        for k in range(7):
+            self.gain_copy(k).start()
+        half = self.core * self.quads
+        self.w[self.section, pl.ds(self.group * 2 * self.quads + half, self.quads)] = self.own[
+            pl.ds(half, self.quads)
+        ]
+        self.gains[self.section, self.group] = self.gain[...]
+
+    def share_gains(self):
+        for k in range(7):
+            self.gain_landed(k).wait_recv()
+        for k in range(7, 10):
+            self.gain_copy(k).start()
+
+    def wait_gains(self):
+        for k in range(7, 10):
+            self.gain_landed(k).wait_recv()
+
+    def kick(self, layer):
+        self.spread_wait(layer)
+        for k in range(1, 4):
+            self.z_copy(layer, k).start()
+        self.y_copy(layer, 0).start()
+        self.core_copy(layer, 0).start()
+
+    def serve(self, layer, step):
+        if step < 4:
+            self.z_landed(layer, step).wait_recv()
+            self.y_copy(layer, step).start()
+            self.core_copy(layer, step).start()
+        else:
+            self.y_copy(layer, step - 4, False).wait_recv()
+            self.core_copy(layer, step).start()
+
+    def finish(self, layer):
+        for k in range(8):
+            self.core_copy(layer, k, False).wait_recv()
+
+    def end(self, layers):
+        for k in range(3):
+            self.spread_copy(k).wait_send()
+        for k in range(10):
+            self.gain_copy(k).wait_send()
+
+        def per_layer(layer, _):
+            for k in range(1, 4):
+                self.z_copy(layer, k).wait_send()
+            for k in range(4):
+                self.y_copy(layer, k).wait_send()
+            for k in range(8):
+                self.core_copy(layer, k).wait_send()
+            return 0
+
+        lax.fori_loop(0, layers, per_layer, 0)
+
+
 def forward_kernel(
-    layers, half, info_ref, scale_ref, x_ref, target_ref, w_ref, gain_ref,
+    layers, half, info_ref, scale_ref, x_ref, target_ref, own_ref, own_gain_ref,
     probs_ref, heads_ref, att_ref, middle_ref, hidden_ref, slope_ref, sent_ref, loss_grad_ref, stats_ref,
-    hold_ref, out_ref,
+    full_ref, gains_out_ref, hold_ref, out_ref, w_all_ref, gains_ref, *sems,
 ):
     seg, width = x_ref.shape
     dim = width // HEADS
@@ -59,19 +227,51 @@
     rows = 256
     chunks = seg // rows
     length = info_ref[0]
+    gather = Gather(own_ref, own_gain_ref, w_all_ref, gains_ref, sems)
+    w_ref = w_all_ref.at[pl.ds(layer, 1)]
+
+    def keep_copy(index):
+        return pltpu.make_async_copy(w_all_ref.at[index], full_ref.at[index], gather.local.at[index])
 
     @pl.when(layer == 0)
     def _():
+        gather.begin()
         sent_ref[0] = x_ref[...]
         stats_ref[...] = jnp.zeros_like(stats_ref)
+        gather.kick(0)
+        gather.share_gains()
+        for step in range(1, 4):
+            gather.serve(0, step)
+        gather.kick(1)
+        for step in range(4, 8):
+            gather.serve(0, step)
+        gather.wait_gains()
+
+    gather.finish(layer)
+    keep_copy(layer).start()
+    more = layer + 1 < layers
+
+    def serve(step):
+        @pl.when(more)
+        def _():
+            gather.serve(layer + 1, step)
+        if step == 3:
+            @pl.when(layer + 2 < layers)
+            def _():
+                gather.kick(layer + 2)
 
     def stream_of(at):
         prev = sent_ref[layer, at].astype(F32)
         skip = sent_ref[jnp.maximum(layer + 1 - half, 0), at].astype(F32)
         return prev + jnp.where(layer >= half, skip, 0.0)
 
-    gain_one = gain_ref[0, 0:1]
-    gain_two = gain_ref[0, 1:2]
+    def gain_row(which):
+        return jnp.concatenate(
+            [gains_ref[layer, g, which : which + 1, : width // 8] for g in range(8)], axis=1
+        ).astype(BF16).astype(F32)
+
+    gain_one = gain_row(0)
+    gain_two = gain_row(1)
 
     def qkv_step(i, _):
         at = pl.ds(pl.multiple_of(i * rows, rows), rows)
@@ -99,6 +299,10 @@
             probs = (expd * (1.0 / jnp.sum(expd, axis=-1, keepdims=True))).astype(BF16)
             probs_ref[0, h, at] = probs
             hold_ref[h, at] = dot_nn(probs, values).astype(BF16)
+        for step in range(1, 8):
+            @pl.when(h == step)
+            def _():
+                serve(step)
         return 0
 
     lax.fori_loop(0, HEADS, head_step, 0)
@@ -167,6 +371,10 @@
             return 0
 
         lax.fori_loop(0, chunks, loss_step, 0)
+        gains_out_ref[...] = gains_ref[...]
+        gather.end(layers)
+        for k in range(layers):
+            keep_copy(k).wait()
 
 
 def norm_reverse(value, gain, grad):
@@ -707,7 +915,7 @@
     return pl.BlockSpec(shape, lambda i: (0,) * len(shape))
 
 
-def forward(layers, info, inverse, x_seg, target_seg, full_w, full_g):
+def forward(layers, info, inverse, x_seg, target_seg, own_w, own_gain):
     seg, width = x_seg.shape
     dim = width // HEADS
     part = width // 4
@@ -724,20 +932,36 @@
             pl.BlockSpec(memory_space=pltpu.SMEM),
             whole_block((seg, width)),
             whole_block((seg, width // 2)),
-            layer_block((48, part, width)),
-            layer_block((2, width)),
+            pl.BlockSpec(memory_space=pltpu.VMEM),
+            pl.BlockSpec(memory_space=pltpu.VMEM),
         ],
         out_specs=[layer_block(s) for s in shapes]
-        + [whole_block((layers, seg, width)), whole_block((seg, width)), whole_block((layers, 8, width))],
+        + [whole_block((layers, seg, width)), whole_block((seg, width)), whole_block((layers, 8, width))]
+        + [pl.BlockSpec(memory_space=pl.ANY), pl.BlockSpec(memory_space=pltpu.VMEM)],
         out_shape=[jax.ShapeDtypeStruct((layers,) + s, k) for s, k in zip(shapes, kinds)]
         + [
             jax.ShapeDtypeStruct((layers, seg, width), BF16),
             jax.ShapeDtypeStruct((seg, width), F32),
             jax.ShapeDtypeStruct((layers, 8, width), F32),
+            jax.ShapeDtypeStruct((layers, 48, part, width), BF16),
+            jax.ShapeDtypeStruct((layers, 8, 8, 128), F32),
         ],
-        scratch_shapes=[pltpu.VMEM((HEADS, seg, dim), BF16), pltpu.VMEM((seg, width), F32)],
-        compiler_params=pltpu.CompilerParams(vmem_limit_bytes=VMEM_LIMIT),
-    )(info, inverse, x_seg, target_seg, full_w, full_g)
+        scratch_shapes=[
+            pltpu.VMEM((HEADS, seg, dim), BF16),
+            pltpu.VMEM((seg, width), F32),
+            pltpu.VMEM((layers, 48, part, width), BF16),
+            pltpu.VMEM((layers, 8, 8, 128), F32),
+            pltpu.SemaphoreType.DMA((2, 3)),
+            pltpu.SemaphoreType.DMA((2, layers, 4)),
+            pltpu.SemaphoreType.DMA((2, layers, 4)),
+            pltpu.SemaphoreType.DMA((2, layers, 8)),
+            pltpu.SemaphoreType.DMA((2, 10)),
+            pltpu.SemaphoreType.DMA((layers,)),
+        ],
+        compiler_params=pltpu.CompilerParams(
+            vmem_limit_bytes=VMEM_LIMIT, collective_id=0, has_side_effects=True
+        ),
+    )(info, inverse, x_seg, target_seg, own_w, own_gain)
 
 
 def backward(layers, loss_grad, full_w, full_g, sent, saved):
@@ -801,12 +1025,7 @@
         w_master[0].astype(BF16).reshape(own_blocks // 4, 4, part, part).transpose(0, 2, 1, 3)
         .reshape(own_blocks // 4, part, width)
     )
-    full_w = lax.all_gather(own_w, ("section", "dp"), axis=0, tiled=True).reshape(
-        layers, -1, part, width
-    )
-    full_g = lax.all_gather(
-        lax.all_gather(norm_gains[0], "dp", axis=1, tiled=True), "section", axis=0
-    ).astype(BF16).astype(F32)
+    gain_tile = jnp.zeros((8, 128), F32).at[:2, :own_gain].set(norm_gains[0])
     slot = jnp.minimum(section_idx, micro - 1)
     used = (section_idx < micro).astype(jnp.int32)
     at = group_idx * micro + slot
@@ -814,8 +1033,11 @@
     frame_count = jnp.sum(valid_len).astype(F32)
     x_seg = lax.dynamic_slice_in_dim(x_in, slot * seg, seg, 0)
     target_seg = lax.dynamic_slice_in_dim(targets, slot * seg, seg, 0)
-    *saved, sent, loss_grad, stats = forward(
-        layers, info, (1.0 / frame_count)[None], x_seg, target_seg, full_w, full_g
+    *saved, sent, loss_grad, stats, full_w, tiles = forward(
+        layers, info, (1.0 / frame_count)[None], x_seg, target_seg, own_w, gain_tile
+    )
+    full_g = (
+        tiles[:, :, :2, :own_gain].transpose(0, 2, 1, 3).reshape(layers, 2, width).astype(BF16).astype(F32)
     )
     grads, gain_grads = backward(layers, loss_grad, full_w, full_g, sent, saved)
     own_quads = lax.psum_scatter(
@@ -875,7 +1097,7 @@
     def step(*args):
         layers, groups = mesh.shape["section"], mesh.shape["dp"]
         micro, own_blocks = args[2].shape[0] // groups, args[4].shape[1]
-        if micro <= layers and own_blocks % 4 == 0:
+        if micro <= layers == 4 and groups == 8 and own_blocks == 24:
             return body(*args)
         return pipelined_body(*args)
 

time: 516 us -> 495 us (0.959)
  Pallas kernels: 155 us -> 225 us
  waiting for transfers between devices: 173 us -> 112 us
  blocking collectives: 116 us -> 86.2 us
    pallas_call x1, Pallas kernels: 72.3 us -> 142 us  [forward(): pl.pallas_call(functools.partial(forward_kernel, layers, half), grid=(lay...]
    all_gather x1 -> x0, waiting for transfers between devices: 62.1 us -> none  [body(): lax.all_gather(own_w, ('section', 'dp'), axis=0, tiled=True)]
    all_gather x2 -> x0, blocking collectives: 36.7 us -> none  [the longest x1 31.5 us: body(): lax.all_gather(norm_gains[0], 'dp', axis=1, tiled=True)]
    psum x1, blocking collectives: 39.3 us -> 45.8 us  [body(): lax.psum((gain_grads[:, :2], jnp.sum(stats, axis=2)), ('section', 'dp'))]
  transfers between devices with their start and end apart: 2 -> 1, of which waited for: 2 -> 1; matrix products, arithmetic and copies ran while one was open for 3% -> 2% of each run, Pallas kernels for 0% -> 0%
where the time goes in v2:
time: 495 us; the launch traced here: 494 us
  Pallas kernels  225 us (45%)
  waiting for transfers between devices  112 us (23%)
  blocking collectives  86.2 us (17%)
  local copies, waits for them, and re-layouts  27.3 us (6%)
  between operations  21.3 us (4%)
  other arithmetic  14.1 us (3%)
  matrix products  8.17 us (2%)
    pallas_call x1, Pallas kernels, forward(): pl.pallas_call(functools.partial(forward_kernel, layers, half), grid=(lay...  142 us
    reduce_scatter x1, waiting for transfers between devices, body(): lax.psum_scatter(grads.reshape(-1, part, width), ('section', 'dp'), scatt...  112 us
    pallas_call x1, Pallas kernels, backward(): pl.pallas_call(functools.partial(backward_kernel, layers, half), grid=(la...  82.9 us
    psum x1, blocking collectives, body(): lax.psum((gain_grads[:, :2], jnp.sum(stats, axis=2)), ('section', 'dp'))  45.8 us
    psum x1, blocking collectives, body(): total_square = lax.psum(own_square, ('section', 'dp'))  40.3 us
  transfers between devices with their start and end apart: 1, of which 1 were waited for; matrix products, arithmetic and copies ran while one was open for 2% of the time, Pallas kernels for 0%

profile of v2, /device:TPU:2, one launch (start us, length us, event | category | flops | bytes accessed | tf_op | source)
XLA Modules:
  0.0 494.1 jit_solution(15223317129325653521)
XLA Ops:
  7.2 0.0 copy-start
  7.2 0.0 reduce-scatter.2.cloned.1.call-start
  7.2 1.4 reduce_sum.36
  8.6 1.2 dynamic_slice.18
  9.9 1.1 constant_dynamic-slice_fusion.2
  11.0 1.0 copy.29.target_ref
  12.0 0.8 constant_dynamic-slice_fusion.3.x_ref
  13.5 0.6 convert_element_type.33
  14.1 0.3 copy.33
  14.4 1.2 reshape.110.own_ref
  15.6 0.2 multiply_reduce_fusion
  16.4 0.6 pad_add_fusion.info_ref
  17.1 0.6 scatter.4.own_gain_ref
  17.7 142.4 %shard_map.204 = (bf16[4,8,512,512]{3,2,1,0:T(8,128)(2,1)}, bf16[4,24,512,48]{3,2,1,0:T(8,128)(2,1)}, bf16[4,512,384]{2,1,0:T(8,128)(2,1)}, f32[4,512,384]{2,1,0...) custom-call(s32[5]{0:T(128)} %pad_add_fusion.info_ref, ...), custom_call_target="tpu_custom_call" | custom-call | tf_op jit(solution)/shard_map/pallas_call | solution.py:927
  160.1 0.9 convert_bitcast_fusion
  161.0 0.7 reshape.114.gain_ref
  161.7 82.9 %shard_map.205 = (bf16[4,48,96,384]{3,2,1,0:T(8,128)(2,1)}, f32[4,8,384]{2,1,0:T(8,128)}) custom-call(f32[512,384]{1,0:T(8,128)} %get-tuple-element.35.loss_grad_ref, bf16[4,48,96,384]{3,2,1,0:T(8,128)(2,1)} %get-tuple-element.36.w_ref, f32[4,2,384]{2,1,0:T(2,128)} %reshape.114.gain_ref, bf16[4,512,384]{2,1,0:T(8,128)(2,1)} %get-tuple-element.38.sent_ref, ...), custom_call_target="tpu_custom_call" | custom-call | tf_op jit(solution)/shard_map/pallas_call | solution.py:977
  244.6 0.0 reduce-scatter.2.cloned.1.call-update
  244.6 0.9 slice.43
  245.5 0.1 reduce_sum.39
  246.4 0.5 reshape_squeeze.8
  246.8 1.6 reshape_squeeze.9
  248.5 1.2 broadcast_multiply_fusion.1
  249.7 1.5 mul.172
  251.2 1.2 broadcast_multiply_fusion
  252.4 1.5 mul.175
  254.0 45.8 %psum.21 = f32[4,2,384]{2,1,0:T(2,128)S(1)} all-reduce(f32[4,2,384]{2,1,0:T(2,128)S(1)} %slice.43), channel_id=1, replica_groups=mesh['section'=4,'dp'=8] {'section','dp'}, use_global_device_ids=true, to_apply=%region_3.0 | all-reduce | flops 3072 | bytes 24576 | tf_op jit(solution)/shard_map/psum | solution.py:1050
  299.8 0.7 multiply_reduce_fusion.1
  300.5 111.8 %reduce-scatter.2.cloned.1.call-done = bf16[6,96,384]{2,1,0:T(8,128)(2,1)} async-done(((bf16[192,96,384]{2,1,0:T(8,128)(2,1)}), bf16[6,96,384]{2,1,0:T(8,128)(2,1)}) %reduce-scatter.2.cloned.1.call-update) | async-done | bytes 442384 | tf_op jit(solution)/shard_map/reduce_scatter | solution.py:1043
  412.2 1.8 fusion.2
  415.4 40.3 %all-reduce.1 = (f32[]{:T(128)}, f32[4,8]{1,0:T(4,128)}) all-reduce(f32[]{:T(128)S(6)} %add.65, f32[4,8]{1,0:T(4,128)S(1)} %reduce_sum.39), channel_id=1, replica_groups=mesh['section'=4,'dp'=8] {'section','dp'}, use_global_device_ids=true, to_apply=%region_5.0 | all-reduce | flops 33 | bytes 264 | tf_op jit(solution)/shard_map/psum | solution.py:1055
  456.5 1.1 convert_multiply_fusion
  457.5 1.2 fusion.7
  458.8 1.7 mul.168
  460.5 1.3 pad_maximum_fusion
  461.8 1.2 fusion.8
  463.0 1.3 fusion.9
  464.3 1.6 reshape.113
  466.0 2.3 multiply_subtract_fusion
  468.3 2.6 fusion.1
  470.8 1.6 broadcast_in_dim_reshape.6
  472.4 3.1 fusion
  475.5 3.0 broadcast_in_dim_reshape.7
  478.5 1.2 copy.32
  479.6 2.9 mul.170
  482.5 0.6 slice.48
  483.1 0.5 fusion.5
  484.3 0.7 divide_subtract_fusion
  (29 shorter events, 0.1 us)
Async XLA Ops:
  7.2 4.8 copy-start
  7.2 405.1 %reduce-scatter.2.cloned.1.call-start = ((), (), s32[]{:S(2)}) async-start(), calls=%async_computation.1 | async-start | bytes 14598144 | tf_op jit(solution)/shard_map/reduce_scatter | solution.py:1043
  9.9 3.5 copy-start.5
  14.1 1.5 copy-start.10
  14.1 3.0 copy-start.9
  244.6 0.9 copy-start.8
  244.6 1.7 copy-start.7
  464.3 1.6 copy-start.6
  466.0 2.3 copy-start.4
  470.8 1.6 copy-start.3
  475.5 3.0 copy-start.2
  478.5 6.5 %copy-start.1 = (bf16[2048,384]{1,0:T(8,128)(2,1)S(1)}, bf16[2048,384]{1,0:T(8,128)(2,1)}, u32[]{:S(2)}) copy-start(bf16[2048,384]{1,0:T(8,128)(2,1)} %param.15) | copy-start | bytes 4718596
  479.6 2.9 copy-start.13
  479.6 4.7 copy-start.11
  479.6 4.7 copy-start.12
Sparse Core Ops, SparseCore 0:
  244.8 167.4 reduce-scatter.1

commit v3 on v2

--- a/solution.py
+++ b/solution.py
@@ -11,7 +11,7 @@
 HEADS = 8
 F32 = jnp.float32
 BF16 = jnp.bfloat16
-VMEM_LIMIT = 60 * 1024 * 1024
+VMEM_LIMIT = 61 * 1024 * 1024
 
 
 def dot_nn(a, b):
@@ -377,6 +377,239 @@
             keep_copy(k).wait()
 
 
+class Scatter:
+    def __init__(self, refs, sems):
+        self.grads, self.core_in, self.y_in, self.z_in, self.last_out, self.last_in = refs
+        self.core_sems, self.y_sems, self.z_sems, self.last_sems = sems
+        self.section, self.group, self.core, self.y, self.z_peers = mesh_place()
+        self.x = self.section // 2
+        self.quads = self.grads.shape[3] // 2
+        self.mine = pl.ds(self.core * self.quads, self.quads)
+        self.theirs = pl.ds((1 - self.core) * self.quads, self.quads)
+
+    def core_copy(self, layer, late):
+        slot = lax.rem(layer, 2)
+        zs = pl.ds(0, 1) if late else pl.ds(1, 3)
+        return remote(
+            self.grads.at[slot, zs, :, self.theirs], self.core_in.at[slot, zs],
+            self.core_sems.at[0, slot, int(late)], self.core_sems.at[1, slot, int(late)],
+            self.section + 1 - 2 * self.core, self.group,
+        )
+
+    def y_copy(self, layer, k):
+        slot = lax.rem(layer, 2)
+        return remote(
+            self.grads.at[slot, self.z_peers[k], 1 - self.y, self.mine], self.y_in.at[slot, k],
+            self.y_sems.at[0, slot, k], self.y_sems.at[1, slot, k],
+            self.section, self.group + 1 - 2 * self.y,
+        )
+
+    def z_copy(self, layer, k):
+        slot = lax.rem(layer, 2)
+        return remote(
+            self.grads.at[slot, self.z_peers[k], self.y, self.mine], self.z_in.at[layer, k - 1],
+            self.z_sems.at[0, layer, k - 1], self.z_sems.at[1, layer, k - 1],
+            self.section, self.z_peers[k] * 2 + self.y,
+        )
+
+    def last_copy(self, layer):
+        slot = lax.rem(layer, 2)
+        place = lax.rem(self.section - layer + 4, 4) - 1
+        place = jnp.maximum(place, 0)
+        return remote(
+            self.last_out.at[slot], self.last_in.at[place],
+            self.last_sems.at[0, slot], self.last_sems.at[1, place], layer, self.group,
+        )
+
+    def last_landed(self, place):
+        return remote(
+            self.last_in.at[place], self.last_in.at[place],
+            self.last_sems.at[0, 0], self.last_sems.at[1, place], self.section, self.group,
+        )
+
+    def for_part(self, late, act):
+        for k in (1, 2, 3, 0):
+            @pl.when((self.z_peers[k] == 0) == late)
+            def _():
+                act(k)
+
+    def add_core(self, layer, late):
+        slot = lax.rem(layer, 2)
+        self.core_copy(layer, late).wait_recv()
+
+        def add(i, _):
+            z, y = i // 2, lax.rem(i, 2)
+            for q in range(self.quads):
+                at = self.core * self.quads + q
+                self.grads[slot, z, y, at] = self.grads[slot, z, y, at] + self.core_in[slot, z, y, q]
+            return 0
+
+        lax.fori_loop(0 if late else 2, 2 if late else 8, add, 0)
+        self.for_part(late, lambda k: self.y_copy(layer, k).start())
+
+    def add_y(self, layer, k):
+        slot = lax.rem(layer, 2)
+        self.y_copy(layer, k).wait_recv()
+        for q in range(self.quads):
+            at = self.core * self.quads + q
+            z = self.z_peers[k]
+            self.grads[slot, z, self.y, at] = self.grads[slot, z, self.y, at] + self.y_in[slot, k, q]
+        if k:
+            self.z_copy(layer, k).start()
+
+    def add_y_if(self, layer, k, late):
+        @pl.when((self.z_peers[k] == 0) == late)
+        def _():
+            self.add_y(layer, k)
+
+    def add_z(self, layer, result_ref):
+        slot = lax.rem(layer, 2)
+        for k in range(1, 4):
+            self.z_copy(layer, k).wait_recv()
+        for q in range(self.quads):
+            at = self.core * self.quads + q
+            total = self.grads[slot, self.z_peers[0], self.y, at].astype(F32)
+            for k in range(3):
+                total = total + self.z_in[layer, k, q].astype(F32)
+
+            @pl.when(layer == self.section)
+            def _():
+                result_ref[at] = total
+
+            @pl.when(layer != self.section)
+            def _():
+                self.last_out[slot, q] = total.astype(BF16)
+
+        @pl.when(layer != self.section)
+        def _():
+            self.last_copy(layer).start()
+
+    def wait_sends(self, layer):
+        for late in (False, True):
+            self.core_copy(layer, late).wait_send()
+        for k in range(4):
+            self.y_copy(layer, k).wait_send()
+        for k in range(1, 4):
+            self.z_copy(layer, k).wait_send()
+
+        @pl.when(layer != self.section)
+        def _():
+            self.last_copy(layer).wait_send()
+
+    def collect(self, result_ref):
+        for place in range(3):
+            self.last_landed(place).wait_recv()
+        for q in range(self.quads):
+            mine = self.core * self.quads + q
+            theirs = (1 - self.core) * self.quads + q
+            result_ref[mine] = result_ref[mine] + self.last_in[1, q].astype(F32)
+            result_ref[theirs] = self.last_in[0, q].astype(F32) + self.last_in[2, q].astype(F32)
+
+
+class Totals:
+    def __init__(self, refs, sems):
+        self.stage_in, self.z_in, self.norm_section, self.norm_group = refs
+        self.stage_sems, self.z_sems, self.section_sems, self.group_sems = sems
+        self.section, self.group, self.core, self.y, self.z_peers = mesh_place()
+
+    def stage_copy(self, k):
+        peer = (
+            (self.section + 1 - 2 * self.core, self.group),
+            (self.section, self.group + 1 - 2 * self.y),
+            (lax.rem(self.section + 2, 4), self.group),
+        )[k]
+        return remote(
+            self.stage_in.at[2 * k], self.stage_in.at[2 * k + 1],
+            self.stage_sems.at[0, k], self.stage_sems.at[1, k], *peer,
+        )
+
+    def z_copy(self, k):
+        z = self.z_peers[0]
+        return remote(
+            self.z_in.at[z], self.z_in.at[z], self.z_sems.at[0, k - 1], self.z_sems.at[1, k - 1],
+            self.section, self.z_peers[k] * 2 + self.y,
+        )
+
+    def z_landed(self, k):
+        z = self.z_peers[k]
+        return remote(
+            self.z_in.at[z], self.z_in.at[z], self.z_sems.at[0, k - 1], self.z_sems.at[1, k - 1],
+            self.section, self.z_peers[k] * 2 + self.y,
+        )
+
+    def begin(self, tile):
+        self.stage_in[0] = tile
+        self.stage_copy(0).start()
+
+    def after_core(self):
+        self.stage_copy(0).wait_recv()
+        self.stage_in[2] = self.stage_in[0] + self.stage_in[1]
+        self.stage_copy(1).start()
+
+    def after_y(self):
+        self.stage_copy(1).wait_recv()
+        self.z_in[self.z_peers[0]] = self.stage_in[2] + self.stage_in[3]
+        for k in range(1, 4):
+            self.z_copy(k).start()
+
+    def after_z(self):
+        for k in range(1, 4):
+            self.z_landed(k).wait_recv()
+        self.stage_in[4] = self.z_in[0] + self.z_in[1] + self.z_in[2] + self.z_in[3]
+        self.stage_copy(2).start()
+
+    def after_x(self):
+        self.stage_copy(2).wait_recv()
+        return self.stage_in[4] + self.stage_in[5]
+
+    def norm_copy(self, k):
+        if k < 3:
+            peer = (lax.rem(self.section + k + 1, 4), self.group)
+            ref = self.norm_section.at[self.section]
+            return remote(ref, ref, self.section_sems.at[0, k], self.section_sems.at[1, k], *peer)
+        k = k - 3
+        peer = (self.section, lax.rem(self.group + k + 1, 8))
+        ref = self.norm_group.at[self.group]
+        return remote(ref, ref, self.group_sems.at[0, k], self.group_sems.at[1, k], *peer)
+
+    def norm_landed(self, k):
+        if k < 3:
+            ref = self.norm_section.at[lax.rem(self.section - k - 1 + 4, 4)]
+            return remote(
+                ref, ref, self.section_sems.at[0, k], self.section_sems.at[1, k], self.section, self.group
+            )
+        k = k - 3
+        ref = self.norm_group.at[lax.rem(self.group - k - 1 + 8, 8)]
+        return remote(ref, ref, self.group_sems.at[0, k], self.group_sems.at[1, k], self.section, self.group)
+
+    def norm(self, value):
+        self.norm_section[self.section] = value
+        for k in range(3):
+            self.norm_copy(k).start()
+        for k in range(3):
+            self.norm_landed(k).wait_recv()
+        total = self.norm_section[0]
+        for k in range(1, 4):
+            total = total + self.norm_section[k]
+        self.norm_group[self.group] = total
+        for k in range(3, 10):
+            self.norm_copy(k).start()
+        for k in range(3, 10):
+            self.norm_landed(k).wait_recv()
+        total = self.norm_group[0]
+        for k in range(1, 8):
+            total = total + self.norm_group[k]
+        return total
+
+    def end(self):
+        for k in range(3):
+            self.stage_copy(k).wait_send()
+        for k in range(1, 4):
+            self.z_copy(k).wait_send()
+        for k in range(10):
+            self.norm_copy(k).wait_send()
+
+
 def norm_reverse(value, gain, grad):
     factor = lax.rsqrt(jnp.mean(value * value, axis=-1, keepdims=True) + 1e-06)
     scaled = grad * gain
@@ -388,9 +621,10 @@
 
 def backward_kernel(
     layers, half, loss_grad_ref, w_ref, gain_ref, sent_ref,
-    probs_ref, heads_ref, att_ref, middle_ref, hidden_ref, slope_ref,
-    grads_ref, gain_grad_ref,
+    probs_ref, heads_ref, att_ref, middle_ref, hidden_ref, slope_ref, stats_ref,
+    result_ref, totals_ref, square_ref,
     sends_ref, dffn_ref, dpre_ref, normed_ref, dmid_ref, datt_ref, dhold_ref, dheads_ref, dqkv_ref,
+    gain_grad_ref, *comm_refs,
 ):
     seg, width = loss_grad_ref.shape
     dim = width // HEADS
@@ -400,15 +634,33 @@
     chunks = seg // rows
     gain_one = gain_ref[0, 0:1]
     gain_two = gain_ref[0, 1:2]
-    gain_grad_ref[...] = jnp.zeros_like(gain_grad_ref)
+    scatter = Scatter(comm_refs[:6], comm_refs[10:14])
+    totals = Totals(comm_refs[6:10], comm_refs[14:])
+    grads_ref = comm_refs[0]
+    slot = lax.rem(layer, 2)
 
     @pl.when(layer == layers - 1)
     def _():
+        section, group = scatter.section, scatter.group
+        greet(
+            [(lax.rem(section + k, 4), group) for k in range(1, 4)]
+            + [(section, lax.rem(group + k, 8)) for k in range(1, 8)]
+        )
         sends_ref[...] = jnp.zeros_like(sends_ref)
+        gain_grad_ref[...] = jnp.zeros_like(gain_grad_ref)
 
     def put_grad(first, step, value):
         for r in range(4):
-            grads_ref[0, first + step * r] = value[r * part : (r + 1) * part].astype(grads_ref.dtype)
+            quad = first + step * r
+            owner = quad // 6
+            grads_ref[slot, owner // 2, lax.rem(owner, 2), lax.rem(quad, 6)] = value[
+                r * part : (r + 1) * part
+            ].astype(BF16)
+
+    def before(act):
+        @pl.when(layer < layers - 1)
+        def _():
+            act(layer + 1)
 
     def ffn_step(i, _):
         at = pl.ds(pl.multiple_of(i * rows, rows), rows)
@@ -426,7 +678,7 @@
             dpre_ref[c, at] = dpre
             dnormed = dnormed + dot_nt(dpre, stack_quads(w_ref, 16 + c, 4, 4))
         back, gain_grad, normed = norm_reverse(middle_ref[0, at], gain_two, dnormed)
-        gain_grad_ref[0, 1:2] += gain_grad
+        gain_grad_ref[layer, 1:2] += gain_grad
         normed_ref[at] = normed
         dmid = upstream + back
         dmid_ref[at] = dmid
@@ -435,9 +687,19 @@
         dattended = dot_nt(datt, stack_quads(w_ref, 12, 1, 4)).astype(BF16)
         for h in range(HEADS):
             dhold_ref[h, at] = dattended[:, h * dim : (h + 1) * dim]
+
+        @pl.when(i == 0)
+        def _():
+            before(lambda at: scatter.add_core(at, True))
+
         return 0
 
     lax.fori_loop(0, chunks, ffn_step, 0)
+    before(lambda at: scatter.for_part(True, lambda k: scatter.add_y(at, k)))
+
+    @pl.when(layer < layers - 2)
+    def _():
+        scatter.wait_sends(layer + 2)
 
     def ffn_grad_step(c, _):
         put_grad(32 + 4 * c, 1, dot_tn(hidden_ref[0, c], dffn_ref[...]))
@@ -446,6 +708,7 @@
 
     lax.fori_loop(0, 4, ffn_grad_step, 0)
     put_grad(12, 1, dot_tn(att_ref[0], datt_ref[...]))
+    scatter.core_copy(layer, False).start()
 
     def head_step(h, _):
         queries = heads_ref[0, h]
@@ -466,6 +729,16 @@
             dkeys = dkeys + dot_tn(dscores, heads_ref[0, h, at])
         dheads_ref[HEADS + h] = (dkeys * dim ** (-0.5)).astype(BF16)
         dheads_ref[2 * HEADS + h] = dvalues.astype(BF16)
+
+        @pl.when(h == 1)
+        def _():
+            scatter.add_core(layer, False)
+
+        for k, after in ((1, 5), (2, 6), (3, 7)):
+            @pl.when(h == after)
+            def _():
+                scatter.add_y_if(layer, k, False)
+
         return 0
 
     lax.fori_loop(0, HEADS, head_step, 0)
@@ -481,7 +754,7 @@
         skip = sent_ref[jnp.maximum(layer + 1 - half, 0), at].astype(F32)
         stream = prev + jnp.where(layer >= half, skip, 0.0)
         back, gain_grad, normed = norm_reverse(stream, gain_one, dnormed)
-        gain_grad_ref[0, 0:1] += gain_grad
+        gain_grad_ref[layer, 0:1] += gain_grad
         normed_ref[at] = normed
         sends_ref[layer, at] = (dmid_ref[at] + back).astype(BF16)
         return 0
@@ -493,6 +766,39 @@
         return 0
 
     lax.fori_loop(0, 3, qkv_grad_step, 0)
+    scatter.add_y_if(layer, 0, False)
+    scatter.core_copy(layer, True).start()
+    before(lambda at: scatter.add_z(at, result_ref))
+
+    @pl.when(layer == 0)
+    def _():
+        lane = lax.broadcasted_iota(jnp.int32, (1, width), 1)
+        rows_out = [gain_grad_ref[k // 2, k % 2 : k % 2 + 1] for k in range(2 * layers)]
+        for k in range(layers):
+            row = jnp.zeros((1, width), F32)
+            for i in range(4):
+                value = jnp.sum(stats_ref[k, i : i + 1], axis=1, keepdims=True)
+                row = jnp.where(lane == i, value, row)
+            rows_out.append(row)
+        rows_out.append(jnp.zeros((16 - 3 * layers, width), F32))
+        totals.begin(jnp.concatenate(rows_out, axis=0))
+        scatter.add_core(0, True)
+        totals.after_core()
+        scatter.for_part(True, lambda k: scatter.add_y(0, k))
+        totals.after_y()
+        scatter.add_z(0, result_ref)
+        totals.after_z()
+        scatter.collect(result_ref)
+        square = jnp.zeros((8, width), F32)
+        for q in range(6):
+            value = result_ref[q]
+            square = square + jnp.sum((value * value).reshape(part // 8, 8, width), axis=0)
+        folded = square[:, :128] + square[:, 128:256] + square[:, 256:]
+        square_ref[...] = totals.norm(folded)
+        totals_ref[...] = totals.after_x()
+        scatter.wait_sends(1)
+        scatter.wait_sends(0)
+        totals.end()
 
 
 FF = 1536
@@ -964,7 +1270,7 @@
     )(info, inverse, x_seg, target_seg, own_w, own_gain)
 
 
-def backward(layers, loss_grad, full_w, full_g, sent, saved):
+def backward(layers, loss_grad, full_w, full_g, sent, saved, stats):
     seg, width = loss_grad.shape
     dim = width // HEADS
     part = width // 4
@@ -983,14 +1289,13 @@
             from_end(full_g),
             whole_block((layers, seg, width)),
         ]
-        + [from_end(a) for a in saved],
-        out_specs=[
-            pl.BlockSpec((1, 48, part, width), lambda i: (layers - 1 - i, 0, 0, 0)),
-            pl.BlockSpec((1, 8, width), lambda i: (layers - 1 - i, 0, 0)),
-        ],
+        + [from_end(a) for a in saved]
+        + [pl.BlockSpec(memory_space=pltpu.VMEM)],
+        out_specs=[pl.BlockSpec(memory_space=pltpu.VMEM)] * 3,
         out_shape=[
-            jax.ShapeDtypeStruct((layers, 48, part, width), BF16),
-            jax.ShapeDtypeStruct((layers, 8, width), F32),
+            jax.ShapeDtypeStruct((6, part, width), F32),
+            jax.ShapeDtypeStruct((16, width), F32),
+            jax.ShapeDtypeStruct((8, 128), F32),
         ],
         scratch_shapes=[
             pltpu.VMEM((layers, seg, width), BF16),
@@ -1002,9 +1307,30 @@
             pltpu.VMEM((HEADS, seg, dim), BF16),
             pltpu.VMEM((3 * HEADS, seg, dim), BF16),
             pltpu.VMEM((3, seg, width), BF16),
+            pltpu.VMEM((layers, 8, width), F32),
+            pltpu.VMEM((2, 4, 2, 6, part, width), BF16),
+            pltpu.VMEM((2, 4, 2, 3, part, width), BF16),
+            pltpu.VMEM((2, 4, 3, part, width), BF16),
+            pltpu.VMEM((layers, 3, 3, part, width), BF16),
+            pltpu.VMEM((2, 3, part, width), BF16),
+            pltpu.VMEM((3, 3, part, width), BF16),
+            pltpu.VMEM((6, 16, width), F32),
+            pltpu.VMEM((4, 16, width), F32),
+            pltpu.VMEM((4, 8, 128), F32),
+            pltpu.VMEM((8, 8, 128), F32),
+            pltpu.SemaphoreType.DMA((2, 2, 2)),
+            pltpu.SemaphoreType.DMA((2, 2, 4)),
+            pltpu.SemaphoreType.DMA((2, layers, 3)),
+            pltpu.SemaphoreType.DMA((2, 3)),
+            pltpu.SemaphoreType.DMA((2, 3)),
+            pltpu.SemaphoreType.DMA((2, 3)),
+            pltpu.SemaphoreType.DMA((2, 3)),
+            pltpu.SemaphoreType.DMA((2, 7)),
         ],
-        compiler_params=pltpu.CompilerParams(vmem_limit_bytes=VMEM_LIMIT),
-    )(loss_grad, full_w, full_g, sent, *saved)
+        compiler_params=pltpu.CompilerParams(
+            vmem_limit_bytes=VMEM_LIMIT, collective_id=1, has_side_effects=True
+        ),
+    )(loss_grad, full_w, full_g, sent, *saved, stats)
 
 
 def body(
@@ -1039,20 +1365,17 @@
     full_g = (
         tiles[:, :, :2, :own_gain].transpose(0, 2, 1, 3).reshape(layers, 2, width).astype(BF16).astype(F32)
     )
-    grads, gain_grads = backward(layers, loss_grad, full_w, full_g, sent, saved)
-    own_quads = lax.psum_scatter(
-        grads.reshape(-1, part, width), ("section", "dp"), scatter_dimension=0, tiled=True
-    ).astype(F32)
+    own_quads, tile, squares = backward(layers, loss_grad, full_w, full_g, sent, saved, stats)
     own_grad = (
         own_quads.reshape(own_blocks // 4, part, 4, part).transpose(0, 2, 1, 3)
         .reshape(own_blocks, part * part)
     )
-    summed_g, sums = lax.psum((gain_grads[:, :2], jnp.sum(stats, axis=2)), ("section", "dp"))
+    summed_g = tile[: 2 * layers].reshape(layers, 2, width)
+    sums = tile[2 * layers : 3 * layers, :4]
     own_gain_grad = lax.dynamic_slice(
         summed_g, (section_idx, 0, group_idx * own_gain), (1, 2, own_gain)
     )[0]
-    own_square = jnp.sum(own_grad * own_grad) + jnp.sum(own_gain_grad * own_gain_grad)
-    total_square = lax.psum(own_square, ("section", "dp"))
+    total_square = jnp.sum(squares) + jnp.sum(summed_g * summed_g)
     loss_value = sums[0, 3] / frame_count
     grad_norm = jnp.sqrt(total_square)
     clip_limit = 0.00015 * math.sqrt(layers * (own_blocks * groups * part * part + 2 * width))

time: 495 us -> 383 us (0.77)
  waiting for transfers between devices: 112 us -> 0 us
  Pallas kernels: 225 us -> 318 us
  blocking collectives: 86.2 us -> 0 us
  between operations: 21.3 us -> 7.21 us
    reduce_scatter x1 -> x0, waiting for transfers between devices: 112 us -> none  [body(): lax.psum_scatter(grads.reshape(-1, part, width), ('section', 'dp'), scatt...]
    pallas_call x1, Pallas kernels: 82.9 us -> 176 us  [backward(): pl.pallas_call(functools.partial(backward_kernel, layers, half), grid=(la...]
    psum x2 -> x0, blocking collectives: 86.2 us -> none  [the longest x1 45.8 us: body(): lax.psum((gain_grads[:, :2], jnp.sum(stats, axis=2)), ('section', 'dp'))]
  transfers between devices with their start and end apart: 1 -> 0, of which waited for: 1 -> 0; matrix products, arithmetic and copies ran while one was open for 2% -> 0% of each run, Pallas kernels for 0% -> 0%
where the time goes in v3:
time: 383 us; the launch traced here: 382 us
  Pallas kernels  318 us (83%)
  local copies, waits for them, and re-layouts  31.9 us (8%)
  matrix products  12.7 us (3%)
  other arithmetic  12.4 us (3%)
  between operations  7.21 us (2%)
    pallas_call x1, Pallas kernels, backward(): pl.pallas_call(functools.partial(backward_kernel, layers, half), grid=(la...  176 us
    pallas_call x1, Pallas kernels, forward(): pl.pallas_call(functools.partial(forward_kernel, layers, half), grid=(lay...  142 us

profile of v3, /device:TPU:2, one launch (start us, length us, event | category | flops | bytes accessed | tf_op | source)
XLA Modules:
  0.0 381.9 jit_solution(6140659772750876732)
XLA Ops:
  0.6 0.0 copy-start
  0.7 1.4 dynamic_slice.18
  2.7 0.9 multiply_reduce_fusion.1
  3.5 0.6 pad_add_fusion.info_ref
  4.1 1.1 constant_dynamic-slice_fusion.2
  5.2 1.0 copy.29.target_ref
  6.2 0.8 constant_dynamic-slice_fusion.3.x_ref
  7.0 0.6 reduce_sum.27
  8.4 0.0 copy-done.2
  8.4 0.6 convert_element_type.30
  9.0 0.0 copy-start.7
  9.0 0.3 copy.31
  9.3 1.2 reshape.108.own_ref
  10.5 0.6 scatter.4.own_gain_ref
  11.1 142.2 %shard_map.204 = (bf16[4,8,512,512]{3,2,1,0:T(8,128)(2,1)}, bf16[4,24,512,48]{3,2,1,0:T(8,128)(2,1)}, bf16[4,512,384]{2,1,0:T(8,128)(2,1)}, f32[4,512,384]{2,1,0...) custom-call(s32[5]{0:T(128)} %pad_add_fusion.info_ref, ...), custom_call_target="tpu_custom_call" | custom-call | tf_op jit(solution)/shard_map/pallas_call | solution.py:1233
  153.3 0.9 convert_bitcast_fusion
  154.2 0.7 reshape.112.gain_ref
  154.9 175.6 %shard_map.205 = (f32[6,96,384]{2,1,0:T(8,128)}, f32[16,384]{1,0:T(8,128)}, f32[8,128]{1,0:T(8,128)}) custom-call(f32[512,384]{1,0:T(8,128)} %get-tuple-element.36.loss_grad_ref, bf16[4,48,96,384]{3,2,1,0:T(8,128)(2,1)} %get-tuple-element.37.w_ref, f32[4,2,384]{2,1,0:T(2,128)} %reshape.112.gain_ref, bf16[4,512,384]{2,1,0:T(8,128)(2,1)} %get-tuple-element.39.sent_ref, ...), custom_call_target="tpu_custom_call" | custom-call | tf_op jit(solution)/shard_map/pallas_call | solution.py:1283
  330.5 1.3 fusion.8
  331.8 1.3 reduce_sum.28
  335.2 0.7 divide_subtract_fusion
  335.9 1.2 broadcast_multiply_fusion.2
  337.1 0.3 fusion.7
  337.4 0.0 copy-start.6
  337.4 0.1 pad_maximum_fusion
  337.5 1.1 copy-done.6
  338.6 1.5 reshape_squeeze.8
  340.1 2.5 fusion.9
  342.6 2.7 reshape_squeeze.9
  345.2 3.6 fusion.10
  348.8 3.0 reshape.110
  351.8 2.3 multiply_subtract_fusion
  354.1 1.0 broadcast_multiply_fusion.1
  355.1 1.6 mul.164
  356.7 3.6 fusion.1
  360.3 3.0 broadcast_in_dim_reshape.6
  363.2 0.0 copy-done.5
  363.3 1.0 broadcast_multiply_fusion
  364.2 1.6 mul.167
  365.9 3.1 fusion
  369.0 2.9 broadcast_in_dim_reshape.7
  371.8 0.7 mul.160
  372.5 0.0 copy-start.1
  372.5 1.2 copy.26
  373.7 2.9 mul.162
  376.5 0.7 slice.53
  377.2 0.5 fusion.5
  377.8 1.3 slice.52
  (18 shorter events, 0.1 us)
Async XLA Ops:
  0.6 5.6 %copy-start = (bf16[2048,384]{1,0:T(8,128)(2,1)S(1)}, bf16[2048,384]{1,0:T(8,128)(2,1)}, u32[]{:S(2)}) copy-start(bf16[2048,384]{1,0:T(8,128)(2,1)} %param.15) | copy-start | bytes 4718596
  4.1 2.9 copy-start.10
  4.1 4.2 %copy-start.2 = (f32[1,24,9216]{2,1,0:T(8,128)S(1)}, f32[1,24,9216]{2,1,0:T(8,128)}, u32[]{:S(2)}) copy-start(f32[1,24,9216]{2,1,0:T(8,128)} %param.19) | copy-start | bytes 2654212
  9.0 1.5 copy-start.7
  154.9 180.3 %copy-start.8 = (f32[1,2,48]{2,1,0:T(2,128)S(1)}, f32[1,2,48]{2,1,0:T(2,128)}, u32[]{:S(2)}) copy-start(f32[1,2,48]{2,1,0:T(2,128)} %param.21) | copy-start | bytes 1156
  154.9 180.3 %copy-start.9 = (f32[1,2,48]{2,1,0:T(2,128)S(1)}, f32[1,2,48]{2,1,0:T(2,128)}, u32[]{:S(2)}) copy-start(f32[1,2,48]{2,1,0:T(2,128)} %param.22) | copy-start | bytes 1156
  337.4 1.2 copy-start.6
  348.8 3.0 copy-start.3
  351.8 2.3 copy-start.4
  360.3 3.0 copy-start.5
  372.5 7.2 %copy-start.1 = (bf16[2048,384]{1,0:T(8,128)(2,1)S(1)}, bf16[2048,384]{1,0:T(8,128)(2,1)}, u32[]{:S(2)}) copy-start(bf16[2048,384]{1,0:T(8,128)(2,1)} %param.15) | copy-start | bytes 4718596

commit v4 on v3

--- a/solution.py
+++ b/solution.py
@@ -299,8 +299,8 @@
             probs = (expd * (1.0 / jnp.sum(expd, axis=-1, keepdims=True))).astype(BF16)
             probs_ref[0, h, at] = probs
             hold_ref[h, at] = dot_nn(probs, values).astype(BF16)
-        for step in range(1, 8):
-            @pl.when(h == step)
+        for step, after in ((1, 1), (2, 4), (3, 7)):
+            @pl.when(h == after)
             def _():
                 serve(step)
         return 0
@@ -333,9 +333,16 @@
         valid = (lax.broadcasted_iota(jnp.int32, (rows, 1), 0) + i * rows < length).astype(F32)
         for k, value in enumerate((stream, branch_attn, branch_ffn)):
             stats_ref[layer, k : k + 1] += jnp.sum(valid * value * value, axis=0, keepdims=True)
+
+        @pl.when(i == 0)
+        def _():
+            serve(4)
+
         return 0
 
     lax.fori_loop(0, chunks, ffn_step, 0)
+    for step in range(5, 8):
+        serve(step)
 
     @pl.when(layer == layers - 1)
     def _():
@@ -691,11 +698,15 @@
         @pl.when(i == 0)
         def _():
             before(lambda at: scatter.add_core(at, True))
+            before(lambda at: scatter.add_y_if(at, 2, False))
+
+        @pl.when(i == 1)
+        def _():
+            before(lambda at: scatter.add_y_if(at, 3, False))
 
         return 0
 
     lax.fori_loop(0, chunks, ffn_step, 0)
-    before(lambda at: scatter.for_part(True, lambda k: scatter.add_y(at, k)))
 
     @pl.when(layer < layers - 2)
     def _():
@@ -709,6 +720,8 @@
     lax.fori_loop(0, 4, ffn_grad_step, 0)
     put_grad(12, 1, dot_tn(att_ref[0], datt_ref[...]))
     scatter.core_copy(layer, False).start()
+    before(lambda at: scatter.add_y_if(at, 0, False))
+    before(lambda at: scatter.for_part(True, lambda k: scatter.add_y(at, k)))
 
     def head_step(h, _):
         queries = heads_ref[0, h]
@@ -730,14 +743,9 @@
         dheads_ref[HEADS + h] = (dkeys * dim ** (-0.5)).astype(BF16)
         dheads_ref[2 * HEADS + h] = dvalues.astype(BF16)
 
-        @pl.when(h == 1)
+        @pl.when(h == 3)
         def _():
             scatter.add_core(layer, False)
-
-        for k, after in ((1, 5), (2, 6), (3, 7)):
-            @pl.when(h == after)
-            def _():
-                scatter.add_y_if(layer, k, False)
 
         return 0
 
@@ -766,9 +774,9 @@
         return 0
 
     lax.fori_loop(0, 3, qkv_grad_step, 0)
-    scatter.add_y_if(layer, 0, False)
     scatter.core_copy(layer, True).start()
     before(lambda at: scatter.add_z(at, result_ref))
+    scatter.add_y_if(layer, 1, False)
 
     @pl.when(layer == 0)
     def _():
@@ -783,7 +791,10 @@
         rows_out.append(jnp.zeros((16 - 3 * layers, width), F32))
         totals.begin(jnp.concatenate(rows_out, axis=0))
         scatter.add_core(0, True)
+        scatter.add_y_if(0, 2, False)
         totals.after_core()
+        scatter.add_y_if(0, 3, False)
+        scatter.add_y_if(0, 0, False)
         scatter.for_part(True, lambda k: scatter.add_y(0, k))
         totals.after_y()
         scatter.add_z(0, result_ref)
@@ -1333,6 +1344,122 @@
     )(loss_grad, full_w, full_g, sent, *saved, stats)
 
 
+def flat_rows(array):
+    blocks, area = array.shape
+    return (
+        array.reshape(blocks // 8, 8, area // 128, 128).transpose(0, 2, 1, 3).reshape(-1, 128)
+    )
+
+
+def from_flat_rows(rows, blocks):
+    return (
+        rows.reshape(blocks // 8, -1, 8, 128).transpose(0, 2, 1, 3).reshape(blocks, -1)
+    )
+
+
+def load_block(rows_ref, base, block_ref):
+    lane = lax.broadcasted_iota(jnp.int32, (24, 128), 1)
+    a, b, c = (rows_ref[pl.ds(base + 8 * m, 24, stride=24), :] for m in range(3))
+    block_ref[pl.ds(0, 24, stride=4), :] = a
+    block_ref[pl.ds(1, 24, stride=4), :] = jnp.where(lane < 32, pltpu.roll(a, 32, 1), pltpu.roll(b, 32, 1))
+    block_ref[pl.ds(2, 24, stride=4), :] = jnp.where(lane < 64, pltpu.roll(b, 64, 1), pltpu.roll(c, 64, 1))
+    block_ref[pl.ds(3, 24, stride=4), :] = pltpu.roll(c, 96, 1)
+
+
+def flat_parts(block_ref):
+    lane = lax.broadcasted_iota(jnp.int32, (24, 128), 1)
+    a, b, c, d = (block_ref[pl.ds(r, 24, stride=4), :] for r in range(4))
+    b, c, d = pltpu.roll(b, 96, 1), pltpu.roll(c, 64, 1), pltpu.roll(d, 32, 1)
+    return jnp.where(lane < 96, a, b), jnp.where(lane < 64, b, c), jnp.where(lane < 32, c, d)
+
+
+def split(value):
+    high = value.astype(BF16)
+    return high, (value - high.astype(F32)).astype(BF16)
+
+
+def dot_split(dot, left, right):
+    return dot(left[0], right[0]) + (dot(left[0], right[1]) + dot(left[1], right[0]))
+
+
+def update_kernel(
+    layers, limit, step_ref, square_ref, tile_ref, quads_ref, w_ref, l_ref, r_ref, lroot_ref, rroot_ref,
+    gain_ref, gain_m_ref, gain_v_ref,
+    w_out, grad_out, l_out, r_out, gain_out, m_out, v_out, norm_out,
+    block_ref,
+):
+    part, width = quads_ref.shape[1:]
+    gains = tile_ref[: 2 * layers]
+    norm = jnp.sqrt(jnp.sum(square_ref[...], keepdims=True) + jnp.sum(gains * gains, keepdims=True))
+    factor = limit / jnp.maximum(norm, limit)
+
+    def quad_step(q, _):
+        for c in range(4):
+            base = 4 * q + c
+            load_block(lroot_ref, base, block_ref.at[0])
+            load_block(rroot_ref, base, block_ref.at[1])
+            grad = quads_ref[q, :, part * c : part * (c + 1)] * factor
+            pair = split(grad)
+            left = dot_split(dot_nn, split(block_ref[0, :, :part]), pair)
+            pre = dot_split(dot_nn, split(left), split(block_ref[1, :, :part]))
+            for i, value in enumerate((
+                grad, pre, dot_split(dot_nt, pair, pair), dot_split(dot_tn, pair, pair)
+            )):
+                block_ref[2 + i, :, :part] = value
+            parts = [flat_parts(block_ref.at[2 + i]) for i in range(4)]
+            for m in range(3):
+                at = (pl.ds(base + 8 * m, 24, stride=24), slice(None))
+                grad_out[at] = parts[0][m]
+                master = w_ref[at]
+                w_out[at] = master - 0.5 * (parts[1][m] + 0.01 * master)
+                l_out[at] = 0.95 * l_ref[at] + 0.05 * parts[2][m]
+                r_out[at] = 0.95 * r_ref[at] + 0.05 * parts[3][m]
+        return 0
+
+    lax.fori_loop(0, 2, quad_step, 0)
+
+    @pl.when(pl.program_id(0) == 0)
+    def _():
+        section, group = lax.axis_index("section"), lax.axis_index("dp")
+        share = gain_ref.shape[1]
+        row = tile_ref[:2]
+        for k in range(1, layers):
+            row = jnp.where(section == k, tile_ref[2 * k : 2 * k + 2], row)
+        own = row[:, :share]
+        for g in range(1, width // share):
+            own = jnp.where(group == g, row[:, g * share : (g + 1) * share], own)
+        grad = own * factor
+        m_new = 0.9 * gain_m_ref[...] + 0.1 * grad
+        v_new = 0.999 * gain_v_ref[...] + 0.001 * grad * grad
+        step = jnp.full((1, 1), step_ref[0], jnp.int32).astype(F32)
+        m_hat = m_new / (1.0 - jnp.exp(step * math.log(0.9)))
+        v_hat = v_new / (1.0 - jnp.exp(step * math.log(0.999)))
+        gain_out[...] = gain_ref[...] - 0.5 * m_hat / (jnp.sqrt(v_hat) + 1e-08)
+        m_out[...] = m_new
+        v_out[...] = v_new
+        norm_out[...] = jnp.broadcast_to(norm, norm_out.shape)
+
+
+def update(layers, limit, step_count, squares, tile, quads, flats, gains):
+    blocks = 4 * quads.shape[0]
+    part, width = quads.shape[1:]
+    rows = flats[0].shape[0]
+    whole = [pl.BlockSpec(memory_space=pltpu.VMEM)]
+    flat = [pl.BlockSpec((rows // 3, 128), lambda i: (i, 0))]
+    share = gains[0].shape
+    return pl.pallas_call(
+        functools.partial(update_kernel, layers, limit),
+        grid=(3,),
+        in_specs=[pl.BlockSpec(memory_space=pltpu.SMEM)] + whole * 2
+        + [pl.BlockSpec((2, part, width), lambda i: (i, 0, 0))] + flat * 5 + whole * 3,
+        out_specs=flat * 4 + whole * 4,
+        out_shape=[jax.ShapeDtypeStruct((rows, 128), F32)] * 4
+        + [jax.ShapeDtypeStruct(share, F32)] * 3 + [jax.ShapeDtypeStruct((8, 128), F32)],
+        scratch_shapes=[pltpu.VMEM((6, part, 128), F32)],
+        compiler_params=pltpu.CompilerParams(vmem_limit_bytes=VMEM_LIMIT),
+    )(step_count, squares, tile, quads, *flats, *gains)
+
+
 def body(
     x_in, targets, valid_len, present_stems, w_master, norm_gains, gain_m, gain_v,
     l_stats, r_stats, l_roots, r_roots, step_count,
@@ -1366,47 +1493,22 @@
         tiles[:, :, :2, :own_gain].transpose(0, 2, 1, 3).reshape(layers, 2, width).astype(BF16).astype(F32)
     )
     own_quads, tile, squares = backward(layers, loss_grad, full_w, full_g, sent, saved, stats)
-    own_grad = (
-        own_quads.reshape(own_blocks // 4, part, 4, part).transpose(0, 2, 1, 3)
-        .reshape(own_blocks, part * part)
-    )
-    summed_g = tile[: 2 * layers].reshape(layers, 2, width)
     sums = tile[2 * layers : 3 * layers, :4]
-    own_gain_grad = lax.dynamic_slice(
-        summed_g, (section_idx, 0, group_idx * own_gain), (1, 2, own_gain)
-    )[0]
-    total_square = jnp.sum(squares) + jnp.sum(summed_g * summed_g)
     loss_value = sums[0, 3] / frame_count
-    grad_norm = jnp.sqrt(total_square)
     clip_limit = 0.00015 * math.sqrt(layers * (own_blocks * groups * part * part + 2 * width))
-    factor = clip_limit / jnp.maximum(grad_norm, clip_limit)
-    grad_blocks = own_grad * factor
-    square = (own_blocks, part, part)
-    shaped = grad_blocks.reshape(square)
-    highest = lax.Precision.HIGHEST
-    l_new = 0.95 * l_stats[0].reshape(square) + 0.05 * jnp.einsum(
-        "bij,bkj->bik", shaped, shaped, precision=highest
-    )
-    r_new = 0.95 * r_stats[0].reshape(square) + 0.05 * jnp.einsum(
-        "bji,bjk->bik", shaped, shaped, precision=highest
-    )
-    left_side = jnp.einsum("bij,bjk->bik", l_roots[0].reshape(square), shaped, precision=highest)
-    precond = jnp.einsum("bij,bjk->bik", left_side, r_roots[0].reshape(square), precision=highest)
-    master = w_master[0]
-    w_new = master - 0.5 * (precond.reshape(master.shape) + 0.01 * master)
-    gain_grad = own_gain_grad * factor
-    m_new = 0.9 * gain_m[0] + 0.1 * gain_grad
-    v_new = 0.999 * gain_v[0] + 0.001 * gain_grad * gain_grad
-    step_num = step_count[0].astype(F32)
-    m_hat = m_new / (1.0 - jnp.power(0.9, step_num))
-    v_hat = v_new / (1.0 - jnp.power(0.999, step_num))
-    gains_new = norm_gains[0] - 0.5 * m_hat / (jnp.sqrt(v_hat) + 1e-08)
+    flats = [flat_rows(a[0]) for a in (w_master, l_stats, r_stats, l_roots, r_roots)]
+    *news, gains_new, m_new, v_new, norms = update(
+        layers, clip_limit, step_count, squares, tile, own_quads, flats,
+        (norm_gains[0], gain_m[0], gain_v[0]),
+    )
+    w_new, grad_blocks, l_new, r_new = (from_flat_rows(a, own_blocks) for a in news)
+    grad_norm = norms[0, 0]
     rms = jnp.sqrt(sums[section_idx, :3] / (frame_count * width)).reshape(1, 3)
     return (
         w_new[None],
         grad_blocks[None],
-        l_new.reshape(master.shape)[None],
-        r_new.reshape(master.shape)[None],
+        l_new[None],
+        r_new[None],
         gains_new[None],
         m_new[None],
         v_new[None],

time: 383 us -> 317 us (0.83)
  Pallas kernels: 318 us -> 296 us
  local copies, waits for them, and re-layouts: 31.9 us -> 11.4 us
  matrix products: 12.7 us -> 0 us
  other arithmetic: 12.4 us -> 4.24 us
    pallas_call x1, Pallas kernels: 176 us -> 150 us  [backward(): pl.pallas_call(functools.partial(backward_kernel, layers, half), grid=(la...]
    dot_general x4 -> x0, matrix products: 12.7 us -> none  [the longest x1 3.59 us: body(): jnp.einsum('bij,bkj->bik', shaped, shaped, precision=highest)]
    pallas_call x0 -> x1, Pallas kernels: none -> 11.1 us  [update(): pl.pallas_call(functools.partial(update_kernel, layers, limit), grid=(3,)...]
    another operation x5 -> x0, local copies, waits for them, and re-layouts: 10.3 us -> none  [the longest x1 2.95 us: body(): l_new.reshape(master.shape)[None]]
    mul x5 -> x0, local copies, waits for them, and re-layouts: 7.96 us -> none  [the longest x3 4.7 us: body(): grad_blocks = own_grad * factor]
    pallas_call x1, Pallas kernels: 142 us -> 135 us  [forward(): pl.pallas_call(functools.partial(forward_kernel, layers, half), grid=(lay...]
where the time goes in v4:
time: 317 us; the launch traced here: 316 us
  Pallas kernels  296 us (93%)
  local copies, waits for them, and re-layouts  11.4 us (4%)
  between operations  4.51 us (1%)
  other arithmetic  4.24 us (1%)
    pallas_call x1, Pallas kernels, backward(): pl.pallas_call(functools.partial(backward_kernel, layers, half), grid=(la...  150 us
    pallas_call x1, Pallas kernels, forward(): pl.pallas_call(functools.partial(forward_kernel, layers, half), grid=(lay...  135 us
    pallas_call x1, Pallas kernels, update(): pl.pallas_call(functools.partial(update_kernel, layers, limit), grid=(3,)...  11.1 us

profile of v4, /device:TPU:2, one launch (start us, length us, event | category | flops | bytes accessed | tf_op | source)
XLA Modules:
  0.0 316.0 jit_solution(11959972332829243331)
XLA Ops:
  0.6 0.0 copy-start
  0.7 0.0 copy-start.2
  0.7 1.4 dynamic_slice.15
  2.7 0.9 multiply_reduce_fusion
  3.6 0.6 pad_add_fusion.info_ref
  4.2 1.0 constant_dynamic-slice_fusion.1
  5.2 1.0 copy.26.target_ref
  6.2 0.0 copy-done
  6.2 0.8 constant_dynamic-slice_fusion.2.x_ref
  7.0 1.3 reduce_sum.9
  9.0 1.3 scatter.4.own_gain_ref
  10.3 0.0 copy-done.2
  10.3 0.6 convert_element_type.26
  10.9 0.3 copy.28
  11.2 1.2 reshape.93.own_ref
  12.4 134.8 %shard_map.204 = (bf16[4,8,512,512]{3,2,1,0:T(8,128)(2,1)}, bf16[4,24,512,48]{3,2,1,0:T(8,128)(2,1)}, bf16[4,512,384]{2,1,0:T(8,128)(2,1)}, f32[4,512,384]{2,1,0...) custom-call(s32[5]{0:T(128)} %pad_add_fusion.info_ref, ...), custom_call_target="tpu_custom_call" | custom-call | tf_op jit(solution)/shard_map/pallas_call | solution.py:1244
  147.2 0.9 convert_bitcast_fusion
  148.1 0.7 reshape.104.gain_ref
  148.8 0.0 copy-start.1
  148.8 150.0 %shard_map.205 = (f32[6,96,384]{2,1,0:T(8,128)}, f32[16,384]{1,0:T(8,128)}, f32[8,128]{1,0:T(8,128)}) custom-call(f32[512,384]{1,0:T(8,128)} %get-tuple-element.44.loss_grad_ref, bf16[4,48,96,384]{3,2,1,0:T(8,128)(2,1)} %get-tuple-element.45.w_ref, f32[4,2,384]{2,1,0:T(2,128)} %reshape.104.gain_ref, bf16[4,512,384]{2,1,0:T(8,128)(2,1)} %get-tuple-element.47.sent_ref, ...), custom_call_target="tpu_custom_call" | custom-call | tf_op jit(solution)/shard_map/pallas_call | solution.py:1294
  299.5 11.1 %shard_map.206 = (f32[1728,128]{1,0:T(8,128)}, f32[1728,128]{1,0:T(8,128)}, f32[1728,128]{1,0:T(8,128)}, f32[1728,128]{1,0:T(8,128)}, f32[2,48]{1,0:T(2,128)}, /...) custom-call(s32[1]{0:T(128)S(6)} %copy.29.step_ref, f32[8,128]{1,0:T(8,128)} %get-tuple-element.55.square_ref, ...), custom_call_target="tpu_custom_call" | custom-call | tf_op jit(solution)/shard_map/pallas_call | solution.py:1450
  310.5 1.2 slice.36
  311.7 0.7 slice.37
  312.4 0.5 fusion.1
  312.9 1.2 slice.35
  314.8 0.0 copy-done.1
  (2 shorter events, 0.0 us)
Async XLA Ops:
  0.6 5.6 %copy-start = (bf16[2048,384]{1,0:T(8,128)(2,1)S(1)}, bf16[2048,384]{1,0:T(8,128)(2,1)}, u32[]{:S(2)}) copy-start(bf16[2048,384]{1,0:T(8,128)(2,1)} %param.15) | copy-start | bytes 4718596
  0.7 9.6 %copy-start.2 = (f32[1,24,9216]{2,1,0:T(8,128)S(1)}, f32[1,24,9216]{2,1,0:T(8,128)}, u32[]{:S(2)}) copy-start(f32[1,24,9216]{2,1,0:T(8,128)} %param.19) | copy-start | bytes 2654212
  148.8 166.0 %copy-start.1 = (bf16[2048,384]{1,0:T(8,128)(2,1)S(1)}, bf16[2048,384]{1,0:T(8,128)(2,1)}, u32[]{:S(2)}) copy-start(bf16[2048,384]{1,0:T(8,128)(2,1)} %param.15) | copy-start | bytes 4718596

commit v5 on v4

--- a/solution.py
+++ b/solution.py
@@ -44,7 +44,12 @@
 
 
 def stack_quads(w_ref, first, step, number):
-    return jnp.concatenate([w_ref[0, first + step * i] for i in range(number)], axis=0)
+    part = w_ref.shape[2] // 4
+    if step == 1:
+        return w_ref[0, first * part : (first + number) * part]
+    return jnp.concatenate(
+        [w_ref[0, (first + step * i) * part : (first + step * i + 1) * part] for i in range(number)], axis=0
+    )
 
 
 MESH = pl.DeviceIdType.MESH
@@ -74,67 +79,86 @@
     pl.semaphore_wait(barrier, len(places))
 
 
-class Gather:
+class Slabs:
+    def __init__(self, rows):
+        self.section, self.group, self.core, self.y, self.z_peers = mesh_place()
+        self.x = self.section // 2
+        self.rows, self.half = rows, rows // 2
+        self.edge = self.half * 5 // 18
+        self.slab = self.half - self.edge
+
+    def slab_of(self, x, core):
+        return pl.ds(pl.multiple_of(self.half * core + self.edge * x, 16), self.slab)
+
+    def edge_of(self, x, core):
+        return pl.ds(pl.multiple_of(self.half * core + self.slab * x, 16), self.edge)
+
+    def half_of(self, core):
+        return pl.ds(pl.multiple_of(self.half * core, 16), self.half)
+
+    def x_peer(self):
+        return lax.rem(self.section + 2, 4), self.group
+
+    def y_peer(self):
+        return self.section, self.group + 1 - 2 * self.y
+
+    def z_peer(self, k):
+        return self.section, self.z_peers[k] * 2 + self.y
+
+    def core_peer(self):
+        return self.section + 1 - 2 * self.core, self.group
+
+    def greet_all(self):
+        greet(
+            [(lax.rem(self.section + k, 4), self.group) for k in range(1, 4)]
+            + [(self.section, lax.rem(self.group + k, 8)) for k in range(1, 8)]
+        )
+
+
+class Gather(Slabs):
     def __init__(self, own_ref, gain_ref, w_ref, gains_ref, sems):
+        super().__init__(own_ref.shape[0])
         self.own, self.gain, self.w, self.gains = own_ref, gain_ref, w_ref, gains_ref
-        self.spread, self.z_sems, self.y_sems, self.core_sems, self.gain_sems, self.local = sems
-        self.section, self.group, self.core, self.y, self.z_peers = mesh_place()
-        self.quads = own_ref.shape[0] // 2
+        self.spread, self.z_sems, self.y_sems, self.x_sems, self.core_sems, self.gain_sems, self.local = sems
         self.others = [lax.rem(self.section + k, 4) for k in range(1, 4)]
-        self.places = [(o, self.group) for o in self.others] + [
-            (self.section, lax.rem(self.group + k, 8)) for k in range(1, 8)
-        ]
-
-    def piece(self, layer, group):
-        return self.w.at[layer, pl.ds(group * 2 * self.quads + self.quads * self.core, self.quads)]
+
+    def chunk(self, k):
+        y = self.y if k < 4 else 1 - self.y
+        return self.z_peers[k % 4] * 2 + y
+
+    def at(self, layer, group, rows):
+        return self.w.at[layer, pl.ds(pl.multiple_of(group * self.rows + rows.start, 16), rows.size)]
 
     def spread_copy(self, k):
         peer = self.others[k]
-        half = lax.rem(peer, 2) * self.quads
+        rows = self.slab_of(peer // 2, lax.rem(peer, 2))
         return remote(
-            self.own.at[pl.ds(half, self.quads)],
-            self.w.at[self.section, pl.ds(self.group * 2 * self.quads + half, self.quads)],
+            self.own.at[rows], self.at(self.section, self.group, rows),
             self.spread.at[0, k], self.spread.at[1, k], peer, self.group,
         )
 
     def spread_wait(self, layer):
+        ref = self.at(layer, self.group, self.slab_of(self.x, self.core))
         for k in range(3):
             @pl.when(lax.rem(layer + k + 1, 4) == self.section)
             def _():
-                ref = self.piece(layer, self.group)
                 remote(ref, ref, self.spread.at[0, k], self.spread.at[1, k], self.others[0], self.group).wait_recv()
 
-    def z_copy(self, layer, k):
-        ref = self.piece(layer, self.group)
-        return remote(
-            ref, ref, self.z_sems.at[0, layer, k], self.z_sems.at[1, layer, k],
-            self.section, self.z_peers[k] * 2 + self.y,
-        )
-
-    def z_landed(self, layer, k):
-        ref = self.piece(layer, self.z_peers[k] * 2 + self.y)
-        return remote(
-            ref, ref, self.z_sems.at[0, layer, k], self.z_sems.at[1, layer, k],
-            self.section, self.z_peers[k] * 2 + self.y,
-        )
-
-    def y_copy(self, layer, k, mine=True):
-        y = self.y if mine else 1 - self.y
-        ref = self.piece(layer, self.z_peers[k] * 2 + y)
-        return remote(
-            ref, ref, self.y_sems.at[0, layer, k], self.y_sems.at[1, layer, k],
-            self.section, self.group + 1 - 2 * self.y,
-        )
-
-    def core_copy(self, layer, k, mine=True):
-        y = self.y if k < 4 else 1 - self.y
-        core = self.core if mine else 1 - self.core
-        at = (self.z_peers[k % 4] * 2 + y) * 2 * self.quads + self.quads * core
-        ref = self.w.at[layer, pl.ds(at, self.quads)]
-        return remote(
-            ref, ref, self.core_sems.at[0, layer, k], self.core_sems.at[1, layer, k],
-            self.section + 1 - 2 * self.core, self.group,
-        )
+    def z_copy(self, layer, k, landed=False):
+        ref = self.at(layer, self.chunk(k) if landed else self.group, self.slab_of(self.x, self.core))
+        return remote(ref, ref, self.z_sems.at[0, layer, k], self.z_sems.at[1, layer, k], *self.z_peer(k))
+
+    def y_copy(self, layer, k, landed=False):
+        ref = self.at(layer, self.chunk(k + 4 if landed else k), self.slab_of(self.x, self.core))
+        return remote(ref, ref, self.y_sems.at[0, layer, k], self.y_sems.at[1, layer, k], *self.y_peer())
+
+    def x_copy(self, layer, k, landed=False):
+        ref = self.at(layer, self.chunk(k), self.edge_of(1 - self.x if landed else self.x, self.core))
+        return remote(ref, ref, self.x_sems.at[0, layer, k], self.x_sems.at[1, layer, k], *self.x_peer())
+
+    def core_copy(self, layer, k, landed=False):
+        ref = self.at(layer, self.chunk(k), self.half_of(1 - self.core if landed else self.core))
+        return remote(ref, ref, self.core_sems.at[0, layer, k], self.core_sems.at[1, layer, k], *self.core_peer())
 
     def gain_copy(self, k):
         if k < 7:
@@ -156,15 +180,13 @@
         return remote(ref, ref, self.gain_sems.at[0, k], self.gain_sems.at[1, k], self.section, self.group)
 
     def begin(self):
-        greet(self.places)
+        self.greet_all()
         for k in range(3):
             self.spread_copy(k).start()
         for k in range(7):
             self.gain_copy(k).start()
-        half = self.core * self.quads
-        self.w[self.section, pl.ds(self.group * 2 * self.quads + half, self.quads)] = self.own[
-            pl.ds(half, self.quads)
-        ]
+        rows = self.slab_of(self.x, self.core)
+        self.w[self.section, pl.ds(pl.multiple_of(self.group * self.rows + rows.start, 16), rows.size)] = self.own[rows]
         self.gains[self.section, self.group] = self.gain[...]
 
     def share_gains(self):
@@ -182,20 +204,24 @@
         for k in range(1, 4):
             self.z_copy(layer, k).start()
         self.y_copy(layer, 0).start()
-        self.core_copy(layer, 0).start()
-
-    def serve(self, layer, step):
-        if step < 4:
-            self.z_landed(layer, step).wait_recv()
-            self.y_copy(layer, step).start()
-            self.core_copy(layer, step).start()
-        else:
-            self.y_copy(layer, step - 4, False).wait_recv()
-            self.core_copy(layer, step).start()
+        self.x_copy(layer, 0).start()
+
+    def serve_z(self, layer, k):
+        self.z_copy(layer, k, True).wait_recv()
+        self.y_copy(layer, k).start()
+        self.x_copy(layer, k).start()
+
+    def serve_y(self, layer, k):
+        self.y_copy(layer, k, True).wait_recv()
+        self.x_copy(layer, k + 4).start()
+
+    def serve_x(self, layer, k):
+        self.x_copy(layer, k, True).wait_recv()
+        self.core_copy(layer, k).start()
 
     def finish(self, layer):
         for k in range(8):
-            self.core_copy(layer, k, False).wait_recv()
+            self.core_copy(layer, k, True).wait_recv()
 
     def end(self, layers):
         for k in range(3):
@@ -209,6 +235,7 @@
             for k in range(4):
                 self.y_copy(layer, k).wait_send()
             for k in range(8):
+                self.x_copy(layer, k).wait_send()
                 self.core_copy(layer, k).wait_send()
             return 0
 
@@ -240,25 +267,36 @@
         stats_ref[...] = jnp.zeros_like(stats_ref)
         gather.kick(0)
         gather.share_gains()
-        for step in range(1, 4):
-            gather.serve(0, step)
+        gather.serve_z(0, 1)
+        gather.serve_z(0, 2)
+        gather.serve_x(0, 0)
+        gather.serve_x(0, 1)
+        gather.serve_z(0, 3)
         gather.kick(1)
-        for step in range(4, 8):
-            gather.serve(0, step)
         gather.wait_gains()
+        gather.serve_y(0, 0)
+        gather.serve_x(0, 2)
+        gather.serve_y(0, 1)
+        gather.serve_y(0, 2)
+        gather.serve_x(0, 3)
+        gather.serve_y(0, 3)
+        for k in range(4, 8):
+            gather.serve_x(0, k)
 
     gather.finish(layer)
     keep_copy(layer).start()
     more = layer + 1 < layers
 
-    def serve(step):
-        @pl.when(more)
+    def serve(here, *steps):
+        @pl.when(more & here)
         def _():
-            gather.serve(layer + 1, step)
-        if step == 3:
-            @pl.when(layer + 2 < layers)
-            def _():
-                gather.kick(layer + 2)
+            for kind, k in steps:
+                getattr(gather, kind)(layer + 1, k)
+
+    def kick(here):
+        @pl.when((layer + 2 < layers) & here)
+        def _():
+            gather.kick(layer + 2)
 
     def stream_of(at):
         prev = sent_ref[layer, at].astype(F32)
@@ -299,10 +337,11 @@
             probs = (expd * (1.0 / jnp.sum(expd, axis=-1, keepdims=True))).astype(BF16)
             probs_ref[0, h, at] = probs
             hold_ref[h, at] = dot_nn(probs, values).astype(BF16)
-        for step, after in ((1, 1), (2, 4), (3, 7)):
-            @pl.when(h == after)
-            def _():
-                serve(step)
+        serve(h == 1, ("serve_z", 1), ("serve_z", 2))
+        serve(h == 3, ("serve_z", 3), ("serve_x", 0))
+        kick(h == 3)
+        serve(h == 5, ("serve_x", 1), ("serve_y", 0))
+        serve(h == 7, ("serve_x", 2), ("serve_y", 1))
         return 0
 
     lax.fori_loop(0, HEADS, head_step, 0)
@@ -334,15 +373,11 @@
         for k, value in enumerate((stream, branch_attn, branch_ffn)):
             stats_ref[layer, k : k + 1] += jnp.sum(valid * value * value, axis=0, keepdims=True)
 
-        @pl.when(i == 0)
-        def _():
-            serve(4)
-
+        serve(i == 0, ("serve_x", 3), ("serve_y", 2), ("serve_y", 3), ("serve_x", 4))
         return 0
 
     lax.fori_loop(0, chunks, ffn_step, 0)
-    for step in range(5, 8):
-        serve(step)
+    serve(True, ("serve_x", 5), ("serve_x", 6), ("serve_x", 7))
 
     @pl.when(layer == layers - 1)
     def _():
@@ -384,45 +419,45 @@
             keep_copy(k).wait()
 
 
-class Scatter:
+class Scatter(Slabs):
     def __init__(self, refs, sems):
-        self.grads, self.core_in, self.y_in, self.z_in, self.last_out, self.last_in = refs
-        self.core_sems, self.y_sems, self.z_sems, self.last_sems = sems
-        self.section, self.group, self.core, self.y, self.z_peers = mesh_place()
-        self.x = self.section // 2
-        self.quads = self.grads.shape[3] // 2
-        self.mine = pl.ds(self.core * self.quads, self.quads)
-        self.theirs = pl.ds((1 - self.core) * self.quads, self.quads)
+        self.grads, self.core_in, self.x_in, self.y_in, self.z_in, self.last_out, self.last_in = refs
+        super().__init__(self.grads.shape[3])
+        self.core_sems, self.x_sems, self.y_sems, self.z_sems, self.last_sems = sems
+        self.mine = self.slab_of(self.x, self.core)
 
     def core_copy(self, layer, late):
         slot = lax.rem(layer, 2)
         zs = pl.ds(0, 1) if late else pl.ds(1, 3)
         return remote(
-            self.grads.at[slot, zs, :, self.theirs], self.core_in.at[slot, zs],
-            self.core_sems.at[0, slot, int(late)], self.core_sems.at[1, slot, int(late)],
-            self.section + 1 - 2 * self.core, self.group,
+            self.grads.at[slot, zs, :, self.half_of(1 - self.core)], self.core_in.at[slot, zs],
+            self.core_sems.at[0, slot, int(late)], self.core_sems.at[1, slot, int(late)], *self.core_peer(),
+        )
+
+    def x_copy(self, layer, k):
+        slot = lax.rem(layer, 2)
+        return remote(
+            self.grads.at[slot, self.z_peers[k], :, self.edge_of(1 - self.x, self.core)], self.x_in.at[slot, k],
+            self.x_sems.at[0, slot, k], self.x_sems.at[1, slot, k], *self.x_peer(),
         )
 
     def y_copy(self, layer, k):
         slot = lax.rem(layer, 2)
         return remote(
             self.grads.at[slot, self.z_peers[k], 1 - self.y, self.mine], self.y_in.at[slot, k],
-            self.y_sems.at[0, slot, k], self.y_sems.at[1, slot, k],
-            self.section, self.group + 1 - 2 * self.y,
+            self.y_sems.at[0, slot, k], self.y_sems.at[1, slot, k], *self.y_peer(),
         )
 
     def z_copy(self, layer, k):
         slot = lax.rem(layer, 2)
         return remote(
             self.grads.at[slot, self.z_peers[k], self.y, self.mine], self.z_in.at[layer, k - 1],
-            self.z_sems.at[0, layer, k - 1], self.z_sems.at[1, layer, k - 1],
-            self.section, self.z_peers[k] * 2 + self.y,
+            self.z_sems.at[0, layer, k - 1], self.z_sems.at[1, layer, k - 1], *self.z_peer(k),
         )
 
     def last_copy(self, layer):
         slot = lax.rem(layer, 2)
-        place = lax.rem(self.section - layer + 4, 4) - 1
-        place = jnp.maximum(place, 0)
+        place = jnp.maximum(lax.rem(self.section - layer + 4, 4) - 1, 0)
         return remote(
             self.last_out.at[slot], self.last_in.at[place],
             self.last_sems.at[0, slot], self.last_sems.at[1, place], layer, self.group,
@@ -443,58 +478,60 @@
     def add_core(self, layer, late):
         slot = lax.rem(layer, 2)
         self.core_copy(layer, late).wait_recv()
+        rows = self.half_of(self.core)
 
         def add(i, _):
             z, y = i // 2, lax.rem(i, 2)
-            for q in range(self.quads):
-                at = self.core * self.quads + q
-                self.grads[slot, z, y, at] = self.grads[slot, z, y, at] + self.core_in[slot, z, y, q]
+            self.grads[slot, z, y, rows] = self.grads[slot, z, y, rows] + self.core_in[slot, z, y]
             return 0
 
         lax.fori_loop(0 if late else 2, 2 if late else 8, add, 0)
-        self.for_part(late, lambda k: self.y_copy(layer, k).start())
-
-    def add_y(self, layer, k):
-        slot = lax.rem(layer, 2)
-        self.y_copy(layer, k).wait_recv()
-        for q in range(self.quads):
-            at = self.core * self.quads + q
-            z = self.z_peers[k]
-            self.grads[slot, z, self.y, at] = self.grads[slot, z, self.y, at] + self.y_in[slot, k, q]
-        if k:
-            self.z_copy(layer, k).start()
-
-    def add_y_if(self, layer, k, late):
+        self.for_part(late, lambda k: self.x_copy(layer, k).start())
+
+    def add_x(self, layer, k, late):
         @pl.when((self.z_peers[k] == 0) == late)
         def _():
-            self.add_y(layer, k)
+            slot = lax.rem(layer, 2)
+            self.x_copy(layer, k).wait_recv()
+            rows = self.edge_of(self.x, self.core)
+            z = self.z_peers[k]
+            for y in range(2):
+                self.grads[slot, z, y, rows] = self.grads[slot, z, y, rows] + self.x_in[slot, k, y]
+            self.y_copy(layer, k).start()
+
+    def add_y(self, layer, k, late):
+        @pl.when((self.z_peers[k] == 0) == late)
+        def _():
+            slot = lax.rem(layer, 2)
+            self.y_copy(layer, k).wait_recv()
+            z = self.z_peers[k]
+            self.grads[slot, z, self.y, self.mine] = self.grads[slot, z, self.y, self.mine] + self.y_in[slot, k]
+            if k:
+                self.z_copy(layer, k).start()
 
     def add_z(self, layer, result_ref):
         slot = lax.rem(layer, 2)
         for k in range(1, 4):
             self.z_copy(layer, k).wait_recv()
-        for q in range(self.quads):
-            at = self.core * self.quads + q
-            total = self.grads[slot, self.z_peers[0], self.y, at].astype(F32)
-            for k in range(3):
-                total = total + self.z_in[layer, k, q].astype(F32)
-
-            @pl.when(layer == self.section)
-            def _():
-                result_ref[at] = total
-
-            @pl.when(layer != self.section)
-            def _():
-                self.last_out[slot, q] = total.astype(BF16)
+        total = self.grads[slot, self.z_peers[0], self.y, self.mine].astype(F32)
+        for k in range(3):
+            total = total + self.z_in[layer, k].astype(F32)
+
+        @pl.when(layer == self.section)
+        def _():
+            result_ref[...] = jnp.zeros_like(result_ref)
+            result_ref[self.mine] = total
 
         @pl.when(layer != self.section)
         def _():
+            self.last_out[slot] = total.astype(BF16)
             self.last_copy(layer).start()
 
     def wait_sends(self, layer):
         for late in (False, True):
             self.core_copy(layer, late).wait_send()
         for k in range(4):
+            self.x_copy(layer, k).wait_send()
             self.y_copy(layer, k).wait_send()
         for k in range(1, 4):
             self.z_copy(layer, k).wait_send()
@@ -504,13 +541,11 @@
             self.last_copy(layer).wait_send()
 
     def collect(self, result_ref):
-        for place in range(3):
+        for place in (0, 2, 1):
             self.last_landed(place).wait_recv()
-        for q in range(self.quads):
-            mine = self.core * self.quads + q
-            theirs = (1 - self.core) * self.quads + q
-            result_ref[mine] = result_ref[mine] + self.last_in[1, q].astype(F32)
-            result_ref[theirs] = self.last_in[0, q].astype(F32) + self.last_in[2, q].astype(F32)
+            peer = lax.rem(self.section + place + 1, 4)
+            rows = self.slab_of(peer // 2, lax.rem(peer, 2))
+            result_ref[rows] = result_ref[rows] + self.last_in[place].astype(F32)
 
 
 class Totals:
@@ -641,18 +676,14 @@
     chunks = seg // rows
     gain_one = gain_ref[0, 0:1]
     gain_two = gain_ref[0, 1:2]
-    scatter = Scatter(comm_refs[:6], comm_refs[10:14])
-    totals = Totals(comm_refs[6:10], comm_refs[14:])
+    scatter = Scatter(comm_refs[:7], comm_refs[11:16])
+    totals = Totals(comm_refs[7:11], comm_refs[16:])
     grads_ref = comm_refs[0]
     slot = lax.rem(layer, 2)
 
     @pl.when(layer == layers - 1)
     def _():
-        section, group = scatter.section, scatter.group
-        greet(
-            [(lax.rem(section + k, 4), group) for k in range(1, 4)]
-            + [(section, lax.rem(group + k, 8)) for k in range(1, 8)]
-        )
+        scatter.greet_all()
         sends_ref[...] = jnp.zeros_like(sends_ref)
         gain_grad_ref[...] = jnp.zeros_like(gain_grad_ref)
 
@@ -660,9 +691,8 @@
         for r in range(4):
             quad = first + step * r
             owner = quad // 6
-            grads_ref[slot, owner // 2, lax.rem(owner, 2), lax.rem(quad, 6)] = value[
-                r * part : (r + 1) * part
-            ].astype(BF16)
+            at = pl.ds(pl.multiple_of(lax.rem(quad, 6) * part, part), part)
+            grads_ref[slot, owner // 2, lax.rem(owner, 2), at] = value[r * part : (r + 1) * part].astype(BF16)
 
     def before(act):
         @pl.when(layer < layers - 1)
@@ -698,11 +728,12 @@
         @pl.when(i == 0)
         def _():
             before(lambda at: scatter.add_core(at, True))
-            before(lambda at: scatter.add_y_if(at, 2, False))
+            before(lambda at: scatter.add_x(at, 3, False))
 
         @pl.when(i == 1)
         def _():
-            before(lambda at: scatter.add_y_if(at, 3, False))
+            before(lambda at: scatter.add_x(at, 0, False))
+            before(lambda at: scatter.add_y(at, 1, False))
 
         return 0
 
@@ -720,8 +751,13 @@
     lax.fori_loop(0, 4, ffn_grad_step, 0)
     put_grad(12, 1, dot_tn(att_ref[0], datt_ref[...]))
     scatter.core_copy(layer, False).start()
-    before(lambda at: scatter.add_y_if(at, 0, False))
-    before(lambda at: scatter.for_part(True, lambda k: scatter.add_y(at, k)))
+
+    @pl.when(layer < layers - 1)
+    def _():
+        for k in range(4):
+            scatter.add_x(layer + 1, k, True)
+        for k in (2, 3, 0):
+            scatter.add_y(layer + 1, k, False)
 
     def head_step(h, _):
         queries = heads_ref[0, h]
@@ -747,6 +783,15 @@
         def _():
             scatter.add_core(layer, False)
 
+        @pl.when(h == 5)
+        def _():
+            for k in range(4):
+                before(lambda at: scatter.add_y(at, k, True))
+
+        @pl.when(h == 7)
+        def _():
+            scatter.add_x(layer, 1, False)
+
         return 0
 
     lax.fori_loop(0, HEADS, head_step, 0)
@@ -776,7 +821,7 @@
     lax.fori_loop(0, 3, qkv_grad_step, 0)
     scatter.core_copy(layer, True).start()
     before(lambda at: scatter.add_z(at, result_ref))
-    scatter.add_y_if(layer, 1, False)
+    scatter.add_x(layer, 2, False)
 
     @pl.when(layer == 0)
     def _():
@@ -791,18 +836,24 @@
         rows_out.append(jnp.zeros((16 - 3 * layers, width), F32))
         totals.begin(jnp.concatenate(rows_out, axis=0))
         scatter.add_core(0, True)
-        scatter.add_y_if(0, 2, False)
+        scatter.add_y(0, 1, False)
+        scatter.add_x(0, 3, False)
         totals.after_core()
-        scatter.add_y_if(0, 3, False)
-        scatter.add_y_if(0, 0, False)
-        scatter.for_part(True, lambda k: scatter.add_y(0, k))
+        scatter.add_x(0, 0, False)
+        scatter.add_y(0, 2, False)
+        for k in range(4):
+            scatter.add_x(0, k, True)
+        scatter.add_y(0, 3, False)
+        scatter.add_y(0, 0, False)
+        for k in range(4):
+            scatter.add_y(0, k, True)
         totals.after_y()
         scatter.add_z(0, result_ref)
         totals.after_z()
         scatter.collect(result_ref)
         square = jnp.zeros((8, width), F32)
         for q in range(6):
-            value = result_ref[q]
+            value = result_ref[q * part : (q + 1) * part]
             square = square + jnp.sum((value * value).reshape(part // 8, 8, width), axis=0)
         folded = square[:, :128] + square[:, 128:256] + square[:, 256:]
         square_ref[...] = totals.norm(folded)
@@ -1260,17 +1311,18 @@
             jax.ShapeDtypeStruct((layers, seg, width), BF16),
             jax.ShapeDtypeStruct((seg, width), F32),
             jax.ShapeDtypeStruct((layers, 8, width), F32),
-            jax.ShapeDtypeStruct((layers, 48, part, width), BF16),
+            jax.ShapeDtypeStruct((layers, 48 * part, width), BF16),
             jax.ShapeDtypeStruct((layers, 8, 8, 128), F32),
         ],
         scratch_shapes=[
             pltpu.VMEM((HEADS, seg, dim), BF16),
             pltpu.VMEM((seg, width), F32),
-            pltpu.VMEM((layers, 48, part, width), BF16),
+            pltpu.VMEM((layers, 48 * part, width), BF16),
             pltpu.VMEM((layers, 8, 8, 128), F32),
             pltpu.SemaphoreType.DMA((2, 3)),
             pltpu.SemaphoreType.DMA((2, layers, 4)),
             pltpu.SemaphoreType.DMA((2, layers, 4)),
+            pltpu.SemaphoreType.DMA((2, layers, 8)),
             pltpu.SemaphoreType.DMA((2, layers, 8)),
             pltpu.SemaphoreType.DMA((2, 10)),
             pltpu.SemaphoreType.DMA((layers,)),
@@ -1304,7 +1356,7 @@
         + [pl.BlockSpec(memory_space=pltpu.VMEM)],
         out_specs=[pl.BlockSpec(memory_space=pltpu.VMEM)] * 3,
         out_shape=[
-            jax.ShapeDtypeStruct((6, part, width), F32),
+            jax.ShapeDtypeStruct((6 * part, width), F32),
             jax.ShapeDtypeStruct((16, width), F32),
             jax.ShapeDtypeStruct((8, 128), F32),
         ],
@@ -1319,17 +1371,19 @@
             pltpu.VMEM((3 * HEADS, seg, dim), BF16),
             pltpu.VMEM((3, seg, width), BF16),
             pltpu.VMEM((layers, 8, width), F32),
-            pltpu.VMEM((2, 4, 2, 6, part, width), BF16),
-            pltpu.VMEM((2, 4, 2, 3, part, width), BF16),
-            pltpu.VMEM((2, 4, 3, part, width), BF16),
-            pltpu.VMEM((layers, 3, 3, part, width), BF16),
-            pltpu.VMEM((2, 3, part, width), BF16),
-            pltpu.VMEM((3, 3, part, width), BF16),
+            pltpu.VMEM((2, 4, 2, 576, width), BF16),
+            pltpu.VMEM((2, 4, 2, 288, width), BF16),
+            pltpu.VMEM((2, 4, 2, 80, width), BF16),
+            pltpu.VMEM((2, 4, 208, width), BF16),
+            pltpu.VMEM((layers, 3, 208, width), BF16),
+            pltpu.VMEM((2, 208, width), BF16),
+            pltpu.VMEM((3, 208, width), BF16),
             pltpu.VMEM((6, 16, width), F32),
             pltpu.VMEM((4, 16, width), F32),
             pltpu.VMEM((4, 8, 128), F32),
             pltpu.VMEM((8, 8, 128), F32),
             pltpu.SemaphoreType.DMA((2, 2, 2)),
+            pltpu.SemaphoreType.DMA((2, 2, 4)),
             pltpu.SemaphoreType.DMA((2, 2, 4)),
             pltpu.SemaphoreType.DMA((2, layers, 3)),
             pltpu.SemaphoreType.DMA((2, 3)),
@@ -1476,7 +1530,7 @@
     own_gain = norm_gains.shape[2]
     own_w = (
         w_master[0].astype(BF16).reshape(own_blocks // 4, 4, part, part).transpose(0, 2, 1, 3)
-        .reshape(own_blocks // 4, part, width)
+        .reshape(own_blocks // 4 * part, width)
     )
     gain_tile = jnp.zeros((8, 128), F32).at[:2, :own_gain].set(norm_gains[0])
     slot = jnp.minimum(section_idx, micro - 1)
@@ -1498,7 +1552,7 @@
     clip_limit = 0.00015 * math.sqrt(layers * (own_blocks * groups * part * part + 2 * width))
     flats = [flat_rows(a[0]) for a in (w_master, l_stats, r_stats, l_roots, r_roots)]
     *news, gains_new, m_new, v_new, norms = update(
-        layers, clip_limit, step_count, squares, tile, own_quads, flats,
+        layers, clip_limit, step_count, squares, tile, own_quads.reshape(-1, part, width), flats,
         (norm_gains[0], gain_m[0], gain_v[0]),
     )
     w_new, grad_blocks, l_new, r_new = (from_flat_rows(a, own_blocks) for a in news)

time: 317 us -> 302 us (0.953)
  Pallas kernels: 296 us -> 282 us
    pallas_call x1, Pallas kernels: 135 us -> 126 us  [forward(): pl.pallas_call(functools.partial(forward_kernel, layers, half), grid=(lay...]
    pallas_call x1, Pallas kernels: 150 us -> 144 us  [backward(): pl.pallas_call(functools.partial(backward_kernel, layers, half), grid=(la...]
where the time goes in v5:
time: 302 us
  Pallas kernels  282 us (93%)
  local copies, waits for them, and re-layouts  11.4 us (4%)
  between operations  4.51 us (1%)
  other arithmetic  4.24 us (1%)
    pallas_call x1, Pallas kernels, backward(): pl.pallas_call(functools.partial(backward_kernel, layers, half), grid=(la...  144 us
    pallas_call x1, Pallas kernels, forward(): pl.pallas_call(functools.partial(forward_kernel, layers, half), grid=(lay...  126 us
    pallas_call x1, Pallas kernels, update(): pl.pallas_call(functools.partial(update_kernel, layers, limit), grid=(3,)...  11.1 us

profile of v5, /device:TPU:2, one launch (start us, length us, event | category | flops | bytes accessed | tf_op | source)
XLA Modules:
  0.0 301.8 jit_solution(513337123397236601)
XLA Ops:
  0.6 0.0 copy-start
  0.7 0.0 copy-start.2
  0.7 1.4 dynamic_slice.15
  2.7 0.9 multiply_reduce_fusion
  3.6 0.6 pad_add_fusion.info_ref
  4.2 1.0 constant_dynamic-slice_fusion.1
  5.2 1.0 copy.26.target_ref
  6.2 0.0 copy-done
  6.2 0.8 constant_dynamic-slice_fusion.2.x_ref
  7.0 1.3 reduce_sum.9
  9.0 1.3 scatter.4.own_gain_ref
  10.3 0.0 copy-done.2
  10.3 0.6 convert_element_type.26
  10.9 0.3 copy.28
  11.2 1.2 reshape.96.own_ref
  12.4 126.3 %shard_map.204 = (bf16[4,8,512,512]{3,2,1,0:T(8,128)(2,1)}, bf16[4,24,512,48]{3,2,1,0:T(8,128)(2,1)}, bf16[4,512,384]{2,1,0:T(8,128)(2,1)}, f32[4,512,384]{2,1,0...) custom-call(s32[5]{0:T(128)} %pad_add_fusion.info_ref, ...), custom_call_target="tpu_custom_call" | custom-call | tf_op jit(solution)/shard_map/pallas_call | solution.py:1295
  138.7 0.9 convert_bitcast_fusion
  139.7 0.7 reshape.108.gain_ref
  140.3 0.0 copy-start.1
  140.4 144.3 %shard_map.205 = (f32[576,384]{1,0:T(8,128)}, f32[16,384]{1,0:T(8,128)}, f32[8,128]{1,0:T(8,128)}) custom-call(f32[512,384]{1,0:T(8,128)} %get-tuple-element.44.loss_grad_ref, bf16[4,4608,384]{2,1,0:T(8,128)(2,1)} %get-tuple-element.45.w_ref, f32[4,2,384]{2,1,0:T(2,128)} %reshape.108.gain_ref, bf16[4,512,384]{2,1,0:T(8,128)(2,1)} %get-tuple-element.47.sent_ref, ...), custom_call_target="tpu_custom_call" | custom-call | tf_op jit(solution)/shard_map/pallas_call | solution.py:1346
  285.3 11.1 %shard_map.206 = (f32[1728,128]{1,0:T(8,128)}, f32[1728,128]{1,0:T(8,128)}, f32[1728,128]{1,0:T(8,128)}, f32[1728,128]{1,0:T(8,128)}, f32[2,48]{1,0:T(2,128)}, /...) custom-call(s32[1]{0:T(128)S(6)} %copy.29.step_ref, f32[8,128]{1,0:T(8,128)} %get-tuple-element.55.square_ref, ...), custom_call_target="tpu_custom_call" | custom-call | tf_op jit(solution)/shard_map/pallas_call | solution.py:1504
  296.3 1.2 slice.36
  297.5 0.7 slice.37
  298.2 0.5 fusion.1
  298.7 1.2 slice.35
  300.6 0.0 copy-done.1
  (2 shorter events, 0.0 us)
Async XLA Ops:
  0.6 5.6 %copy-start = (bf16[2048,384]{1,0:T(8,128)(2,1)S(1)}, bf16[2048,384]{1,0:T(8,128)(2,1)}, u32[]{:S(2)}) copy-start(bf16[2048,384]{1,0:T(8,128)(2,1)} %param.15) | copy-start | bytes 4718596
  0.7 9.6 %copy-start.2 = (f32[1,24,9216]{2,1,0:T(8,128)S(1)}, f32[1,24,9216]{2,1,0:T(8,128)}, u32[]{:S(2)}) copy-start(f32[1,24,9216]{2,1,0:T(8,128)} %param.19) | copy-start | bytes 2654212
  140.3 160.3 %copy-start.1 = (bf16[2048,384]{1,0:T(8,128)(2,1)S(1)}, bf16[2048,384]{1,0:T(8,128)(2,1)}, u32[]{:S(2)}) copy-start(bf16[2048,384]{1,0:T(8,128)(2,1)} %param.15) | copy-start | bytes 4718596

commit v6 on v5

--- a/solution.py
+++ b/solution.py
@@ -52,6 +52,35 @@
     )
 
 
+def flat_rows(array):
+    blocks, area = array.shape
+    return (
+        array.reshape(blocks // 8, 8, area // 128, 128).transpose(0, 2, 1, 3).reshape(-1, 128)
+    )
+
+
+def from_flat_rows(rows, blocks):
+    return (
+        rows.reshape(blocks // 8, -1, 8, 128).transpose(0, 2, 1, 3).reshape(blocks, -1)
+    )
+
+
+def load_block(rows_ref, base, block_ref):
+    lane = lax.broadcasted_iota(jnp.int32, (24, 128), 1)
+    a, b, c = (rows_ref[pl.ds(base + 8 * m, 24, stride=24), :] for m in range(3))
+    block_ref[pl.ds(0, 24, stride=4), :] = a
+    block_ref[pl.ds(1, 24, stride=4), :] = jnp.where(lane < 32, pltpu.roll(a, 32, 1), pltpu.roll(b, 32, 1))
+    block_ref[pl.ds(2, 24, stride=4), :] = jnp.where(lane < 64, pltpu.roll(b, 64, 1), pltpu.roll(c, 64, 1))
+    block_ref[pl.ds(3, 24, stride=4), :] = pltpu.roll(c, 96, 1)
+
+
+def flat_parts(block_ref):
+    lane = lax.broadcasted_iota(jnp.int32, (24, 128), 1)
+    a, b, c, d = (block_ref[pl.ds(r, 24, stride=4), :] for r in range(4))
+    b, c, d = pltpu.roll(b, 96, 1), pltpu.roll(c, 64, 1), pltpu.roll(d, 32, 1)
+    return jnp.where(lane < 96, a, b), jnp.where(lane < 64, b, c), jnp.where(lane < 32, c, d)
+
+
 MESH = pl.DeviceIdType.MESH
 
 
@@ -180,7 +209,6 @@
         return remote(ref, ref, self.gain_sems.at[0, k], self.gain_sems.at[1, k], self.section, self.group)
 
     def begin(self):
-        self.greet_all()
         for k in range(3):
             self.spread_copy(k).start()
         for k in range(7):
@@ -242,10 +270,21 @@
         lax.fori_loop(0, layers, per_layer, 0)
 
 
+def segment_info(micro, length_ref, stems_ref):
+    section, group = lax.axis_index("section"), lax.axis_index("dp")
+    at = group * micro + jnp.minimum(section, micro - 1)
+    used = (section < micro).astype(jnp.int32)
+    frames = length_ref[0]
+    for k in range(1, length_ref.shape[0]):
+        frames = frames + length_ref[k]
+    return length_ref[at] * used, [stems_ref[at, k] * used for k in range(4)], frames
+
+
 def forward_kernel(
-    layers, half, info_ref, scale_ref, x_ref, target_ref, own_ref, own_gain_ref,
+    layers, half, micro, length_ref, stems_ref, x_ref, target_ref, flat_ref, raw_gain_ref,
     probs_ref, heads_ref, att_ref, middle_ref, hidden_ref, slope_ref, sent_ref, loss_grad_ref, stats_ref,
-    full_ref, gains_out_ref, hold_ref, out_ref, w_all_ref, gains_ref, *sems,
+    full_ref, gains_out_ref,
+    hold_ref, out_ref, w_all_ref, gains_ref, own_ref, own_gain_ref, block_ref, *sems,
 ):
     seg, width = x_ref.shape
     dim = width // HEADS
@@ -253,15 +292,27 @@
     layer = pl.program_id(0)
     rows = 256
     chunks = seg // rows
-    length = info_ref[0]
+    length, present_flags, frame_total = segment_info(micro, length_ref, stems_ref)
     gather = Gather(own_ref, own_gain_ref, w_all_ref, gains_ref, sems)
     w_ref = w_all_ref.at[pl.ds(layer, 1)]
 
+    def own_step(q, _):
+        for c in range(4):
+            block = 4 * q + c
+            load_block(flat_ref, (block // 8) * 576 + lax.rem(block, 8), block_ref.at[c])
+        quad = jnp.concatenate([block_ref[c, :, :part] for c in range(4)], axis=1)
+        own_ref[pl.ds(pl.multiple_of(q * part, part), part)] = quad.astype(BF16)
+        return 0
+
     def keep_copy(index):
         return pltpu.make_async_copy(w_all_ref.at[index], full_ref.at[index], gather.local.at[index])
 
     @pl.when(layer == 0)
     def _():
+        gather.greet_all()
+        lax.fori_loop(0, flat_ref.shape[0] // 288, own_step, 0)
+        own_gain_ref[...] = jnp.zeros_like(own_gain_ref)
+        own_gain_ref[:2, : raw_gain_ref.shape[1]] = raw_gain_ref[...]
         gather.begin()
         sent_ref[0] = x_ref[...]
         stats_ref[...] = jnp.zeros_like(stats_ref)
@@ -282,6 +333,8 @@
         gather.serve_y(0, 3)
         for k in range(4, 8):
             gather.serve_x(0, k)
+        gather.serve_z(1, 1)
+        gather.serve_z(1, 2)
 
     gather.finish(layer)
     keep_copy(layer).start()
@@ -293,10 +346,11 @@
             for kind, k in steps:
                 getattr(gather, kind)(layer + 1, k)
 
-    def kick(here):
+    def ahead(here, *steps):
         @pl.when((layer + 2 < layers) & here)
         def _():
-            gather.kick(layer + 2)
+            for kind, *k in steps:
+                getattr(gather, kind)(layer + 2, *k)
 
     def stream_of(at):
         prev = sent_ref[layer, at].astype(F32)
@@ -310,6 +364,8 @@
 
     gain_one = gain_row(0)
     gain_two = gain_row(1)
+    gains_out_ref[layer, 0:1] = gain_one
+    gains_out_ref[layer, 1:2] = gain_two
 
     def qkv_step(i, _):
         at = pl.ds(pl.multiple_of(i * rows, rows), rows)
@@ -326,25 +382,23 @@
     frames = lax.broadcasted_iota(jnp.int32, (1, seg), 1)
     masking = jnp.where(frames < length, 0.0, -1e30).astype(F32)
 
-    def head_step(h, _):
+    def head_step(h):
         keys = heads_ref[0, HEADS + h]
         values = heads_ref[0, 2 * HEADS + h]
-        for i in range(chunks):
-            at = pl.ds(i * rows, rows)
-            scores = dot_nt(heads_ref[0, h, at], keys) * dim ** (-0.5) + masking
-            top = jnp.max(scores, axis=-1, keepdims=True)
-            expd = jnp.exp(scores - top)
-            probs = (expd * (1.0 / jnp.sum(expd, axis=-1, keepdims=True))).astype(BF16)
-            probs_ref[0, h, at] = probs
-            hold_ref[h, at] = dot_nn(probs, values).astype(BF16)
-        serve(h == 1, ("serve_z", 1), ("serve_z", 2))
-        serve(h == 3, ("serve_z", 3), ("serve_x", 0))
-        kick(h == 3)
-        serve(h == 5, ("serve_x", 1), ("serve_y", 0))
-        serve(h == 7, ("serve_x", 2), ("serve_y", 1))
-        return 0
-
-    lax.fori_loop(0, HEADS, head_step, 0)
+        scores = dot_nt(heads_ref[0, h], keys) * dim ** (-0.5) + masking
+        top = jnp.max(scores, axis=-1, keepdims=True)
+        expd = jnp.exp(scores - top)
+        probs = (expd * (1.0 / jnp.sum(expd, axis=-1, keepdims=True))).astype(BF16)
+        probs_ref[0, h] = probs
+        hold_ref[h] = dot_nn(probs, values).astype(BF16)
+
+    for h in range(HEADS // 2):
+        head_step(h)
+    serve(True, ("serve_z", 3), ("serve_x", 0), ("serve_x", 1))
+    ahead(True, ("kick",))
+    for h in range(HEADS // 2, HEADS):
+        head_step(h)
+    serve(True, ("serve_y", 0), ("serve_x", 2), ("serve_y", 1))
 
     def ffn_step(i, _):
         at = pl.ds(pl.multiple_of(i * rows, rows), rows)
@@ -373,11 +427,13 @@
         for k, value in enumerate((stream, branch_attn, branch_ffn)):
             stats_ref[layer, k : k + 1] += jnp.sum(valid * value * value, axis=0, keepdims=True)
 
-        serve(i == 0, ("serve_x", 3), ("serve_y", 2), ("serve_y", 3), ("serve_x", 4))
+        ahead(i == 0, ("serve_z", 1))
+        serve(i == 0, ("serve_x", 3), ("serve_x", 4), ("serve_y", 2))
         return 0
 
     lax.fori_loop(0, chunks, ffn_step, 0)
-    serve(True, ("serve_x", 5), ("serve_x", 6), ("serve_x", 7))
+    ahead(True, ("serve_z", 2))
+    serve(True, ("serve_y", 3), ("serve_x", 5), ("serve_x", 6), ("serve_x", 7))
 
     @pl.when(layer == layers - 1)
     def _():
@@ -387,8 +443,8 @@
         stem = lane // (2 * bins)
         present = jnp.zeros((1, width), F32)
         for k in range(4):
-            present = jnp.where(stem == k, info_ref[1 + k].astype(F32), present)
-        inverse = scale_ref[0]
+            present = jnp.where(stem == k, present_flags[k].astype(F32), present)
+        inverse = 1.0 / jnp.full((1, 1), frame_total, jnp.int32).astype(F32)
 
         def loss_step(i, _):
             at = pl.ds(pl.multiple_of(i * rows, rows), rows)
@@ -398,7 +454,7 @@
                 is_real, pltpu.roll(square, width - bins, 1), pltpu.roll(square, bins, 1)
             )
             magnitude = jnp.sqrt(square + other + 0.01)
-            goal = target_ref[at]
+            goal = target_ref[:, at].T
             goal = jnp.concatenate(
                 [goal[:, (k // 2) * bins : (k // 2 + 1) * bins] for k in range(8)], axis=1
             )
@@ -413,7 +469,6 @@
             return 0
 
         lax.fori_loop(0, chunks, loss_step, 0)
-        gains_out_ref[...] = gains_ref[...]
         gather.end(layers)
         for k in range(layers):
             keep_copy(k).wait()
@@ -748,7 +803,8 @@
         put_grad(16 + c, 4, dot_tn(normed_ref[...], dpre_ref[c]))
         return 0
 
-    lax.fori_loop(0, 4, ffn_grad_step, 0)
+    for c in range(4):
+        ffn_grad_step(c, 0)
     put_grad(12, 1, dot_tn(att_ref[0], datt_ref[...]))
     scatter.core_copy(layer, False).start()
 
@@ -759,42 +815,30 @@
         for k in (2, 3, 0):
             scatter.add_y(layer + 1, k, False)
 
-    def head_step(h, _):
+    def head_step(h):
         queries = heads_ref[0, h]
         keys = heads_ref[0, HEADS + h]
-        values = heads_ref[0, 2 * HEADS + h]
-        dkeys = jnp.zeros((seg, dim), F32)
-        dvalues = jnp.zeros((seg, dim), F32)
-        for i in range(chunks):
-            at = pl.ds(i * rows, rows)
-            probs = probs_ref[0, h, at]
-            dhold = dhold_ref[h, at]
-            dprobs = dot_nt(dhold, values)
-            wide = probs.astype(F32)
-            dot_sum = jnp.sum(wide * dprobs, axis=-1, keepdims=True)
-            dscores = (wide * (dprobs - dot_sum)).astype(BF16)
-            dheads_ref[h, at] = (dot_nn(dscores, keys) * dim ** (-0.5)).astype(BF16)
-            dvalues = dvalues + dot_tn(probs, dhold)
-            dkeys = dkeys + dot_tn(dscores, heads_ref[0, h, at])
-        dheads_ref[HEADS + h] = (dkeys * dim ** (-0.5)).astype(BF16)
-        dheads_ref[2 * HEADS + h] = dvalues.astype(BF16)
-
-        @pl.when(h == 3)
-        def _():
-            scatter.add_core(layer, False)
-
-        @pl.when(h == 5)
-        def _():
-            for k in range(4):
-                before(lambda at: scatter.add_y(at, k, True))
-
-        @pl.when(h == 7)
-        def _():
-            scatter.add_x(layer, 1, False)
-
-        return 0
-
-    lax.fori_loop(0, HEADS, head_step, 0)
+        probs = probs_ref[0, h]
+        dhold = dhold_ref[h]
+        dprobs = dot_nt(dhold, heads_ref[0, 2 * HEADS + h])
+        wide = probs.astype(F32)
+        dot_sum = jnp.sum(wide * dprobs, axis=-1, keepdims=True)
+        dscores = (wide * (dprobs - dot_sum)).astype(BF16)
+        dheads_ref[h] = (dot_nn(dscores, keys) * dim ** (-0.5)).astype(BF16)
+        dheads_ref[HEADS + h] = (dot_tn(dscores, queries) * dim ** (-0.5)).astype(BF16)
+        dheads_ref[2 * HEADS + h] = dot_tn(probs, dhold).astype(BF16)
+
+    for h in range(HEADS // 2):
+        head_step(h)
+
+    @pl.when(layer < layers - 1)
+    def _():
+        for k in range(4):
+            scatter.add_y(layer + 1, k, True)
+
+    for h in range(HEADS // 2, HEADS):
+        head_step(h)
+    scatter.add_core(layer, False)
 
     def qkv_step(i, _):
         at = pl.ds(pl.multiple_of(i * rows, rows), rows)
@@ -818,9 +862,11 @@
         put_grad(t, 3, dot_tn(normed_ref[...], dqkv_ref[t]))
         return 0
 
-    lax.fori_loop(0, 3, qkv_grad_step, 0)
+    for t in range(3):
+        qkv_grad_step(t, 0)
     scatter.core_copy(layer, True).start()
     before(lambda at: scatter.add_z(at, result_ref))
+    scatter.add_x(layer, 1, False)
     scatter.add_x(layer, 2, False)
 
     @pl.when(layer == 0)
@@ -1283,8 +1329,9 @@
     return pl.BlockSpec(shape, lambda i: (0,) * len(shape))
 
 
-def forward(layers, info, inverse, x_seg, target_seg, own_w, own_gain):
-    seg, width = x_seg.shape
+def forward(layers, micro, valid_len, present_stems, x_in, targets, flat_w, gain):
+    width = x_in.shape[1]
+    seg = x_in.shape[0] // micro
     dim = width // HEADS
     part = width // 4
     half = layers // 2
@@ -1292,33 +1339,40 @@
         (HEADS, seg, seg), (3 * HEADS, seg, dim), (seg, width), (seg, width), (4, seg, width), (4, seg, width)
     )
     kinds = (BF16, BF16, BF16, F32, BF16, BF16)
+
+    def slot():
+        return jnp.minimum(lax.axis_index("section"), micro - 1)
+
     return pl.pallas_call(
-        functools.partial(forward_kernel, layers, half),
+        functools.partial(forward_kernel, layers, half, micro),
         grid=(layers,),
         in_specs=[
             pl.BlockSpec(memory_space=pltpu.SMEM),
             pl.BlockSpec(memory_space=pltpu.SMEM),
-            whole_block((seg, width)),
-            whole_block((seg, width // 2)),
+            pl.BlockSpec((seg, width), lambda i: (slot(), 0)),
+            pl.BlockSpec((width // 2, seg), lambda i: (0, slot())),
             pl.BlockSpec(memory_space=pltpu.VMEM),
             pl.BlockSpec(memory_space=pltpu.VMEM),
         ],
         out_specs=[layer_block(s) for s in shapes]
         + [whole_block((layers, seg, width)), whole_block((seg, width)), whole_block((layers, 8, width))]
-        + [pl.BlockSpec(memory_space=pl.ANY), pl.BlockSpec(memory_space=pltpu.VMEM)],
+        + [pl.BlockSpec(memory_space=pl.ANY), whole_block((layers, 8, width))],
         out_shape=[jax.ShapeDtypeStruct((layers,) + s, k) for s, k in zip(shapes, kinds)]
         + [
             jax.ShapeDtypeStruct((layers, seg, width), BF16),
             jax.ShapeDtypeStruct((seg, width), F32),
             jax.ShapeDtypeStruct((layers, 8, width), F32),
             jax.ShapeDtypeStruct((layers, 48 * part, width), BF16),
-            jax.ShapeDtypeStruct((layers, 8, 8, 128), F32),
+            jax.ShapeDtypeStruct((layers, 8, width), F32),
         ],
         scratch_shapes=[
             pltpu.VMEM((HEADS, seg, dim), BF16),
             pltpu.VMEM((seg, width), F32),
             pltpu.VMEM((layers, 48 * part, width), BF16),
             pltpu.VMEM((layers, 8, 8, 128), F32),
+            pltpu.VMEM((6 * part, width), BF16),
+            pltpu.VMEM((8, 128), F32),
+            pltpu.VMEM((4, part, 128), F32),
             pltpu.SemaphoreType.DMA((2, 3)),
             pltpu.SemaphoreType.DMA((2, layers, 4)),
             pltpu.SemaphoreType.DMA((2, layers, 4)),
@@ -1330,7 +1384,7 @@
         compiler_params=pltpu.CompilerParams(
             vmem_limit_bytes=VMEM_LIMIT, collective_id=0, has_side_effects=True
         ),
-    )(info, inverse, x_seg, target_seg, own_w, own_gain)
+    )(valid_len, present_stems, x_in, targets.T, flat_w, gain)
 
 
 def backward(layers, loss_grad, full_w, full_g, sent, saved, stats):
@@ -1398,35 +1452,6 @@
     )(loss_grad, full_w, full_g, sent, *saved, stats)
 
 
-def flat_rows(array):
-    blocks, area = array.shape
-    return (
-        array.reshape(blocks // 8, 8, area // 128, 128).transpose(0, 2, 1, 3).reshape(-1, 128)
-    )
-
-
-def from_flat_rows(rows, blocks):
-    return (
-        rows.reshape(blocks // 8, -1, 8, 128).transpose(0, 2, 1, 3).reshape(blocks, -1)
-    )
-
-
-def load_block(rows_ref, base, block_ref):
-    lane = lax.broadcasted_iota(jnp.int32, (24, 128), 1)
-    a, b, c = (rows_ref[pl.ds(base + 8 * m, 24, stride=24), :] for m in range(3))
-    block_ref[pl.ds(0, 24, stride=4), :] = a
-    block_ref[pl.ds(1, 24, stride=4), :] = jnp.where(lane < 32, pltpu.roll(a, 32, 1), pltpu.roll(b, 32, 1))
-    block_ref[pl.ds(2, 24, stride=4), :] = jnp.where(lane < 64, pltpu.roll(b, 64, 1), pltpu.roll(c, 64, 1))
-    block_ref[pl.ds(3, 24, stride=4), :] = pltpu.roll(c, 96, 1)
-
-
-def flat_parts(block_ref):
-    lane = lax.broadcasted_iota(jnp.int32, (24, 128), 1)
-    a, b, c, d = (block_ref[pl.ds(r, 24, stride=4), :] for r in range(4))
-    b, c, d = pltpu.roll(b, 96, 1), pltpu.roll(c, 64, 1), pltpu.roll(d, 32, 1)
-    return jnp.where(lane < 96, a, b), jnp.where(lane < 64, b, c), jnp.where(lane < 32, c, d)
-
-
 def split(value):
     high = value.astype(BF16)
     return high, (value - high.astype(F32)).astype(BF16)
@@ -1437,9 +1462,9 @@
 
 
 def update_kernel(
-    layers, limit, step_ref, square_ref, tile_ref, quads_ref, w_ref, l_ref, r_ref, lroot_ref, rroot_ref,
+    layers, limit, length_ref, step_ref, square_ref, tile_ref, quads_ref, w_ref, l_ref, r_ref, lroot_ref, rroot_ref,
     gain_ref, gain_m_ref, gain_v_ref,
-    w_out, grad_out, l_out, r_out, gain_out, m_out, v_out, norm_out,
+    w_out, grad_out, l_out, r_out, gain_out, m_out, v_out, loss_out, norm_out, rms_out,
     block_ref,
 ):
     part, width = quads_ref.shape[1:]
@@ -1491,10 +1516,19 @@
         gain_out[...] = gain_ref[...] - 0.5 * m_hat / (jnp.sqrt(v_hat) + 1e-08)
         m_out[...] = m_new
         v_out[...] = v_new
-        norm_out[...] = jnp.broadcast_to(norm, norm_out.shape)
-
-
-def update(layers, limit, step_count, squares, tile, quads, flats, gains):
+        norm_out[...] = norm
+        frames = length_ref[0]
+        for k in range(1, length_ref.shape[0]):
+            frames = frames + length_ref[k]
+        frames = jnp.full((1, 1), frames, jnp.int32).astype(F32)
+        loss_out[...] = tile_ref[2 * layers : 2 * layers + 1, 3:4] / frames
+        squares = tile_ref[2 * layers : 2 * layers + 1, :3]
+        for k in range(1, layers):
+            squares = jnp.where(section == k, tile_ref[2 * layers + k : 2 * layers + k + 1, :3], squares)
+        rms_out[...] = jnp.sqrt(squares / (frames * width))
+
+
+def update(layers, limit, valid_len, step_count, squares, tile, quads, flats, gains):
     blocks = 4 * quads.shape[0]
     part, width = quads.shape[1:]
     rows = flats[0].shape[0]
@@ -1504,14 +1538,15 @@
     return pl.pallas_call(
         functools.partial(update_kernel, layers, limit),
         grid=(3,),
-        in_specs=[pl.BlockSpec(memory_space=pltpu.SMEM)] + whole * 2
+        in_specs=[pl.BlockSpec(memory_space=pltpu.SMEM)] * 2 + whole * 2
         + [pl.BlockSpec((2, part, width), lambda i: (i, 0, 0))] + flat * 5 + whole * 3,
-        out_specs=flat * 4 + whole * 4,
+        out_specs=flat * 4 + whole * 6,
         out_shape=[jax.ShapeDtypeStruct((rows, 128), F32)] * 4
-        + [jax.ShapeDtypeStruct(share, F32)] * 3 + [jax.ShapeDtypeStruct((8, 128), F32)],
+        + [jax.ShapeDtypeStruct(share, F32)] * 3
+        + [jax.ShapeDtypeStruct((1, 1), F32)] * 2 + [jax.ShapeDtypeStruct((1, 3), F32)],
         scratch_shapes=[pltpu.VMEM((6, part, 128), F32)],
         compiler_params=pltpu.CompilerParams(vmem_limit_bytes=VMEM_LIMIT),
-    )(step_count, squares, tile, quads, *flats, *gains)
+    )(valid_len, step_count, squares, tile, quads, *flats, *gains)
 
 
 def body(
@@ -1521,53 +1556,30 @@
     width = x_in.shape[1]
     part = width // 4
     layers = lax.axis_size("section")
-    section_idx = lax.axis_index("section")
     groups = lax.axis_size("dp")
-    group_idx = lax.axis_index("dp")
     micro = valid_len.shape[0] // groups
-    seg = x_in.shape[0] // micro
     own_blocks = w_master.shape[1]
-    own_gain = norm_gains.shape[2]
-    own_w = (
-        w_master[0].astype(BF16).reshape(own_blocks // 4, 4, part, part).transpose(0, 2, 1, 3)
-        .reshape(own_blocks // 4 * part, width)
-    )
-    gain_tile = jnp.zeros((8, 128), F32).at[:2, :own_gain].set(norm_gains[0])
-    slot = jnp.minimum(section_idx, micro - 1)
-    used = (section_idx < micro).astype(jnp.int32)
-    at = group_idx * micro + slot
-    info = jnp.concatenate([valid_len[at][None] * used, present_stems[at] * used])
-    frame_count = jnp.sum(valid_len).astype(F32)
-    x_seg = lax.dynamic_slice_in_dim(x_in, slot * seg, seg, 0)
-    target_seg = lax.dynamic_slice_in_dim(targets, slot * seg, seg, 0)
-    *saved, sent, loss_grad, stats, full_w, tiles = forward(
-        layers, info, (1.0 / frame_count)[None], x_seg, target_seg, own_w, gain_tile
-    )
-    full_g = (
-        tiles[:, :, :2, :own_gain].transpose(0, 2, 1, 3).reshape(layers, 2, width).astype(BF16).astype(F32)
+    flats = [flat_rows(a[0]) for a in (w_master, l_stats, r_stats, l_roots, r_roots)]
+    *saved, sent, loss_grad, stats, full_w, full_g = forward(
+        layers, micro, valid_len, present_stems, x_in, targets, flats[0], norm_gains[0]
     )
     own_quads, tile, squares = backward(layers, loss_grad, full_w, full_g, sent, saved, stats)
-    sums = tile[2 * layers : 3 * layers, :4]
-    loss_value = sums[0, 3] / frame_count
     clip_limit = 0.00015 * math.sqrt(layers * (own_blocks * groups * part * part + 2 * width))
-    flats = [flat_rows(a[0]) for a in (w_master, l_stats, r_stats, l_roots, r_roots)]
-    *news, gains_new, m_new, v_new, norms = update(
-        layers, clip_limit, step_count, squares, tile, own_quads.reshape(-1, part, width), flats,
+    *news, gains_new, m_new, v_new, loss_value, grad_norm, rms = update(
+        layers, clip_limit, valid_len, step_count, squares, tile, own_quads.reshape(-1, part, width), flats,
         (norm_gains[0], gain_m[0], gain_v[0]),
     )
-    w_new, grad_blocks, l_new, r_new = (from_flat_rows(a, own_blocks) for a in news)
-    grad_norm = norms[0, 0]
-    rms = jnp.sqrt(sums[section_idx, :3] / (frame_count * width)).reshape(1, 3)
+    w_new, grad_blocks, l_new, r_new = (from_flat_rows(a, own_blocks)[None] for a in news)
     return (
-        w_new[None],
-        grad_blocks[None],
-        l_new[None],
-        r_new[None],
+        w_new,
+        grad_blocks,
+        l_new,
+        r_new,
         gains_new[None],
         m_new[None],
         v_new[None],
-        loss_value,
-        grad_norm,
+        loss_value.reshape(()),
+        grad_norm.reshape(()),
         rms,
     )
 

time: 302 us -> 276 us (0.914)
  local copies, waits for them, and re-layouts: 11.4 us -> 1.37 us
  Pallas kernels: 282 us -> 273 us
  other arithmetic: 4.24 us -> 0 us
  between operations: 4.51 us -> 1.47 us
    pallas_call x1, Pallas kernels: 144 us -> 138 us  [backward(): pl.pallas_call(functools.partial(backward_kernel, layers, half), grid=(la...]
    dynamic_slice x3 -> x0, local copies, waits for them, and re-layouts: 3.2 us -> none  [the longest x1 1.39 us: body(): valid_len[at][None] * used]
    slice x3 -> x0, local copies, waits for them, and re-layouts: 3.1 us -> none  [the longest x1 1.25 us: body(): loss_value = sums[0, 3] / frame_count]
where the time goes in v6:
time: 276 us
  Pallas kernels  273 us (99%)
    pallas_call x1, Pallas kernels, backward(): pl.pallas_call(functools.partial(backward_kernel, layers, half), grid=(la...  138 us
    pallas_call x1, Pallas kernels, forward(): pl.pallas_call(functools.partial(forward_kernel, layers, half, micro), gr...  124 us
    pallas_call x1, Pallas kernels, update(): pl.pallas_call(functools.partial(update_kernel, layers, limit), grid=(3,)...  11.1 us

profile of v6, /device:TPU:2, one launch (start us, length us, event | category | flops | bytes accessed | tf_op | source)
XLA Modules:
  0.0 275.7 jit_solution(1989750899229515132)
XLA Ops:
  0.6 1.4 copy.23.stems_ref
  2.0 123.8 %shard_map.204 = (bf16[4,8,512,512]{3,2,1,0:T(8,128)(2,1)}, bf16[4,24,512,48]{3,2,1,0:T(8,128)(2,1)}, bf16[4,512,384]{2,1,0:T(8,128)(2,1)}, f32[4,512,384]{2,1,0...) custom-call(s32[32]{0:T(128)} %length_ref.3, ...), custom_call_target="tpu_custom_call" | custom-call | tf_op jit(solution)/shard_map/pallas_call | solution.py:1346
  125.8 138.0 %shard_map.205 = (f32[576,384]{1,0:T(8,128)}, f32[16,384]{1,0:T(8,128)}, f32[8,128]{1,0:T(8,128)}) custom-call(f32[512,384]{1,0:T(8,128)} %get-tuple-element.34.loss_grad_ref, bf16[4,4608,384]{2,1,0:T(8,128)(2,1)} %get-tuple-element.35.w_ref, f32[4,8,384]{2,1,0:T(8,128)} %get-tuple-element.36.gain_ref, bf16[4,512,384]{2,1,0:T(8,128)(2,1)} %get-tuple-element.37.sent_ref, ...), custom_call_target="tpu_custom_call" | custom-call | tf_op jit(solution)/shard_map/pallas_call | solution.py:1400
  264.5 11.1 %shard_map.206 = (f32[1728,128]{1,0:T(8,128)}, f32[1728,128]{1,0:T(8,128)}, f32[1728,128]{1,0:T(8,128)}, f32[1728,128]{1,0:T(8,128)}, f32[2,48]{1,0:T(2,128)}, /...) custom-call(s32[32]{0:T(128)} %length_ref.3, s32[1]{0:T(128)S(6)} %copy.24.step_ref, ...), custom_call_target="tpu_custom_call" | custom-call | tf_op jit(solution)/shard_map/pallas_call | solution.py:1538

commit v7 on v6

--- a/solution.py
+++ b/solution.py
@@ -247,9 +247,17 @@
         self.x_copy(layer, k, True).wait_recv()
         self.core_copy(layer, k).start()
 
-    def finish(self, layer):
+    def finish_first(self, layer):
         for k in range(8):
-            self.core_copy(layer, k, True).wait_recv()
+            @pl.when(self.z_peers[k % 4] == 0)
+            def _():
+                self.core_copy(layer, k, True).wait_recv()
+
+    def finish_rest(self, layer):
+        for k in range(8):
+            @pl.when(self.z_peers[k % 4] != 0)
+            def _():
+                self.core_copy(layer, k, True).wait_recv()
 
     def end(self, layers):
         for k in range(3):
@@ -282,9 +290,9 @@
 
 def forward_kernel(
     layers, half, micro, length_ref, stems_ref, x_ref, target_ref, flat_ref, raw_gain_ref,
-    probs_ref, heads_ref, att_ref, middle_ref, hidden_ref, slope_ref, sent_ref, loss_grad_ref, stats_ref,
+    probs_ref, qkv_ref, att_ref, middle_ref, hidden_ref, slope_ref, sent_ref, loss_grad_ref, stats_ref,
     full_ref, gains_out_ref,
-    hold_ref, out_ref, w_all_ref, gains_ref, own_ref, own_gain_ref, block_ref, *sems,
+    out_ref, w_all_ref, gains_ref, own_ref, own_gain_ref, block_ref, *sems,
 ):
     seg, width = x_ref.shape
     dim = width // HEADS
@@ -334,10 +342,18 @@
         for k in range(4, 8):
             gather.serve_x(0, k)
         gather.serve_z(1, 1)
+        gather.serve_y(1, 0)
         gather.serve_z(1, 2)
 
-    gather.finish(layer)
-    keep_copy(layer).start()
+    @pl.when(layer > 0)
+    def _():
+        gather.serve_x(layer, 7)
+
+    @pl.when(layer + 2 < layers)
+    def _():
+        gather.kick(layer + 2)
+
+    gather.finish_first(layer)
     more = layer + 1 < layers
 
     def serve(here, *steps):
@@ -373,38 +389,39 @@
         factor = lax.rsqrt(jnp.mean(stream * stream, axis=-1, keepdims=True) + 1e-06)
         normed = (stream * factor * gain_one).astype(BF16)
         for t in range(3):
-            qkv = dot_nn(normed, stack_quads(w_ref, t, 3, 4)).astype(BF16)
-            for h in range(HEADS):
-                heads_ref[0, t * HEADS + h, at] = qkv[:, h * dim : (h + 1) * dim]
+            qkv_ref[0, t, at] = dot_nn(normed, stack_quads(w_ref, t, 3, 4)).astype(BF16)
         return 0
 
     lax.fori_loop(0, chunks, qkv_step, 0)
+    serve(layer == 0, ("serve_y", 1))
+    serve(True, ("serve_x", 0), ("serve_x", 1))
     frames = lax.broadcasted_iota(jnp.int32, (1, seg), 1)
     masking = jnp.where(frames < length, 0.0, -1e30).astype(F32)
 
     def head_step(h):
-        keys = heads_ref[0, HEADS + h]
-        values = heads_ref[0, 2 * HEADS + h]
-        scores = dot_nt(heads_ref[0, h], keys) * dim ** (-0.5) + masking
+        queries, keys, values = (qkv_ref[0, t, :, h * dim : (h + 1) * dim] for t in range(3))
+        scores = dot_nt(queries, keys) * dim ** (-0.5) + masking
         top = jnp.max(scores, axis=-1, keepdims=True)
         expd = jnp.exp(scores - top)
         probs = (expd * (1.0 / jnp.sum(expd, axis=-1, keepdims=True))).astype(BF16)
         probs_ref[0, h] = probs
-        hold_ref[h] = dot_nn(probs, values).astype(BF16)
-
-    for h in range(HEADS // 2):
-        head_step(h)
-    serve(True, ("serve_z", 3), ("serve_x", 0), ("serve_x", 1))
-    ahead(True, ("kick",))
-    for h in range(HEADS // 2, HEADS):
-        head_step(h)
-    serve(True, ("serve_y", 0), ("serve_x", 2), ("serve_y", 1))
+        return dot_nn(probs, values).astype(BF16)
+
+    def put_heads(first):
+        heads = [head_step(h) for h in range(first, first + HEADS // 2)]
+        att_ref[0, :, first * dim : (first + HEADS // 2) * dim] = jnp.concatenate(heads, axis=1)
+
+    put_heads(0)
+    serve(True, ("serve_z", 3), ("serve_x", 2), ("serve_x", 4), ("serve_x", 5))
+    put_heads(HEADS // 2)
+    serve(True, ("serve_y", 2))
+    ahead(True, ("serve_z", 1), ("serve_y", 0))
+    gather.finish_rest(layer)
+    keep_copy(layer).start()
 
     def ffn_step(i, _):
         at = pl.ds(pl.multiple_of(i * rows, rows), rows)
-        attended = jnp.concatenate([hold_ref[h, at] for h in range(HEADS)], axis=1)
-        att_ref[0, at] = attended
-        branch_attn = dot_nn(attended, stack_quads(w_ref, 12, 1, 4))
+        branch_attn = dot_nn(att_ref[0, at], stack_quads(w_ref, 12, 1, 4))
         stream = stream_of(at)
         middle = stream + branch_attn
         middle_ref[0, at] = middle
@@ -418,6 +435,9 @@
             hidden_ref[0, c, at] = hidden
             slope_ref[0, c, at] = slope.astype(BF16)
             branch_ffn = branch_ffn + dot_nn(hidden, stack_quads(w_ref, 32 + 4 * c, 1, 4))
+            if c == 1:
+                serve(i == 1, ("serve_y", 3), ("serve_x", 6))
+                ahead(i == 1, ("serve_z", 2))
         output = middle + branch_ffn
         out_ref[at] = output
         sent_ref[jnp.minimum(layer + 1, layers - 1), at] = jnp.where(
@@ -427,13 +447,11 @@
         for k, value in enumerate((stream, branch_attn, branch_ffn)):
             stats_ref[layer, k : k + 1] += jnp.sum(valid * value * value, axis=0, keepdims=True)
 
-        ahead(i == 0, ("serve_z", 1))
-        serve(i == 0, ("serve_x", 3), ("serve_x", 4), ("serve_y", 2))
+        serve(i == 0, ("serve_x", 3))
         return 0
 
     lax.fori_loop(0, chunks, ffn_step, 0)
-    ahead(True, ("serve_z", 2))
-    serve(True, ("serve_y", 3), ("serve_x", 5), ("serve_x", 6), ("serve_x", 7))
+    ahead(True, ("serve_y", 1))
 
     @pl.when(layer == layers - 1)
     def _():
@@ -476,7 +494,7 @@
 
 class Scatter(Slabs):
     def __init__(self, refs, sems):
-        self.grads, self.core_in, self.x_in, self.y_in, self.z_in, self.last_out, self.last_in = refs
+        self.grads, self.core_in, self.x_in, self.y_in, self.stage, self.z_in, self.last_in = refs
         super().__init__(self.grads.shape[3])
         self.core_sems, self.x_sems, self.y_sems, self.z_sems, self.last_sems = sems
         self.mine = self.slab_of(self.x, self.core)
@@ -492,30 +510,28 @@
     def x_copy(self, layer, k):
         slot = lax.rem(layer, 2)
         return remote(
-            self.grads.at[slot, self.z_peers[k], :, self.edge_of(1 - self.x, self.core)], self.x_in.at[slot, k],
-            self.x_sems.at[0, slot, k], self.x_sems.at[1, slot, k], *self.x_peer(),
+            self.grads.at[slot, self.z_peers[k], :, self.edge_of(1 - self.x, self.core)], self.x_in.at[layer, k],
+            self.x_sems.at[0, layer, k], self.x_sems.at[1, layer, k], *self.x_peer(),
         )
 
     def y_copy(self, layer, k):
         slot = lax.rem(layer, 2)
         return remote(
-            self.grads.at[slot, self.z_peers[k], 1 - self.y, self.mine], self.y_in.at[slot, k],
-            self.y_sems.at[0, slot, k], self.y_sems.at[1, slot, k], *self.y_peer(),
+            self.grads.at[slot, self.z_peers[k], 1 - self.y, self.mine], self.y_in.at[layer, k],
+            self.y_sems.at[0, layer, k], self.y_sems.at[1, layer, k], *self.y_peer(),
         )
 
     def z_copy(self, layer, k):
-        slot = lax.rem(layer, 2)
         return remote(
-            self.grads.at[slot, self.z_peers[k], self.y, self.mine], self.z_in.at[layer, k - 1],
+            self.stage.at[layer, k], self.z_in.at[layer, k - 1],
             self.z_sems.at[0, layer, k - 1], self.z_sems.at[1, layer, k - 1], *self.z_peer(k),
         )
 
     def last_copy(self, layer):
-        slot = lax.rem(layer, 2)
         place = jnp.maximum(lax.rem(self.section - layer + 4, 4) - 1, 0)
         return remote(
-            self.last_out.at[slot], self.last_in.at[place],
-            self.last_sems.at[0, slot], self.last_sems.at[1, place], layer, self.group,
+            self.stage.at[layer, 0], self.last_in.at[place],
+            self.last_sems.at[0, layer], self.last_sems.at[1, place], layer, self.group,
         )
 
     def last_landed(self, place):
@@ -549,26 +565,27 @@
             slot = lax.rem(layer, 2)
             self.x_copy(layer, k).wait_recv()
             rows = self.edge_of(self.x, self.core)
+            inner = pl.ds(pl.multiple_of((self.slab - self.edge) * self.x, 16), self.edge)
             z = self.z_peers[k]
-            for y in range(2):
-                self.grads[slot, z, y, rows] = self.grads[slot, z, y, rows] + self.x_in[slot, k, y]
+            self.grads[slot, z, 1 - self.y, rows] = (
+                self.grads[slot, z, 1 - self.y, rows] + self.x_in[layer, k, 1 - self.y]
+            )
             self.y_copy(layer, k).start()
+            self.stage[layer, k] = self.grads[slot, z, self.y, self.mine]
+            self.stage[layer, k, inner] = self.stage[layer, k, inner] + self.x_in[layer, k, self.y]
 
     def add_y(self, layer, k, late):
         @pl.when((self.z_peers[k] == 0) == late)
         def _():
-            slot = lax.rem(layer, 2)
             self.y_copy(layer, k).wait_recv()
-            z = self.z_peers[k]
-            self.grads[slot, z, self.y, self.mine] = self.grads[slot, z, self.y, self.mine] + self.y_in[slot, k]
+            self.stage[layer, k] = self.stage[layer, k] + self.y_in[layer, k]
             if k:
                 self.z_copy(layer, k).start()
 
     def add_z(self, layer, result_ref):
-        slot = lax.rem(layer, 2)
         for k in range(1, 4):
             self.z_copy(layer, k).wait_recv()
-        total = self.grads[slot, self.z_peers[0], self.y, self.mine].astype(F32)
+        total = self.stage[layer, 0].astype(F32)
         for k in range(3):
             total = total + self.z_in[layer, k].astype(F32)
 
@@ -579,7 +596,7 @@
 
         @pl.when(layer != self.section)
         def _():
-            self.last_out[slot] = total.astype(BF16)
+            self.stage[layer, 0] = total.astype(BF16)
             self.last_copy(layer).start()
 
     def wait_sends(self, layer):
@@ -588,12 +605,19 @@
         for k in range(4):
             self.x_copy(layer, k).wait_send()
             self.y_copy(layer, k).wait_send()
-        for k in range(1, 4):
-            self.z_copy(layer, k).wait_send()
-
-        @pl.when(layer != self.section)
-        def _():
-            self.last_copy(layer).wait_send()
+
+    def end(self, layers):
+        def per_layer(layer, _):
+            for k in range(1, 4):
+                self.z_copy(layer, k).wait_send()
+
+            @pl.when(layer != self.section)
+            def _():
+                self.last_copy(layer).wait_send()
+
+            return 0
+
+        lax.fori_loop(0, layers, per_layer, 0)
 
     def collect(self, result_ref):
         for place in (0, 2, 1):
@@ -718,9 +742,9 @@
 
 def backward_kernel(
     layers, half, loss_grad_ref, w_ref, gain_ref, sent_ref,
-    probs_ref, heads_ref, att_ref, middle_ref, hidden_ref, slope_ref, stats_ref,
+    probs_ref, qkv_ref, att_ref, middle_ref, hidden_ref, slope_ref, stats_ref,
     result_ref, totals_ref, square_ref,
-    sends_ref, dffn_ref, dpre_ref, normed_ref, dmid_ref, datt_ref, dhold_ref, dheads_ref, dqkv_ref,
+    sends_ref, dffn_ref, dpre_ref, normed_ref, dmid_ref, datt_ref, dhold_ref, dqkv_ref,
     gain_grad_ref, *comm_refs,
 ):
     seg, width = loss_grad_ref.shape
@@ -749,10 +773,11 @@
             at = pl.ds(pl.multiple_of(lax.rem(quad, 6) * part, part), part)
             grads_ref[slot, owner // 2, lax.rem(owner, 2), at] = value[r * part : (r + 1) * part].astype(BF16)
 
-    def before(act):
-        @pl.when(layer < layers - 1)
+    def serve(back, here, *steps):
+        @pl.when((layer + back < layers) & here)
         def _():
-            act(layer + 1)
+            for kind, *args in steps:
+                getattr(scatter, kind)(layer + back, *args)
 
     def ffn_step(i, _):
         at = pl.ds(pl.multiple_of(i * rows, rows), rows)
@@ -777,19 +802,10 @@
         datt = dmid.astype(BF16)
         datt_ref[at] = datt
         dattended = dot_nt(datt, stack_quads(w_ref, 12, 1, 4)).astype(BF16)
-        for h in range(HEADS):
-            dhold_ref[h, at] = dattended[:, h * dim : (h + 1) * dim]
-
-        @pl.when(i == 0)
-        def _():
-            before(lambda at: scatter.add_core(at, True))
-            before(lambda at: scatter.add_x(at, 3, False))
-
-        @pl.when(i == 1)
-        def _():
-            before(lambda at: scatter.add_x(at, 0, False))
-            before(lambda at: scatter.add_y(at, 1, False))
-
+        dhold_ref[at] = dattended
+
+        serve(1, i == 1, ("add_x", 1, False), ("add_core", True))
+        serve(2, i == 1, ("add_y", 3, False), ("add_y", 0, False))
         return 0
 
     lax.fori_loop(0, chunks, ffn_step, 0)
@@ -808,45 +824,40 @@
     put_grad(12, 1, dot_tn(att_ref[0], datt_ref[...]))
     scatter.core_copy(layer, False).start()
 
-    @pl.when(layer < layers - 1)
-    def _():
-        for k in range(4):
-            scatter.add_x(layer + 1, k, True)
-        for k in (2, 3, 0):
-            scatter.add_y(layer + 1, k, False)
+    serve(1, True, ("add_x", 2, False))
+    serve(2, True, *[("add_y", k, True) for k in range(4)])
 
     def head_step(h):
-        queries = heads_ref[0, h]
-        keys = heads_ref[0, HEADS + h]
+        queries, keys, values = (qkv_ref[0, t, :, h * dim : (h + 1) * dim] for t in range(3))
         probs = probs_ref[0, h]
-        dhold = dhold_ref[h]
-        dprobs = dot_nt(dhold, heads_ref[0, 2 * HEADS + h])
+        dhold = dhold_ref[:, h * dim : (h + 1) * dim]
+        dprobs = dot_nt(dhold, values)
         wide = probs.astype(F32)
         dot_sum = jnp.sum(wide * dprobs, axis=-1, keepdims=True)
         dscores = (wide * (dprobs - dot_sum)).astype(BF16)
-        dheads_ref[h] = (dot_nn(dscores, keys) * dim ** (-0.5)).astype(BF16)
-        dheads_ref[HEADS + h] = (dot_tn(dscores, queries) * dim ** (-0.5)).astype(BF16)
-        dheads_ref[2 * HEADS + h] = dot_tn(probs, dhold).astype(BF16)
-
-    for h in range(HEADS // 2):
-        head_step(h)
-
-    @pl.when(layer < layers - 1)
-    def _():
-        for k in range(4):
-            scatter.add_y(layer + 1, k, True)
-
-    for h in range(HEADS // 2, HEADS):
-        head_step(h)
+        return (
+            (dot_nn(dscores, keys) * dim ** (-0.5)).astype(BF16),
+            (dot_tn(dscores, queries) * dim ** (-0.5)).astype(BF16),
+            dot_tn(probs, dhold).astype(BF16),
+        )
+
+    def put_heads(first, parts):
+        for t in range(3):
+            dqkv_ref[t, :, first * dim : (first + len(parts)) * dim] = jnp.concatenate([p[t] for p in parts], axis=1)
+
+    put_heads(0, [head_step(h) for h in range(HEADS // 2)])
+
+    serve(1, True, ("add_x", 3, False))
+
+    put_heads(HEADS // 2, [head_step(h) for h in range(HEADS // 2, HEADS)])
     scatter.add_core(layer, False)
+    serve(1, True, ("add_x", 0, False), ("add_y", 1, False))
 
     def qkv_step(i, _):
         at = pl.ds(pl.multiple_of(i * rows, rows), rows)
         dnormed = jnp.zeros((rows, width), F32)
         for t in range(3):
-            dqkv = jnp.concatenate([dheads_ref[t * HEADS + h, at] for h in range(HEADS)], axis=1)
-            dqkv_ref[t, at] = dqkv
-            dnormed = dnormed + dot_nt(dqkv, stack_quads(w_ref, t, 3, 4))
+            dnormed = dnormed + dot_nt(dqkv_ref[t, at], stack_quads(w_ref, t, 3, 4))
         prev = sent_ref[layer, at].astype(F32)
         skip = sent_ref[jnp.maximum(layer + 1 - half, 0), at].astype(F32)
         stream = prev + jnp.where(layer >= half, skip, 0.0)
@@ -865,9 +876,8 @@
     for t in range(3):
         qkv_grad_step(t, 0)
     scatter.core_copy(layer, True).start()
-    before(lambda at: scatter.add_z(at, result_ref))
-    scatter.add_x(layer, 1, False)
-    scatter.add_x(layer, 2, False)
+    serve(1, True, *[("add_x", k, True) for k in range(4)], ("add_y", 2, False))
+    serve(2, True, ("add_z", result_ref))
 
     @pl.when(layer == 0)
     def _():
@@ -881,19 +891,26 @@
             rows_out.append(row)
         rows_out.append(jnp.zeros((16 - 3 * layers, width), F32))
         totals.begin(jnp.concatenate(rows_out, axis=0))
+        scatter.add_x(0, 1, False)
         scatter.add_core(0, True)
+        scatter.add_y(1, 3, False)
+        scatter.add_y(1, 0, False)
+        totals.after_core()
+        scatter.add_x(0, 2, False)
+        for k in range(4):
+            scatter.add_y(1, k, True)
+        scatter.add_x(0, 3, False)
+        totals.after_y()
         scatter.add_y(0, 1, False)
-        scatter.add_x(0, 3, False)
-        totals.after_core()
         scatter.add_x(0, 0, False)
-        scatter.add_y(0, 2, False)
         for k in range(4):
             scatter.add_x(0, k, True)
+        scatter.add_y(0, 2, False)
+        scatter.add_z(1, result_ref)
         scatter.add_y(0, 3, False)
         scatter.add_y(0, 0, False)
         for k in range(4):
             scatter.add_y(0, k, True)
-        totals.after_y()
         scatter.add_z(0, result_ref)
         totals.after_z()
         scatter.collect(result_ref)
@@ -906,6 +923,7 @@
         totals_ref[...] = totals.after_x()
         scatter.wait_sends(1)
         scatter.wait_sends(0)
+        scatter.end(layers)
         totals.end()
 
 
@@ -1329,6 +1347,10 @@
     return pl.BlockSpec(shape, lambda i: (0,) * len(shape))
 
 
+def held_block(shape):
+    return pl.BlockSpec(shape, lambda i: (0,) * len(shape), pipeline_mode=pl.Buffered(1))
+
+
 def forward(layers, micro, valid_len, present_stems, x_in, targets, flat_w, gain):
     width = x_in.shape[1]
     seg = x_in.shape[0] // micro
@@ -1336,7 +1358,7 @@
     part = width // 4
     half = layers // 2
     shapes = (
-        (HEADS, seg, seg), (3 * HEADS, seg, dim), (seg, width), (seg, width), (4, seg, width), (4, seg, width)
+        (HEADS, seg, seg), (3, seg, width), (seg, width), (seg, width), (4, seg, width), (4, seg, width)
     )
     kinds = (BF16, BF16, BF16, F32, BF16, BF16)
 
@@ -1366,7 +1388,6 @@
             jax.ShapeDtypeStruct((layers, 8, width), F32),
         ],
         scratch_shapes=[
-            pltpu.VMEM((HEADS, seg, dim), BF16),
             pltpu.VMEM((seg, width), F32),
             pltpu.VMEM((layers, 48 * part, width), BF16),
             pltpu.VMEM((layers, 8, 8, 128), F32),
@@ -1401,10 +1422,10 @@
         functools.partial(backward_kernel, layers, half),
         grid=(layers,),
         in_specs=[
-            whole_block((seg, width)),
+            held_block((seg, width)),
             from_end(full_w),
             from_end(full_g),
-            whole_block((layers, seg, width)),
+            held_block((layers, seg, width)),
         ]
         + [from_end(a) for a in saved]
         + [pl.BlockSpec(memory_space=pltpu.VMEM)],
@@ -1421,26 +1442,25 @@
             pltpu.VMEM((seg, width), BF16),
             pltpu.VMEM((seg, width), F32),
             pltpu.VMEM((seg, width), BF16),
-            pltpu.VMEM((HEADS, seg, dim), BF16),
-            pltpu.VMEM((3 * HEADS, seg, dim), BF16),
+            pltpu.VMEM((seg, width), BF16),
             pltpu.VMEM((3, seg, width), BF16),
             pltpu.VMEM((layers, 8, width), F32),
             pltpu.VMEM((2, 4, 2, 576, width), BF16),
             pltpu.VMEM((2, 4, 2, 288, width), BF16),
-            pltpu.VMEM((2, 4, 2, 80, width), BF16),
-            pltpu.VMEM((2, 4, 208, width), BF16),
+            pltpu.VMEM((layers, 4, 2, 80, width), BF16),
+            pltpu.VMEM((layers, 4, 208, width), BF16),
+            pltpu.VMEM((layers, 4, 208, width), BF16),
             pltpu.VMEM((layers, 3, 208, width), BF16),
-            pltpu.VMEM((2, 208, width), BF16),
             pltpu.VMEM((3, 208, width), BF16),
             pltpu.VMEM((6, 16, width), F32),
             pltpu.VMEM((4, 16, width), F32),
             pltpu.VMEM((4, 8, 128), F32),
             pltpu.VMEM((8, 8, 128), F32),
             pltpu.SemaphoreType.DMA((2, 2, 2)),
-            pltpu.SemaphoreType.DMA((2, 2, 4)),
-            pltpu.SemaphoreType.DMA((2, 2, 4)),
+            pltpu.SemaphoreType.DMA((2, layers, 4)),
+            pltpu.SemaphoreType.DMA((2, layers, 4)),
             pltpu.SemaphoreType.DMA((2, layers, 3)),
-            pltpu.SemaphoreType.DMA((2, 3)),
+            pltpu.SemaphoreType.DMA((2, layers)),
             pltpu.SemaphoreType.DMA((2, 3)),
             pltpu.SemaphoreType.DMA((2, 3)),
             pltpu.SemaphoreType.DMA((2, 3)),

time: 276 us -> 262 us (0.949)
  Pallas kernels: 273 us -> 259 us
    pallas_call x1, Pallas kernels: 138 us -> 130 us  [backward(): pl.pallas_call(functools.partial(backward_kernel, layers, half), grid=(la...]
    pallas_call x1, Pallas kernels: 124 us -> 118 us  [forward(): pl.pallas_call(functools.partial(forward_kernel, layers, half, micro), gr...]
where the time goes in v7:
time: 262 us
  Pallas kernels  259 us (99%)
    pallas_call x1, Pallas kernels, backward(): pl.pallas_call(functools.partial(backward_kernel, layers, half), grid=(la...  130 us
    pallas_call x1, Pallas kernels, forward(): pl.pallas_call(functools.partial(forward_kernel, layers, half, micro), gr...  118 us
    pallas_call x1, Pallas kernels, update(): pl.pallas_call(functools.partial(update_kernel, layers, limit), grid=(3,)...  11.1 us

profile of v7, /device:TPU:2, one launch (start us, length us, event | category | flops | bytes accessed | tf_op | source)
XLA Modules:
  0.0 261.7 jit_solution(16303535910812116866)
XLA Ops:
  0.6 1.4 copy.23.stems_ref
  2.0 118.1 %shard_map.204 = (bf16[4,8,512,512]{3,2,1,0:T(8,128)(2,1)}, bf16[4,3,512,384]{3,2,1,0:T(8,128)(2,1)}, bf16[4,512,384]{2,1,0:T(8,128)(2,1)}, f32[4,512,384]{2,1,0...) custom-call(s32[32]{0:T(128)} %length_ref.3, ...), custom_call_target="tpu_custom_call" | custom-call | tf_op jit(solution)/shard_map/pallas_call | solution.py:1368
  120.1 129.7 %shard_map.205 = (f32[576,384]{1,0:T(8,128)}, f32[16,384]{1,0:T(8,128)}, f32[8,128]{1,0:T(8,128)}) custom-call(f32[512,384]{1,0:T(8,128)} %get-tuple-element.34.loss_grad_ref, bf16[4,4608,384]{2,1,0:T(8,128)(2,1)} %get-tuple-element.35.w_ref, f32[4,8,384]{2,1,0:T(8,128)} %get-tuple-element.36.gain_ref, bf16[4,512,384]{2,1,0:T(8,128)(2,1)} %get-tuple-element.37.sent_ref, ...), custom_call_target="tpu_custom_call" | custom-call | tf_op jit(solution)/shard_map/pallas_call | solution.py:1421
  250.5 11.1 %shard_map.206 = (f32[1728,128]{1,0:T(8,128)}, f32[1728,128]{1,0:T(8,128)}, f32[1728,128]{1,0:T(8,128)}, f32[1728,128]{1,0:T(8,128)}, f32[2,48]{1,0:T(2,128)}, /...) custom-call(s32[32]{0:T(128)} %length_ref.3, s32[1]{0:T(128)S(6)} %copy.24.step_ref, ...), custom_call_target="tpu_custom_call" | custom-call | tf_op jit(solution)/shard_map/pallas_call | solution.py:1558

commit v8 on v7

--- a/solution.py
+++ b/solution.py
@@ -208,9 +208,15 @@
             ref = self.gains.at[lax.rem(self.section - (k - 6) + 4, 4)]
         return remote(ref, ref, self.gain_sems.at[0, k], self.gain_sems.at[1, k], self.section, self.group)
 
-    def begin(self):
+    def spread_own(self):
         for k in range(3):
             self.spread_copy(k).start()
+
+    def begin(self):
+        @pl.when(self.section == 0)
+        def _():
+            self.spread_own()
+
         for k in range(7):
             self.gain_copy(k).start()
         rows = self.slab_of(self.x, self.core)
@@ -288,11 +294,16 @@
     return length_ref[at] * used, [stems_ref[at, k] * used for k in range(4)], frames
 
 
+FIRST_POINTS = {"qkv": "z2 y1 x0 x1", "heads": "z3 x2 x4 x5", "attended": "y2", "ffn1": "x3", "ffn2": "y3 x6", "ffn3": "x7"}
+POINTS = {"qkv": "x0 x1", "heads": "z3 x2 x4 x5", "attended": "y2", "ffn1": "x3", "ffn2": "y3 x6", "ffn3": "x7"}
+AHEAD_POINTS = {"attended": "z1 y0", "ffn2": "z2", "ffn3": "y1"}
+
+
 def forward_kernel(
     layers, half, micro, length_ref, stems_ref, x_ref, target_ref, flat_ref, raw_gain_ref,
     probs_ref, qkv_ref, att_ref, middle_ref, hidden_ref, slope_ref, sent_ref, loss_grad_ref, stats_ref,
     full_ref, gains_out_ref,
-    out_ref, w_all_ref, gains_ref, own_ref, own_gain_ref, block_ref, *sems,
+    out_ref, normed_ref, w_all_ref, gains_ref, own_ref, own_gain_ref, block_ref, *sems,
 ):
     seg, width = x_ref.shape
     dim = width // HEADS
@@ -325,13 +336,18 @@
         sent_ref[0] = x_ref[...]
         stats_ref[...] = jnp.zeros_like(stats_ref)
         gather.kick(0)
+
+        @pl.when(gather.section != 0)
+        def _():
+            gather.spread_own()
+
         gather.share_gains()
         gather.serve_z(0, 1)
         gather.serve_z(0, 2)
+        gather.kick(1)
         gather.serve_x(0, 0)
         gather.serve_x(0, 1)
         gather.serve_z(0, 3)
-        gather.kick(1)
         gather.wait_gains()
         gather.serve_y(0, 0)
         gather.serve_x(0, 2)
@@ -343,11 +359,6 @@
             gather.serve_x(0, k)
         gather.serve_z(1, 1)
         gather.serve_y(1, 0)
-        gather.serve_z(1, 2)
-
-    @pl.when(layer > 0)
-    def _():
-        gather.serve_x(layer, 7)
 
     @pl.when(layer + 2 < layers)
     def _():
@@ -356,17 +367,18 @@
     gather.finish_first(layer)
     more = layer + 1 < layers
 
-    def serve(here, *steps):
-        @pl.when(more & here)
-        def _():
-            for kind, k in steps:
-                getattr(gather, kind)(layer + 1, k)
-
-    def ahead(here, *steps):
-        @pl.when((layer + 2 < layers) & here)
-        def _():
-            for kind, *k in steps:
-                getattr(gather, kind)(layer + 2, *k)
+    def serve(point):
+        for here, steps, later in (
+            (layer == 0, FIRST_POINTS.get(point, ""), ""),
+            (layer > 0, POINTS.get(point, ""), ""),
+            (layer >= 0, "", AHEAD_POINTS.get(point, "")),
+        ):
+            for names, back in ((steps, 1), (later, 2)):
+                if names:
+                    @pl.when((layer + back < layers) & here)
+                    def _():
+                        for name in names.split():
+                            getattr(gather, "serve_" + name[0])(layer + back, int(name[1]))
 
     def stream_of(at):
         prev = sent_ref[layer, at].astype(F32)
@@ -383,18 +395,12 @@
     gains_out_ref[layer, 0:1] = gain_one
     gains_out_ref[layer, 1:2] = gain_two
 
-    def qkv_step(i, _):
-        at = pl.ds(pl.multiple_of(i * rows, rows), rows)
-        stream = stream_of(at)
-        factor = lax.rsqrt(jnp.mean(stream * stream, axis=-1, keepdims=True) + 1e-06)
-        normed = (stream * factor * gain_one).astype(BF16)
-        for t in range(3):
-            qkv_ref[0, t, at] = dot_nn(normed, stack_quads(w_ref, t, 3, 4)).astype(BF16)
-        return 0
-
-    lax.fori_loop(0, chunks, qkv_step, 0)
-    serve(layer == 0, ("serve_y", 1))
-    serve(True, ("serve_x", 0), ("serve_x", 1))
+    first_stream = stream_of(slice(None))
+    first_factor = lax.rsqrt(jnp.mean(first_stream * first_stream, axis=-1, keepdims=True) + 1e-06)
+    first_normed = (first_stream * first_factor * gain_one).astype(BF16)
+    for t in range(3):
+        qkv_ref[0, t] = dot_nn(first_normed, stack_quads(w_ref, t, 3, 4)).astype(BF16)
+    serve("qkv")
     frames = lax.broadcasted_iota(jnp.int32, (1, seg), 1)
     masking = jnp.where(frames < length, 0.0, -1e30).astype(F32)
 
@@ -412,46 +418,49 @@
         att_ref[0, :, first * dim : (first + HEADS // 2) * dim] = jnp.concatenate(heads, axis=1)
 
     put_heads(0)
-    serve(True, ("serve_z", 3), ("serve_x", 2), ("serve_x", 4), ("serve_x", 5))
+    serve("heads")
     put_heads(HEADS // 2)
-    serve(True, ("serve_y", 2))
-    ahead(True, ("serve_z", 1), ("serve_y", 0))
+    serve("attended")
     gather.finish_rest(layer)
     keep_copy(layer).start()
 
-    def ffn_step(i, _):
-        at = pl.ds(pl.multiple_of(i * rows, rows), rows)
-        branch_attn = dot_nn(att_ref[0, at], stack_quads(w_ref, 12, 1, 4))
-        stream = stream_of(at)
-        middle = stream + branch_attn
-        middle_ref[0, at] = middle
-        factor = lax.rsqrt(jnp.mean(middle * middle, axis=-1, keepdims=True) + 1e-06)
-        normed = (middle * factor * gain_two).astype(BF16)
-        branch_ffn = jnp.zeros((rows, width), F32)
-        for c in range(4):
-            pre_act = dot_nn(normed, stack_quads(w_ref, 16 + c, 4, 4))
-            hidden, slope = gelu_parts(pre_act)
-            hidden = hidden.astype(BF16)
-            hidden_ref[0, c, at] = hidden
-            slope_ref[0, c, at] = slope.astype(BF16)
-            branch_ffn = branch_ffn + dot_nn(hidden, stack_quads(w_ref, 32 + 4 * c, 1, 4))
-            if c == 1:
-                serve(i == 1, ("serve_y", 3), ("serve_x", 6))
-                ahead(i == 1, ("serve_z", 2))
-        output = middle + branch_ffn
-        out_ref[at] = output
-        sent_ref[jnp.minimum(layer + 1, layers - 1), at] = jnp.where(
-            layer + 1 < layers, output.astype(BF16), sent_ref[layers - 1, at]
-        )
-        valid = (lax.broadcasted_iota(jnp.int32, (rows, 1), 0) + i * rows < length).astype(F32)
-        for k, value in enumerate((stream, branch_attn, branch_ffn)):
-            stats_ref[layer, k : k + 1] += jnp.sum(valid * value * value, axis=0, keepdims=True)
-
-        serve(i == 0, ("serve_x", 3))
-        return 0
-
-    lax.fori_loop(0, chunks, ffn_step, 0)
-    ahead(True, ("serve_y", 1))
+    valid = (lax.broadcasted_iota(jnp.int32, (seg, 1), 0) < length).astype(F32)
+
+    def add_stat(k, value):
+        stats_ref[layer, k : k + 1] = jnp.sum(valid * value * value, axis=0, keepdims=True)
+
+    branch_attn = dot_nn(att_ref[0], stack_quads(w_ref, 12, 1, 4))
+    stream = stream_of(slice(None))
+    middle = stream + branch_attn
+    middle_ref[0] = middle
+    add_stat(0, stream)
+    add_stat(1, branch_attn)
+    factor = lax.rsqrt(jnp.mean(middle * middle, axis=-1, keepdims=True) + 1e-06)
+    normed_ref[...] = (middle * factor * gain_two).astype(BF16)
+
+    def ffn_step(c):
+        pre_act = dot_nn(normed_ref[...], stack_quads(w_ref, 16 + c, 4, 4))
+        hidden, slope = gelu_parts(pre_act)
+        hidden = hidden.astype(BF16)
+        hidden_ref[0, c] = hidden
+        slope_ref[0, c] = slope.astype(BF16)
+        part_sum = dot_nn(hidden, stack_quads(w_ref, 32 + 4 * c, 1, 4))
+        out_ref[...] = part_sum if c == 0 else out_ref[...] + part_sum
+
+    for c in range(4):
+        ffn_step(c)
+        if c < 3:
+            serve(f"ffn{c}")
+    branch_ffn = out_ref[...]
+    add_stat(2, branch_ffn)
+    output = middle_ref[0] + branch_ffn
+    out_ref[...] = output
+
+    @pl.when(layer + 1 < layers)
+    def _():
+        sent_ref[layer + 1] = out_ref[...].astype(BF16)
+
+    serve("ffn3")
 
     @pl.when(layer == layers - 1)
     def _():
@@ -493,44 +502,53 @@
 
 
 class Scatter(Slabs):
+    PARTS = ((3, 4), (1, 3), (0, 1))
+
     def __init__(self, refs, sems):
         self.grads, self.core_in, self.x_in, self.y_in, self.stage, self.z_in, self.last_in = refs
         super().__init__(self.grads.shape[3])
         self.core_sems, self.x_sems, self.y_sems, self.z_sems, self.last_sems = sems
         self.mine = self.slab_of(self.x, self.core)
-
-    def core_copy(self, layer, late):
+        self.z = self.z_peers[0]
+
+    def core_copy(self, layer, number):
         slot = lax.rem(layer, 2)
-        zs = pl.ds(0, 1) if late else pl.ds(1, 3)
+        first, last = self.PARTS[number]
+        zs = pl.ds(first, last - first)
         return remote(
             self.grads.at[slot, zs, :, self.half_of(1 - self.core)], self.core_in.at[slot, zs],
-            self.core_sems.at[0, slot, int(late)], self.core_sems.at[1, slot, int(late)], *self.core_peer(),
-        )
-
-    def x_copy(self, layer, k):
+            self.core_sems.at[0, slot, number], self.core_sems.at[1, slot, number], *self.core_peer(),
+        )
+
+    def x_copy(self, layer, z):
         slot = lax.rem(layer, 2)
         return remote(
-            self.grads.at[slot, self.z_peers[k], :, self.edge_of(1 - self.x, self.core)], self.x_in.at[layer, k],
-            self.x_sems.at[0, layer, k], self.x_sems.at[1, layer, k], *self.x_peer(),
-        )
-
-    def y_copy(self, layer, k):
+            self.grads.at[slot, z, :, self.edge_of(1 - self.x, self.core)], self.x_in.at[layer, z],
+            self.x_sems.at[0, layer, z], self.x_sems.at[1, layer, z], *self.x_peer(),
+        )
+
+    def y_copy(self, layer, z):
         slot = lax.rem(layer, 2)
         return remote(
-            self.grads.at[slot, self.z_peers[k], 1 - self.y, self.mine], self.y_in.at[layer, k],
-            self.y_sems.at[0, layer, k], self.y_sems.at[1, layer, k], *self.y_peer(),
-        )
-
-    def z_copy(self, layer, k):
+            self.grads.at[slot, z, 1 - self.y, self.mine], self.y_in.at[layer, z],
+            self.y_sems.at[0, layer, z], self.y_sems.at[1, layer, z], *self.y_peer(),
+        )
+
+    def z_copy(self, layer, z):
+        place = jnp.maximum(self.z_peers[z] - 1, 0)
         return remote(
-            self.stage.at[layer, k], self.z_in.at[layer, k - 1],
-            self.z_sems.at[0, layer, k - 1], self.z_sems.at[1, layer, k - 1], *self.z_peer(k),
-        )
+            self.stage.at[layer, z], self.z_in.at[layer, place],
+            self.z_sems.at[0, layer, z], self.z_sems.at[1, layer, place], self.section, z * 2 + self.y,
+        )
+
+    def z_landed(self, layer, place):
+        ref = self.z_in.at[layer, place]
+        return remote(ref, ref, self.z_sems.at[0, layer, 0], self.z_sems.at[1, layer, place], *self.z_peer(place + 1))
 
     def last_copy(self, layer):
         place = jnp.maximum(lax.rem(self.section - layer + 4, 4) - 1, 0)
         return remote(
-            self.stage.at[layer, 0], self.last_in.at[place],
+            self.stage.at[layer, self.z], self.last_in.at[place],
             self.last_sems.at[0, layer], self.last_sems.at[1, place], layer, self.group,
         )
 
@@ -540,52 +558,45 @@
             self.last_sems.at[0, 0], self.last_sems.at[1, place], self.section, self.group,
         )
 
-    def for_part(self, late, act):
-        for k in (1, 2, 3, 0):
-            @pl.when((self.z_peers[k] == 0) == late)
-            def _():
-                act(k)
-
-    def add_core(self, layer, late):
+    def add_core(self, layer, number):
         slot = lax.rem(layer, 2)
-        self.core_copy(layer, late).wait_recv()
+        self.core_copy(layer, number).wait_recv()
         rows = self.half_of(self.core)
+        first, last = self.PARTS[number]
 
         def add(i, _):
             z, y = i // 2, lax.rem(i, 2)
             self.grads[slot, z, y, rows] = self.grads[slot, z, y, rows] + self.core_in[slot, z, y]
             return 0
 
-        lax.fori_loop(0 if late else 2, 2 if late else 8, add, 0)
-        self.for_part(late, lambda k: self.x_copy(layer, k).start())
-
-    def add_x(self, layer, k, late):
-        @pl.when((self.z_peers[k] == 0) == late)
+        lax.fori_loop(2 * first, 2 * last, add, 0)
+        for z in range(first, last):
+            self.x_copy(layer, z).start()
+
+    def add_x(self, layer, z):
+        slot = lax.rem(layer, 2)
+        self.x_copy(layer, z).wait_recv()
+        rows = self.edge_of(self.x, self.core)
+        inner = pl.ds(pl.multiple_of((self.slab - self.edge) * self.x, 16), self.edge)
+        self.grads[slot, z, 1 - self.y, rows] = (
+            self.grads[slot, z, 1 - self.y, rows] + self.x_in[layer, z, 1 - self.y]
+        )
+        self.y_copy(layer, z).start()
+        self.stage[layer, z] = self.grads[slot, z, self.y, self.mine]
+        self.stage[layer, z, inner] = self.stage[layer, z, inner] + self.x_in[layer, z, self.y]
+
+    def add_y(self, layer, z):
+        self.y_copy(layer, z).wait_recv()
+        self.stage[layer, z] = self.stage[layer, z] + self.y_in[layer, z]
+
+        @pl.when(self.z != z)
         def _():
-            slot = lax.rem(layer, 2)
-            self.x_copy(layer, k).wait_recv()
-            rows = self.edge_of(self.x, self.core)
-            inner = pl.ds(pl.multiple_of((self.slab - self.edge) * self.x, 16), self.edge)
-            z = self.z_peers[k]
-            self.grads[slot, z, 1 - self.y, rows] = (
-                self.grads[slot, z, 1 - self.y, rows] + self.x_in[layer, k, 1 - self.y]
-            )
-            self.y_copy(layer, k).start()
-            self.stage[layer, k] = self.grads[slot, z, self.y, self.mine]
-            self.stage[layer, k, inner] = self.stage[layer, k, inner] + self.x_in[layer, k, self.y]
-
-    def add_y(self, layer, k, late):
-        @pl.when((self.z_peers[k] == 0) == late)
-        def _():
-            self.y_copy(layer, k).wait_recv()
-            self.stage[layer, k] = self.stage[layer, k] + self.y_in[layer, k]
-            if k:
-                self.z_copy(layer, k).start()
+            self.z_copy(layer, z).start()
 
     def add_z(self, layer, result_ref):
-        for k in range(1, 4):
-            self.z_copy(layer, k).wait_recv()
-        total = self.stage[layer, 0].astype(F32)
+        for place in range(3):
+            self.z_landed(layer, place).wait_recv()
+        total = self.stage[layer, self.z].astype(F32)
         for k in range(3):
             total = total + self.z_in[layer, k].astype(F32)
 
@@ -596,20 +607,22 @@
 
         @pl.when(layer != self.section)
         def _():
-            self.stage[layer, 0] = total.astype(BF16)
+            self.stage[layer, self.z] = total.astype(BF16)
             self.last_copy(layer).start()
 
-    def wait_sends(self, layer):
-        for late in (False, True):
-            self.core_copy(layer, late).wait_send()
-        for k in range(4):
-            self.x_copy(layer, k).wait_send()
-            self.y_copy(layer, k).wait_send()
+    def wait_sends(self, layer, last):
+        for number in (2,) if last else (0, 1):
+            self.core_copy(layer, number).wait_send()
+        for z in (0, 1) if last else (2, 3):
+            self.x_copy(layer, z).wait_send()
+            self.y_copy(layer, z).wait_send()
 
     def end(self, layers):
         def per_layer(layer, _):
-            for k in range(1, 4):
-                self.z_copy(layer, k).wait_send()
+            for z in range(4):
+                @pl.when(self.z != z)
+                def _():
+                    self.z_copy(layer, z).wait_send()
 
             @pl.when(layer != self.section)
             def _():
@@ -779,15 +792,20 @@
             for kind, *args in steps:
                 getattr(scatter, kind)(layer + back, *args)
 
+    serve(2, True, ("wait_sends", False))
+    later = sends_ref[jnp.minimum(layer + 1, layers - 1)].astype(F32)
+    skip = sends_ref[jnp.minimum(layer + half, layers - 1)].astype(F32)
+    dmid_ref[...] = jnp.where(
+        layer == layers - 1, loss_grad_ref[...], later + jnp.where(layer + half < layers, skip, 0.0)
+    )
+    dffn_ref[...] = dmid_ref[...].astype(BF16)
+    for c in range(4):
+        put_grad(32 + 4 * c, 1, dot_tn(hidden_ref[0, c], dffn_ref[...]))
+    scatter.core_copy(layer, 0).start()
+
     def ffn_step(i, _):
         at = pl.ds(pl.multiple_of(i * rows, rows), rows)
-        later = sends_ref[jnp.minimum(layer + 1, layers - 1), at].astype(F32)
-        skip = sends_ref[jnp.minimum(layer + half, layers - 1), at].astype(F32)
-        upstream = jnp.where(
-            layer == layers - 1, loss_grad_ref[at], later + jnp.where(layer + half < layers, skip, 0.0)
-        )
-        dffn = upstream.astype(BF16)
-        dffn_ref[at] = dffn
+        dffn = dffn_ref[at]
         dnormed = jnp.zeros((rows, width), F32)
         for c in range(4):
             dhidden = dot_nt(dffn, stack_quads(w_ref, 32 + 4 * c, 1, 4))
@@ -797,35 +815,31 @@
         back, gain_grad, normed = norm_reverse(middle_ref[0, at], gain_two, dnormed)
         gain_grad_ref[layer, 1:2] += gain_grad
         normed_ref[at] = normed
-        dmid = upstream + back
+        dmid = dmid_ref[at] + back
         dmid_ref[at] = dmid
         datt = dmid.astype(BF16)
         datt_ref[at] = datt
         dattended = dot_nt(datt, stack_quads(w_ref, 12, 1, 4)).astype(BF16)
         dhold_ref[at] = dattended
 
-        serve(1, i == 1, ("add_x", 1, False), ("add_core", True))
-        serve(2, i == 1, ("add_y", 3, False), ("add_y", 0, False))
+        serve(1, i == 1, ("add_y", 3), ("add_x", 1), ("add_core", 2))
+        serve(2, i == 1, ("add_y", 0))
         return 0
 
     lax.fori_loop(0, chunks, ffn_step, 0)
 
-    @pl.when(layer < layers - 2)
-    def _():
-        scatter.wait_sends(layer + 2)
+    serve(2, True, ("wait_sends", True))
 
     def ffn_grad_step(c, _):
-        put_grad(32 + 4 * c, 1, dot_tn(hidden_ref[0, c], dffn_ref[...]))
         put_grad(16 + c, 4, dot_tn(normed_ref[...], dpre_ref[c]))
         return 0
 
     for c in range(4):
         ffn_grad_step(c, 0)
     put_grad(12, 1, dot_tn(att_ref[0], datt_ref[...]))
-    scatter.core_copy(layer, False).start()
-
-    serve(1, True, ("add_x", 2, False))
-    serve(2, True, *[("add_y", k, True) for k in range(4)])
+    scatter.core_copy(layer, 1).start()
+    scatter.add_core(layer, 0)
+    serve(1, True, ("add_x", 2))
 
     def head_step(h):
         queries, keys, values = (qkv_ref[0, t, :, h * dim : (h + 1) * dim] for t in range(3))
@@ -846,12 +860,12 @@
             dqkv_ref[t, :, first * dim : (first + len(parts)) * dim] = jnp.concatenate([p[t] for p in parts], axis=1)
 
     put_heads(0, [head_step(h) for h in range(HEADS // 2)])
-
-    serve(1, True, ("add_x", 3, False))
+    scatter.add_core(layer, 1)
+    serve(1, True, ("add_x", 0))
 
     put_heads(HEADS // 2, [head_step(h) for h in range(HEADS // 2, HEADS)])
-    scatter.add_core(layer, False)
-    serve(1, True, ("add_x", 0, False), ("add_y", 1, False))
+    scatter.add_x(layer, 3)
+    serve(1, True, ("add_y", 1))
 
     def qkv_step(i, _):
         at = pl.ds(pl.multiple_of(i * rows, rows), rows)
@@ -875,8 +889,8 @@
 
     for t in range(3):
         qkv_grad_step(t, 0)
-    scatter.core_copy(layer, True).start()
-    serve(1, True, *[("add_x", k, True) for k in range(4)], ("add_y", 2, False))
+    scatter.core_copy(layer, 2).start()
+    serve(1, True, ("add_y", 2))
     serve(2, True, ("add_z", result_ref))
 
     @pl.when(layer == 0)
@@ -891,26 +905,18 @@
             rows_out.append(row)
         rows_out.append(jnp.zeros((16 - 3 * layers, width), F32))
         totals.begin(jnp.concatenate(rows_out, axis=0))
-        scatter.add_x(0, 1, False)
-        scatter.add_core(0, True)
-        scatter.add_y(1, 3, False)
-        scatter.add_y(1, 0, False)
+        scatter.add_y(0, 3)
+        scatter.add_x(0, 1)
+        scatter.add_core(0, 2)
+        scatter.add_y(1, 0)
         totals.after_core()
-        scatter.add_x(0, 2, False)
-        for k in range(4):
-            scatter.add_y(1, k, True)
-        scatter.add_x(0, 3, False)
+        scatter.add_x(0, 2)
+        scatter.add_x(0, 0)
         totals.after_y()
-        scatter.add_y(0, 1, False)
-        scatter.add_x(0, 0, False)
-        for k in range(4):
-            scatter.add_x(0, k, True)
-        scatter.add_y(0, 2, False)
+        scatter.add_y(0, 1)
+        scatter.add_y(0, 2)
+        scatter.add_y(0, 0)
         scatter.add_z(1, result_ref)
-        scatter.add_y(0, 3, False)
-        scatter.add_y(0, 0, False)
-        for k in range(4):
-            scatter.add_y(0, k, True)
         scatter.add_z(0, result_ref)
         totals.after_z()
         scatter.collect(result_ref)
@@ -921,8 +927,9 @@
         folded = square[:, :128] + square[:, 128:256] + square[:, 256:]
         square_ref[...] = totals.norm(folded)
         totals_ref[...] = totals.after_x()
-        scatter.wait_sends(1)
-        scatter.wait_sends(0)
+        for back in (1, 0):
+            for last in (False, True):
+                scatter.wait_sends(back, last)
         scatter.end(layers)
         totals.end()
 
@@ -1389,6 +1396,7 @@
         ],
         scratch_shapes=[
             pltpu.VMEM((seg, width), F32),
+            pltpu.VMEM((seg, width), BF16),
             pltpu.VMEM((layers, 48 * part, width), BF16),
             pltpu.VMEM((layers, 8, 8, 128), F32),
             pltpu.VMEM((6 * part, width), BF16),
@@ -1456,10 +1464,10 @@
             pltpu.VMEM((4, 16, width), F32),
             pltpu.VMEM((4, 8, 128), F32),
             pltpu.VMEM((8, 8, 128), F32),
-            pltpu.SemaphoreType.DMA((2, 2, 2)),
+            pltpu.SemaphoreType.DMA((2, 2, 3)),
             pltpu.SemaphoreType.DMA((2, layers, 4)),
             pltpu.SemaphoreType.DMA((2, layers, 4)),
-            pltpu.SemaphoreType.DMA((2, layers, 3)),
+            pltpu.SemaphoreType.DMA((2, layers, 4)),
             pltpu.SemaphoreType.DMA((2, layers)),
             pltpu.SemaphoreType.DMA((2, 3)),
             pltpu.SemaphoreType.DMA((2, 3)),

time: 262 us -> 255 us (0.973)
  Pallas kernels: 259 us -> 252 us
    pallas_call x1, Pallas kernels: 118 us -> 113 us  [forward(): pl.pallas_call(functools.partial(forward_kernel, layers, half, micro), gr...]
where the time goes in v8:
time: 255 us
  Pallas kernels  252 us (99%)
    pallas_call x1, Pallas kernels, backward(): pl.pallas_call(functools.partial(backward_kernel, layers, half), grid=(la...  127 us
    pallas_call x1, Pallas kernels, forward(): pl.pallas_call(functools.partial(forward_kernel, layers, half, micro), gr...  113 us
    pallas_call x1, Pallas kernels, update(): pl.pallas_call(functools.partial(update_kernel, layers, limit), grid=(3,)...  11 us

profile of v8, /device:TPU:2, one launch (start us, length us, event | category | flops | bytes accessed | tf_op | source)
XLA Modules:
  0.0 254.8 jit_solution(5216529534025748374)
XLA Ops:
  0.6 1.4 copy.23.stems_ref
  2.0 113.5 %shard_map.204 = (bf16[4,8,512,512]{3,2,1,0:T(8,128)(2,1)}, bf16[4,3,512,384]{3,2,1,0:T(8,128)(2,1)}, bf16[4,512,384]{2,1,0:T(8,128)(2,1)}, f32[4,512,384]{2,1,0...) custom-call(s32[32]{0:T(128)} %length_ref.3, ...), custom_call_target="tpu_custom_call" | custom-call | tf_op jit(solution)/shard_map/pallas_call | solution.py:1375
  115.5 127.5 %shard_map.205 = (f32[576,384]{1,0:T(8,128)}, f32[16,384]{1,0:T(8,128)}, f32[8,128]{1,0:T(8,128)}) custom-call(f32[512,384]{1,0:T(8,128)} %get-tuple-element.34.loss_grad_ref, bf16[4,4608,384]{2,1,0:T(8,128)(2,1)} %get-tuple-element.35.w_ref, f32[4,8,384]{2,1,0:T(8,128)} %get-tuple-element.36.gain_ref, bf16[4,512,384]{2,1,0:T(8,128)(2,1)} %get-tuple-element.37.sent_ref, ...), custom_call_target="tpu_custom_call" | custom-call | tf_op jit(solution)/shard_map/pallas_call | solution.py:1429
  243.6 11.0 %shard_map.206 = (f32[1728,128]{1,0:T(8,128)}, f32[1728,128]{1,0:T(8,128)}, f32[1728,128]{1,0:T(8,128)}, f32[1728,128]{1,0:T(8,128)}, f32[2,48]{1,0:T(2,128)}, /...) custom-call(s32[32]{0:T(128)} %length_ref.3, s32[1]{0:T(128)S(6)} %copy.24.step_ref, ...), custom_call_target="tpu_custom_call" | custom-call | tf_op jit(solution)/shard_map/pallas_call | solution.py:1566

commit v9 on v8

--- a/solution.py
+++ b/solution.py
@@ -295,7 +295,7 @@
 
 
 FIRST_POINTS = {"qkv": "z2 y1 x0 x1", "heads": "z3 x2 x4 x5", "attended": "y2", "ffn1": "x3", "ffn2": "y3 x6", "ffn3": "x7"}
-POINTS = {"qkv": "x0 x1", "heads": "z3 x2 x4 x5", "attended": "y2", "ffn1": "x3", "ffn2": "y3 x6", "ffn3": "x7"}
+POINTS = {"qkv": "x0 x1", "heads": "z3 x2 x4 x5", "attended": "y2", "ffn0": "x3", "ffn1": "y3", "ffn2": "x6", "ffn3": "x7"}
 AHEAD_POINTS = {"attended": "z1 y0", "ffn2": "z2", "ffn3": "y1"}
 
 
@@ -764,7 +764,7 @@
     dim = width // HEADS
     part = width // 4
     layer = layers - 1 - pl.program_id(0)
-    rows = 256
+    rows = 512
     chunks = seg // rows
     gain_one = gain_ref[0, 0:1]
     gain_two = gain_ref[0, 1:2]
@@ -822,8 +822,8 @@
         dattended = dot_nt(datt, stack_quads(w_ref, 12, 1, 4)).astype(BF16)
         dhold_ref[at] = dattended
 
-        serve(1, i == 1, ("add_y", 3), ("add_x", 1), ("add_core", 2))
-        serve(2, i == 1, ("add_y", 0))
+        serve(1, i == 0, ("add_y", 3), ("add_x", 1), ("add_core", 2))
+        serve(2, i == 0, ("add_y", 0))
         return 0
 
     lax.fori_loop(0, chunks, ffn_step, 0)
@@ -1523,7 +1523,8 @@
                 r_out[at] = 0.95 * r_ref[at] + 0.05 * parts[3][m]
         return 0
 
-    lax.fori_loop(0, 2, quad_step, 0)
+    for q in range(2):
+        quad_step(q, 0)
 
     @pl.when(pl.program_id(0) == 0)
     def _():

time: 255 us -> 250 us (0.980)
  Pallas kernels: 252 us -> 247 us
    pallas_call x1, Pallas kernels: 127 us -> 125 us  [backward(): pl.pallas_call(functools.partial(backward_kernel, layers, half), grid=(la...]
where the time goes in v9:
time: 250 us; the launch traced here: 249 us
  Pallas kernels  247 us (99%)
    pallas_call x1, Pallas kernels, backward(): pl.pallas_call(functools.partial(backward_kernel, layers, half), grid=(la...  125 us
    pallas_call x1, Pallas kernels, forward(): pl.pallas_call(functools.partial(forward_kernel, layers, half, micro), gr...  112 us
    pallas_call x1, Pallas kernels, update(): pl.pallas_call(functools.partial(update_kernel, layers, limit), grid=(3,)...  10 us

profile of v9, /device:TPU:2, one launch (start us, length us, event | category | flops | bytes accessed | tf_op | source)
XLA Modules:
  0.0 249.4 jit_solution(13763116262016105834)
XLA Ops:
  0.6 1.4 copy.23.stems_ref
  2.0 112.0 %shard_map.204 = (bf16[4,8,512,512]{3,2,1,0:T(8,128)(2,1)}, bf16[4,3,512,384]{3,2,1,0:T(8,128)(2,1)}, bf16[4,512,384]{2,1,0:T(8,128)(2,1)}, f32[4,512,384]{2,1,0...) custom-call(s32[32]{0:T(128)} %length_ref.3, ...), custom_call_target="tpu_custom_call" | custom-call | tf_op jit(solution)/shard_map/pallas_call | solution.py:1375
  114.0 124.5 %shard_map.205 = (f32[576,384]{1,0:T(8,128)}, f32[16,384]{1,0:T(8,128)}, f32[8,128]{1,0:T(8,128)}) custom-call(f32[512,384]{1,0:T(8,128)} %get-tuple-element.34.loss_grad_ref, bf16[4,4608,384]{2,1,0:T(8,128)(2,1)} %get-tuple-element.35.w_ref, f32[4,8,384]{2,1,0:T(8,128)} %get-tuple-element.36.gain_ref, bf16[4,512,384]{2,1,0:T(8,128)(2,1)} %get-tuple-element.37.sent_ref, ...), custom_call_target="tpu_custom_call" | custom-call | tf_op jit(solution)/shard_map/pallas_call | solution.py:1429
  239.2 10.0 %shard_map.206 = (f32[1728,128]{1,0:T(8,128)}, f32[1728,128]{1,0:T(8,128)}, f32[1728,128]{1,0:T(8,128)}, f32[1728,128]{1,0:T(8,128)}, f32[2,48]{1,0:T(2,128)}, /...) custom-call(s32[32]{0:T(128)} %length_ref.3, s32[1]{0:T(128)S(6)} %copy.24.step_ref, ...), custom_call_target="tpu_custom_call" | custom-call | tf_op jit(solution)/shard_map/pallas_call | solution.py:1567

commit v10 on v9

--- a/solution.py
+++ b/solution.py
@@ -101,13 +101,6 @@
     )
 
 
-def greet(places):
-    barrier = pltpu.get_barrier_semaphore()
-    for place in places:
-        pl.semaphore_signal(barrier, inc=1, device_id=place, device_id_type=MESH)
-    pl.semaphore_wait(barrier, len(places))
-
-
 class Slabs:
     def __init__(self, rows):
         self.section, self.group, self.core, self.y, self.z_peers = mesh_place()
@@ -137,11 +130,17 @@
     def core_peer(self):
         return self.section + 1 - 2 * self.core, self.group
 
-    def greet_all(self):
-        greet(
-            [(lax.rem(self.section + k, 4), self.group) for k in range(1, 4)]
-            + [(self.section, lax.rem(self.group + k, 8)) for k in range(1, 8)]
-        )
+    def signal_all(self):
+        barrier = pltpu.get_barrier_semaphore()
+        for k in range(1, 4):
+            place = (lax.rem(self.section + k, 4), self.group)
+            pl.semaphore_signal(barrier, inc=1, device_id=place, device_id_type=MESH)
+        for k in range(1, 8):
+            place = (self.section, lax.rem(self.group + k, 8))
+            pl.semaphore_signal(barrier, inc=1, device_id=place, device_id_type=MESH)
+
+    def wait_all(self):
+        pl.semaphore_wait(pltpu.get_barrier_semaphore(), 10)
 
 
 class Gather(Slabs):
@@ -328,10 +327,12 @@
 
     @pl.when(layer == 0)
     def _():
-        gather.greet_all()
-        lax.fori_loop(0, flat_ref.shape[0] // 288, own_step, 0)
+        gather.signal_all()
+        for q in range(flat_ref.shape[0] // 288):
+            own_step(q, 0)
         own_gain_ref[...] = jnp.zeros_like(own_gain_ref)
         own_gain_ref[:2, : raw_gain_ref.shape[1]] = raw_gain_ref[...]
+        gather.wait_all()
         gather.begin()
         sent_ref[0] = x_ref[...]
         stats_ref[...] = jnp.zeros_like(stats_ref)
@@ -775,7 +776,7 @@
 
     @pl.when(layer == layers - 1)
     def _():
-        scatter.greet_all()
+        scatter.signal_all()
         sends_ref[...] = jnp.zeros_like(sends_ref)
         gain_grad_ref[...] = jnp.zeros_like(gain_grad_ref)
 
@@ -801,6 +802,11 @@
     dffn_ref[...] = dmid_ref[...].astype(BF16)
     for c in range(4):
         put_grad(32 + 4 * c, 1, dot_tn(hidden_ref[0, c], dffn_ref[...]))
+
+    @pl.when(layer == layers - 1)
+    def _():
+        scatter.wait_all()
+
     scatter.core_copy(layer, 0).start()
 
     def ffn_step(i, _):

time: 250 us -> 247 us (0.988)
  Pallas kernels: 247 us -> 244 us
where the time goes in v10:
time: 247 us; the launch traced here: 246 us
  Pallas kernels  244 us (99%)
    pallas_call x1, Pallas kernels, backward(): pl.pallas_call(functools.partial(backward_kernel, layers, half), grid=(la...  123 us
    pallas_call x1, Pallas kernels, forward(): pl.pallas_call(functools.partial(forward_kernel, layers, half, micro), gr...  111 us
    pallas_call x1, Pallas kernels, update(): pl.pallas_call(functools.partial(update_kernel, layers, limit), grid=(3,)...  10 us

profile of v10, /device:TPU:2, one launch (start us, length us, event | category | flops | bytes accessed | tf_op | source)
XLA Modules:
  0.0 246.3 jit_solution(10372471878463833302)
XLA Ops:
  0.6 1.4 copy.23.stems_ref
  2.0 110.6 %shard_map.204 = (bf16[4,8,512,512]{3,2,1,0:T(8,128)(2,1)}, bf16[4,3,512,384]{3,2,1,0:T(8,128)(2,1)}, bf16[4,512,384]{2,1,0:T(8,128)(2,1)}, f32[4,512,384]{2,1,0...) custom-call(s32[32]{0:T(128)} %length_ref.3, ...), custom_call_target="tpu_custom_call" | custom-call | tf_op jit(solution)/shard_map/pallas_call | solution.py:1381
  112.6 122.9 %shard_map.205 = (f32[576,384]{1,0:T(8,128)}, f32[16,384]{1,0:T(8,128)}, f32[8,128]{1,0:T(8,128)}) custom-call(f32[512,384]{1,0:T(8,128)} %get-tuple-element.34.loss_grad_ref, bf16[4,4608,384]{2,1,0:T(8,128)(2,1)} %get-tuple-element.35.w_ref, f32[4,8,384]{2,1,0:T(8,128)} %get-tuple-element.36.gain_ref, bf16[4,512,384]{2,1,0:T(8,128)(2,1)} %get-tuple-element.37.sent_ref, ...), custom_call_target="tpu_custom_call" | custom-call | tf_op jit(solution)/shard_map/pallas_call | solution.py:1435
  236.2 10.0 %shard_map.206 = (f32[1728,128]{1,0:T(8,128)}, f32[1728,128]{1,0:T(8,128)}, f32[1728,128]{1,0:T(8,128)}, f32[1728,128]{1,0:T(8,128)}, f32[2,48]{1,0:T(2,128)}, /...) custom-call(s32[32]{0:T(128)} %length_ref.3, s32[1]{0:T(128)S(6)} %copy.24.step_ref, ...), custom_call_target="tpu_custom_call" | custom-call | tf_op jit(solution)/shard_map/pallas_call | solution.py:1573

commit v11 on v10

--- a/solution.py
+++ b/solution.py
@@ -294,7 +294,7 @@
 
 
 FIRST_POINTS = {"qkv": "z2 y1 x0 x1", "heads": "z3 x2 x4 x5", "attended": "y2", "ffn1": "x3", "ffn2": "y3 x6", "ffn3": "x7"}
-POINTS = {"qkv": "x0 x1", "heads": "z3 x2 x4 x5", "attended": "y2", "ffn0": "x3", "ffn1": "y3", "ffn2": "x6", "ffn3": "x7"}
+POINTS = {"qkv": "x0 x1 z3", "heads": "x2 x4 x5", "attended": "y2 x3", "ffn1": "y3", "ffn2": "x6", "ffn3": "x7"}
 AHEAD_POINTS = {"attended": "z1 y0", "ffn2": "z2", "ffn3": "y1"}
 
 
@@ -911,9 +911,9 @@
             rows_out.append(row)
         rows_out.append(jnp.zeros((16 - 3 * layers, width), F32))
         totals.begin(jnp.concatenate(rows_out, axis=0))
+        scatter.add_core(0, 2)
         scatter.add_y(0, 3)
         scatter.add_x(0, 1)
-        scatter.add_core(0, 2)
         scatter.add_y(1, 0)
         totals.after_core()
         scatter.add_x(0, 2)

time: 247 us -> 247 us (level)
  no operation moved by 1% of the time
where the time goes in v11:
time: 247 us
  Pallas kernels  244 us (99%)
    pallas_call x1, Pallas kernels, backward(): pl.pallas_call(functools.partial(backward_kernel, layers, half), grid=(la...  123 us
    pallas_call x1, Pallas kernels, forward(): pl.pallas_call(functools.partial(forward_kernel, layers, half, micro), gr...  111 us
    pallas_call x1, Pallas kernels, update(): pl.pallas_call(functools.partial(update_kernel, layers, limit), grid=(3,)...  10 us

profile of v11, /device:TPU:2, one launch (start us, length us, event | category | flops | bytes accessed | tf_op | source)
XLA Modules:
  0.0 246.7 jit_solution(5243216224877300807)
XLA Ops:
  0.6 1.4 copy.23.stems_ref
  2.0 110.5 %shard_map.204 = (bf16[4,8,512,512]{3,2,1,0:T(8,128)(2,1)}, bf16[4,3,512,384]{3,2,1,0:T(8,128)(2,1)}, bf16[4,512,384]{2,1,0:T(8,128)(2,1)}, f32[4,512,384]{2,1,0...) custom-call(s32[32]{0:T(128)} %length_ref.3, ...), custom_call_target="tpu_custom_call" | custom-call | tf_op jit(solution)/shard_map/pallas_call | solution.py:1381
  112.6 123.3 %shard_map.205 = (f32[576,384]{1,0:T(8,128)}, f32[16,384]{1,0:T(8,128)}, f32[8,128]{1,0:T(8,128)}) custom-call(f32[512,384]{1,0:T(8,128)} %get-tuple-element.34.loss_grad_ref, bf16[4,4608,384]{2,1,0:T(8,128)(2,1)} %get-tuple-element.35.w_ref, f32[4,8,384]{2,1,0:T(8,128)} %get-tuple-element.36.gain_ref, bf16[4,512,384]{2,1,0:T(8,128)(2,1)} %get-tuple-element.37.sent_ref, ...), custom_call_target="tpu_custom_call" | custom-call | tf_op jit(solution)/shard_map/pallas_call | solution.py:1435
  236.5 10.0 %shard_map.206 = (f32[1728,128]{1,0:T(8,128)}, f32[1728,128]{1,0:T(8,128)}, f32[1728,128]{1,0:T(8,128)}, f32[1728,128]{1,0:T(8,128)}, f32[2,48]{1,0:T(2,128)}, /...) custom-call(s32[32]{0:T(128)} %length_ref.3, s32[1]{0:T(128)S(6)} %copy.24.step_ref, ...), custom_call_target="tpu_custom_call" | custom-call | tf_op jit(solution)/shard_map/pallas_call | solution.py:1573
